TPU v7x, 128 devices: a whole 4x4x4 slice. The times are simulated.
128 devices in a mesh: rep: 4 (over y), fsdp: 32 (over z, x, core).
Axes of the slice: x: 4, y: 4, z: 4, core: 2. Of those that a mesh axis runs over, the one named last changes fastest.
Arguments:
- grads: bfloat16 [4, 256, 512, 512], P('rep', None, 'fsdp'), may hold values from -40 to 40
- owner: int32 [256], replicated, may hold values from 0 to 31, as said below
- factor_left: float32 [384, 512, 512], P(('rep', 'fsdp')), may hold values from -0.6 to 0.6
- factor_right: float32 [384, 512, 512], P(('rep', 'fsdp')), may hold values from -0.6 to 0.6
- precond_left: bfloat16 [384, 512, 512], P(('rep', 'fsdp')), may hold values from -0.125 to 1.625
- precond_right: bfloat16 [384, 512, 512], P(('rep', 'fsdp')), may hold values from -0.125 to 1.625
Outputs:
- new_left: float32 [384, 512, 512], P(('rep', 'fsdp'))
- new_right: float32 [384, 512, 512], P(('rep', 'fsdp'))
- direction: bfloat16 [256, 512, 512], P(None, 'fsdp')
Inputs may be any that keep to these rules, and one draw needn't show every extreme that they name: Each owner column holds at most 12 blocks, and some column exactly that many.
All inputs are finite; a program needn't handle non-finite values.
Results may differ from a plain program's by a relative error of at most 0.017.
Values may be sent and summed in bfloat16 or wider, within the bound.
No kernel may reach another device: no remote copies, remote signals or barrier semaphores. Data moves between devices by JAX's collectives and lax.ppermute only.
A program may use at most 128 MiB of HBM per device.

v0:
```python
import jax
import jax.numpy as jnp
from jax import lax
from jax.sharding import PartitionSpec as P

epsilon = 1e-06
decay_rate = 0.9


def local(grads, owner, factor_left, factor_right, precond_left, precond_right):
    replicas = lax.axis_size("rep")
    columns = lax.axis_size("fsdp")
    my_rep = lax.axis_index("rep")
    slots_dev = factor_left.shape[0]
    blocks = owner.shape[0]
    row_band = grads.shape[2]
    block_size = grads.shape[3]
    position = jnp.arange(blocks, dtype=jnp.int32)
    same_owner = (owner[:, None] == owner[None, :]) & (position[None, :] < position[:, None])
    col_rank = jnp.sum(same_owner.astype(jnp.int32), axis=1)
    rep_of = col_rank % replicas
    local_slot = col_rank // replicas
    summed = lax.psum(grads[0].astype(jnp.float32).astype(jnp.bfloat16), "rep").astype(jnp.float32)
    outside = slots_dev * columns
    slot_key = jnp.where(rep_of == my_rep, local_slot * columns + owner, outside)
    slot_table = jnp.full((outside,), blocks, jnp.int32).at[slot_key].set(position, mode="drop")
    padded = jnp.concatenate([summed, jnp.zeros((1, row_band, block_size), jnp.float32)], axis=0)
    outgoing = jnp.take(padded, slot_table, axis=0)
    outgoing = outgoing.reshape(slots_dev, columns, row_band, block_size)
    arrived = lax.all_to_all(
        outgoing.astype(jnp.bfloat16), "fsdp", split_axis=1, concat_axis=1, tiled=True
    ).astype(outgoing.dtype)
    blocks_held = arrived.reshape(slots_dev, block_size, block_size)
    left_gram = jnp.einsum(
        "sik,sjk->sij", blocks_held, blocks_held, precision=lax.Precision.HIGHEST
    )
    right_gram = jnp.einsum(
        "ski,skj->sij", blocks_held, blocks_held, precision=lax.Precision.HIGHEST
    )
    new_left = decay_rate * factor_left + (1.0 - decay_rate) / block_size * left_gram
    new_right = decay_rate * factor_right + (1.0 - decay_rate) / block_size * right_gram
    held_low = blocks_held.astype(jnp.bfloat16)
    left_applied = jnp.einsum(
        "sik,skj->sij", precond_left, held_low, preferred_element_type=jnp.float32
    ).astype(jnp.bfloat16)
    preconditioned = jnp.einsum(
        "sik,skj->sij", left_applied, precond_right, preferred_element_type=jnp.float32
    )
    held_power = jnp.mean(blocks_held * blocks_held, axis=(1, 2))
    precond_power = jnp.mean(preconditioned * preconditioned, axis=(1, 2))
    grafting = jnp.sqrt((held_power + epsilon) / (precond_power + epsilon))
    shaped = (preconditioned * grafting[:, None, None]).astype(jnp.bfloat16)
    returned = lax.all_to_all(
        shaped.reshape(slots_dev, columns, row_band, block_size),
        "fsdp",
        split_axis=1,
        concat_axis=1,
        tiled=True,
    )
    everyone = lax.all_gather(returned, "rep", axis=0, tiled=True)
    all_rows = everyone.reshape(replicas * slots_dev * columns, row_band, block_size)
    pick_index = (rep_of * slots_dev + local_slot) * columns + owner
    direction = jnp.take(all_rows, pick_index, axis=0)
    return (new_left, new_right, direction)


def solution(mesh):
    placed = (
        P("rep", None, "fsdp", None),
        P(),
        P(("rep", "fsdp"), None, None),
        P(("rep", "fsdp"), None, None),
        P(("rep", "fsdp"), None, None),
        P(("rep", "fsdp"), None, None),
    )
    return jax.shard_map(
        local,
        mesh=mesh,
        in_specs=placed,
        out_specs=(
            P(("rep", "fsdp"), None, None),
            P(("rep", "fsdp"), None, None),
            P(None, "fsdp", None),
        ),
        check_vma=False,
    )
```

profile of v0, /device:TPU:0, one launch (start us, length us, event | category | flops | bytes accessed | tf_op | source)
XLA Modules:
  0.0 260.7 jit_solution(2562099491982179414)
XLA Ops:
  7.2 0.0 copy-start
  7.2 0.0 copy-start.3
  7.2 0.0 all-reduce.3.cloned.1.call-start
  7.2 0.7 all-reduce.3.cloned.1.call-update
  7.9 0.0 all-gather.2.cloned.1.call-start
  8.0 0.0 copy-done.3
  8.0 0.2 convert_reduce_fusion
  8.2 1.4 scatter_custom_fusion
  9.6 0.1 broadcast_in_dim.45
  9.7 95.9 %all-reduce.3.cloned.1.call-done = bf16[256,16,512]{2,1,0:T(8,128)(2,1)} async-done(((bf16[256,16,512]{2,1,0:T(8,128)(2,1)}), bf16[256,16,512]{2,1,0:T(8,128)(2,1)}) %all-reduce.3.cloned.1.call-update) | async-done | bytes 4194320 | tf_op jit(solution)/shard_map/psum | solution.py:23
  105.7 4.6 %pad_convert_fusion = bf16[257,16,512]{2,1,0:T(8,128)(2,1)} fusion(bf16[256,16,512]{2,1,0:T(8,128)(2,1)} %all-reduce.3.cloned.1.call-done), kind=kLoop, calls=%fused_computation.3 | loop fusion | bytes 8404992 | tf_op jit(solution)/shard_map/concatenate | solution.py:27
  110.3 2.9 %gather_fusion = bf16[96,16,512]{2,1,0:T(8,128)(2,1)S(1)} fusion(bf16[257,16,512]{2,1,0:T(8,128)(2,1)} %pad_convert_fusion, s32[1024]{0:T(1024)S(1)} %pad_clamp_fusion.1), kind=kCustom, calls=%fused_computation | custom fusion | bytes 3146112 | tf_op jit(solution)/shard_map/jit(_take)/gather | solution.py:28
  113.2 0.3 select_convert_fusion
  113.5 0.1 copy.25
  113.6 30.0 %all_to_all.10 = bf16[3,32,16,512]{3,2,0,1:T(8,128)(2,1)S(1)} all-to-all(bf16[3,32,16,512]{3,2,0,1:T(8,128)(2,1)S(1)} %copy.25), channel_id=1, replica_groups=mesh['rep'=4,'fsdp'=32] {'fsdp'}, dimensions={1} | all-to-all | bytes 3145728 | tf_op jit(solution)/shard_map/all_to_all | solution.py:30
  143.7 1.1 copy-done.1
  144.8 0.1 copy.26
  144.9 0.0 copy-done
  144.9 5.1 %multiply_reduce_fusion = (f32[3]{0:T(128)S(1)}, f32[3,512,512]{2,1,0:T(8,128)}) fusion(bf16[3,512,512]{2,1,0:T(8,128)(2,1)S(1)} %copy-done, bf16[3,512,512]{2,1,0:T(8,128)(2,1)S(1)} %bitcast.12, bf16[3,512,512]{2,1,0:T(8,128)(2,1)} %param.10), kind=kOutput, calls=%fused_computation.6 | convolution fusion | flops 1612972032 | bytes 7864332 | tf_op jit(solution)/shard_map/sik,skj->sij/dot_general | solution.py:46
  150.0 1.9 multiply_reduce_fusion.1
  151.9 2.4 multiply_convert_fusion
  154.3 0.1 copy.30
  154.4 26.4 %all_to_all.11 = bf16[3,32,16,512]{3,2,0,1:T(8,128)(2,1)S(1)} all-to-all(bf16[3,32,16,512]{3,2,0,1:T(8,128)(2,1)S(1)} %copy.30), channel_id=1, replica_groups=mesh['rep'=4,'fsdp'=32] {'fsdp'}, dimensions={1} | all-to-all | bytes 3145728 | tf_op jit(solution)/shard_map/all_to_all | solution.py:53
  180.8 1.3 copy.31
  182.1 0.0 all-gather.2.cloned.1.call-update
  182.1 0.0 copy-start.2
  182.1 4.9 %multiply_add_fusion = f32[3,512,512]{2,1,0:T(8,128)} fusion(f32[3,512,512]{2,1,0:T(8,128)} %param.9, bf16[3,512,512]{2,1,0:T(8,128)(2,1)S(1)} %bitcast.13), kind=kOutput, calls=%fused_computation.8 | convolution fusion | flops 807665664 | bytes 7864320 | tf_op jit(solution)/shard_map/ski,skj->sij/dot_general | solution.py:37
  187.0 0.0 copy-done.2
  187.0 2.8 %multiply_add_fusion.1 = f32[3,512,512]{2,1,0:T(8,128)} fusion(f32[3,512,512]{2,1,0:T(8,128)S(1)} %copy-done.2, bf16[3,512,512]{2,1,0:T(8,128)(2,1)S(1)} %bitcast.14), kind=kOutput, calls=%fused_computation.9 | convolution fusion | flops 807665664 | bytes 7864320 | tf_op jit(solution)/shard_map/sik,sjk->sij/dot_general | solution.py:34
  189.8 54.4 %all-gather.2.cloned.1.call-done = bf16[12,32,16,512]{3,2,1,0:T(8,128)(2,1)} async-done(((bf16[3,32,16,512]{3,2,1,0:T(8,128)(2,1)}), bf16[12,32,16,512]{3,2,1,0:T(8,128)(2,1)}) %all-gather.2.cloned.1.call-update) | async-done | bytes 6291472 | tf_op jit(solution)/shard_map/all_gather | solution.py:60
  244.2 5.6 %gather_fusion.1 = bf16[256,16,512]{2,1,0:T(8,128)(2,1)} fusion(bf16[384,16,512]{2,1,0:T(8,128)(2,1)} %bitcast.18, s32[1024]{0:T(1024)S(1)} %pad_clamp_fusion), kind=kCustom, calls=%fused_computation.1 | custom fusion | bytes 8389632 | tf_op jit(solution)/shard_map/jit(_take)/gather | solution.py:63
  249.8 4.1 %broadcast_select_fusion = bf16[256,16,512]{2,1,0:T(8,128)(2,1)} fusion(bf16[256,16,512]{2,1,0:T(8,128)(2,1)} %gather_fusion.1, pred[256]{0:T(512)(128)(4,1)S(1)} %get-tuple-element.3), kind=kLoop, calls=%fused_computation.4 | loop fusion | flops 2097152 | bytes 8388864 | tf_op jit(solution)/shard_map/jit(_take)/select_n | solution.py:63
  (9 shorter events, 0.1 us)
Async XLA Ops:
  7.2 137.8 %copy-start = (bf16[3,512,512]{2,1,0:T(8,128)(2,1)S(1)}, bf16[3,512,512]{2,1,0:T(8,128)(2,1)}, u32[]{:S(2)}) copy-start(bf16[3,512,512]{2,1,0:T(8,128)(2,1)} %param.11) | copy-start | bytes 4718596
  7.2 0.8 copy-start.3
  7.2 98.5 %all-reduce.3.cloned.1.call-start = ((), (), s32[]{:S(2)}) async-start(), calls=%async_computation.2 | async-start | bytes 8388608 | tf_op jit(solution)/shard_map/psum | solution.py:23
  7.9 236.3 %all-gather.2.cloned.1.call-start = ((), (), s32[]{:S(2)}) async-start(), calls=%async_computation.3 | async-start | bytes 7864320 | tf_op jit(solution)/shard_map/all_gather | solution.py:60
  143.7 1.1 copy-start.1
  182.1 4.9 %copy-start.2 = (f32[3,512,512]{2,1,0:T(8,128)S(1)}, f32[3,512,512]{2,1,0:T(8,128)}, u32[]{:S(2)}) copy-start(f32[3,512,512]{2,1,0:T(8,128)} %param.8) | copy-start | bytes 9437188
Sparse Core Ops, SparseCore 0:
  10.4 95.2 all-reduce.2
  182.2 61.9 all-gather.1
where the time goes:
time: 262 us; the launch traced here: 261 us
  waiting for transfers between devices  151 us (58%)
  blocking collectives  56.4 us (22%)
  local copies, waits for them, and re-layouts  17.4 us (7%)
  between operations  14.2 us (5%)
  matrix products  12.7 us (5%)
  other arithmetic  8.91 us (3%)
    psum x1, waiting for transfers between devices, local(): lax.psum(grads[0].astype(jnp.float32).astype(jnp.bfloat16), 'rep')  95.9 us
    all_gather x1, waiting for transfers between devices, local(): everyone = lax.all_gather(returned, 'rep', axis=0, tiled=True)  54.4 us
    all_to_all x1, blocking collectives, local(): lax.all_to_all(outgoing.astype(jnp.bfloat16), 'fsdp', split_axis=1, conca...  30 us
    all_to_all x1, blocking collectives, local(): lax.all_to_all(shaped.reshape(slots_dev, columns, row_band, block_size),...  26.4 us
    gather x1, local copies, waits for them, and re-layouts, local(): direction = jnp.take(all_rows, pick_index, axis=0)  5.62 us
  transfers between devices with their start and end apart: 2, of which 2 were waited for; matrix products, arithmetic and copies ran while one was open for 4% of the time, Pallas kernels for 0%

commit v1 on v0

v1 whole, which is shorter than its diff:
```python
import functools

import jax
import jax.numpy as jnp
from jax import lax
from jax.experimental import pallas as pl
from jax.experimental.pallas import tpu as pltpu
from jax.sharding import PartitionSpec as P

epsilon = 1e-06
decay_rate = 0.9

ANY = pl.BlockSpec(memory_space=pl.ANY)
SMEM = pl.BlockSpec(memory_space=pltpu.SMEM)
VMEM = pl.BlockSpec(memory_space=pltpu.VMEM)
F32 = jnp.float32
LIMIT = 48 * 1024 * 1024


def params():
    return pltpu.CompilerParams(vmem_limit_bytes=LIMIT)


def cost(nbytes, flops=0):
    return pl.CostEstimate(flops=flops, bytes_accessed=nbytes, transcendentals=0)


def fetch(rows, table, start, count, into, first, sem, last):
    def one(j, _):
        block = jnp.minimum(table[start + j], last)
        pltpu.make_async_copy(rows.at[block], into.at[first + j], sem).start()
        return 0

    lax.fori_loop(0, count, one, 0, unroll=4)


def drain(into, sem):
    pltpu.make_async_copy(into, into, sem).wait()


def first_kernel(size, table, rows, low, high, sems):
    last = rows.shape[0] - 1
    half = size // 2
    fetch(rows, table, 2 * size, half, low, 0, sems.at[0], last)
    fetch(rows, table, 2 * size + half, half, high, 0, sems.at[1], last)
    drain(low, sems.at[0])
    drain(high, sems.at[1])


def second_kernel(size, table, rows, got_low, got_high, up, down, sems):
    last = rows.shape[0] - 1
    half = size // 2
    fetch(rows, table, size, size, up, 0, sems.at[0], last)
    fetch(rows, table, 3 * size, size, down, 0, sems.at[1], last)
    drain(up, sems.at[0])

    def add_low(j, _):
        up[j] = (up[j].astype(F32) + got_low[j].astype(F32)).astype(up.dtype)
        return 0

    lax.fori_loop(0, half, add_low, 0, unroll=4)
    drain(down, sems.at[1])

    def add_high(j, _):
        k = half + j
        down[k] = (down[k].astype(F32) + got_high[j].astype(F32)).astype(down.dtype)
        return 0

    lax.fori_loop(0, half, add_high, 0, unroll=4)


def third_kernel(size, base, table, place, rows, from_up, from_down, out, own, sem):
    last = rows.shape[0] - 1
    fetch(rows, table, 0, size, own, 0, sem, last)
    out[...] = jnp.zeros_like(out)
    drain(own, sem)

    def one(j, _):
        block = table[j]

        @pl.when(block <= last)
        def _():
            where = place[block]
            total = own[j].astype(F32) + from_up[j].astype(F32) + from_down[j].astype(F32)
            out[where % 32, where // 32 - base] = total.astype(out.dtype)

        return 0

    lax.fori_loop(0, size, one, 0)


def pack_kernel(size, base, last, table, place, returned, out, sem):
    def one(j, _):
        block = jnp.minimum(table[j], last)
        where = place[block]
        layer = jnp.maximum(where // 32 - base, 0)
        pltpu.make_async_copy(returned.at[where % 32, layer], out.at[j], sem).start()
        return 0

    lax.fori_loop(0, size, one, 0, unroll=4)
    drain(out, sem)


def place_kernel(plan, last, table, *refs):
    sources, out, sem = refs[: len(plan)], refs[-2], refs[-1]

    def each(act):
        for source, (start, count, shift) in zip(sources, plan):

            def one(j, _, source=source, start=start, shift=shift):
                block = table[start + j]

                @pl.when(block <= last)
                def _():
                    act(pltpu.make_async_copy(source.at[shift + j], out.at[block], sem))

                return 0

            lax.fori_loop(0, count, one, 0)

    each(lambda copy: copy.start())
    each(lambda copy: copy.wait())


def apply_kernel(held, left, right, shaped):
    order = left.shape[-1]
    block = held[...].reshape(order, order)
    applied = jnp.dot(left[0], block, preferred_element_type=F32).astype(jnp.bfloat16)
    product = jnp.dot(applied, right[0], preferred_element_type=F32)
    wide = block.astype(F32)
    count = order * order
    held_power = jnp.sum(wide * wide) / count
    power = jnp.sum(product * product) / count
    scale = jnp.sqrt((held_power + epsilon) / (power + epsilon))
    shaped[...] = (product * scale).astype(jnp.bfloat16).reshape(shaped.shape)


def gram_kernel(held_first, held_rest, left, right, new_left, new_right):
    order = left.shape[-1]
    block = jnp.where(pl.program_id(0) == 0, held_first[...], held_rest[...]).reshape(order, order)
    weight = (1.0 - decay_rate) / order
    left_gram = lax.dot_general(block, block, (((1,), (1,)), ((), ())), preferred_element_type=F32)
    right_gram = lax.dot_general(block, block, (((0,), (0,)), ((), ())), preferred_element_type=F32)
    new_left[0] = decay_rate * left[0] + weight * left_gram
    new_right[0] = decay_rate * right[0] + weight * right_gram


def local(grads, owner, factor_left, factor_right, precond_left, precond_right):
    rows = grads[0]
    blocks, band, width = rows.shape
    columns = lax.axis_size("fsdp")
    replicas = lax.axis_size("rep")
    my_rep = lax.axis_index("rep")
    slots = factor_left.shape[0]
    last = blocks - 1
    up_pairs = [(i, (i + 1) % replicas) for i in range(replicas)]
    down_pairs = [(i, (i - 1) % replicas) for i in range(replicas)]

    position = jnp.arange(blocks, dtype=jnp.int32)
    earlier = position[None, :] < position[:, None]
    same_owner = (owner[:, None] == owner[None, :]) & earlier
    col_rank = jnp.sum(same_owner.astype(jnp.int32), axis=1)
    rep_of = col_rank % replicas
    local_slot = col_rank // replicas
    relative = (rep_of - my_rep) % replicas
    place = local_slot * columns + owner

    def listed(key, size):
        hits = key[None, :] == jnp.arange(size, dtype=jnp.int32)[:, None]
        return jnp.min(jnp.where(hits, position[None, :], blocks), axis=1)

    size_first = columns
    table_first = listed(jnp.where(local_slot == 0, relative * columns + owner, -1), replicas * columns)
    size_rest = 56
    in_rest = local_slot > 0
    same_list = (rep_of[:, None] == rep_of[None, :]) & in_rest[None, :] & earlier
    in_list = jnp.sum(same_list.astype(jnp.int32), axis=1)
    table_rest = listed(jnp.where(in_rest, relative * size_rest + in_list, -1), replicas * size_rest)

    def piece(count):
        return jax.ShapeDtypeStruct((count, band, width), jnp.bfloat16)

    def nbytes(count):
        return count * band * width * 2

    def sums(table, size, base, depth):
        half = size // 2
        low, high = pl.pallas_call(
            functools.partial(first_kernel, size),
            out_shape=(piece(half), piece(half)),
            in_specs=[SMEM, ANY],
            out_specs=(ANY, ANY),
            scratch_shapes=[pltpu.SemaphoreType.DMA((2,))],
            compiler_params=params(),
            cost_estimate=cost(nbytes(2 * size)),
        )(table, rows)
        got_low = lax.ppermute(low, "rep", up_pairs)
        got_high = lax.ppermute(high, "rep", down_pairs)
        up, down = pl.pallas_call(
            functools.partial(second_kernel, size),
            out_shape=(piece(size), piece(size)),
            in_specs=[SMEM, ANY, VMEM, VMEM],
            out_specs=(VMEM, VMEM),
            scratch_shapes=[pltpu.SemaphoreType.DMA((2,))],
            compiler_params=params(),
            cost_estimate=cost(nbytes(5 * size)),
        )(table, rows, got_low, got_high)
        from_up = lax.ppermute(up, "rep", up_pairs)
        from_down = lax.ppermute(down, "rep", down_pairs)
        return pl.pallas_call(
            functools.partial(third_kernel, size, base),
            out_shape=jax.ShapeDtypeStruct((columns, depth, band, width), jnp.bfloat16),
            in_specs=[SMEM, SMEM, ANY, VMEM, VMEM],
            out_specs=VMEM,
            scratch_shapes=[pltpu.VMEM((size, band, width), jnp.bfloat16), pltpu.SemaphoreType.DMA],
            compiler_params=params(),
            cost_estimate=cost(nbytes(5 * size)),
        )(table, place, rows, from_up, from_down)

    def exchange(x):
        return lax.all_to_all(x, "fsdp", split_axis=0, concat_axis=0, tiled=True)

    def applied(held, base, depth):
        order = factor_left.shape[1]
        strip = pl.BlockSpec((columns, 1, band, width), lambda s: (0, s, 0, 0))
        matrix = pl.BlockSpec((1, order, order), lambda s: (s + base, 0, 0))
        return pl.pallas_call(
            apply_kernel,
            grid=(depth,),
            out_shape=jax.ShapeDtypeStruct(held.shape, jnp.bfloat16),
            in_specs=[strip, matrix, matrix],
            out_specs=strip,
            compiler_params=params(),
            cost_estimate=cost(depth * 4 * order * order * 2, depth * 4 * order**3),
        )(held, precond_left, precond_right)

    def spread(chunk):
        half = chunk.shape[0] // 2
        below = lax.ppermute(chunk, "rep", up_pairs)
        above = lax.ppermute(chunk, "rep", down_pairs)
        return below, above, half

    def placed(table, plan, sources, out):
        extra = [] if out is None else [out]

        def kernel(*refs):
            place_kernel(plan, last, *refs[: 1 + len(plan)], *refs[-2:])

        return pl.pallas_call(
            kernel,
            out_shape=piece(blocks),
            in_specs=[SMEM] + [ANY] * (len(sources) + len(extra)),
            out_specs=ANY,
            scratch_shapes=[pltpu.SemaphoreType.DMA],
            input_output_aliases={} if out is None else {1 + len(sources): 0},
            compiler_params=params(),
            cost_estimate=cost(nbytes(2 * sum(p[1] for p in plan))),
        )(table, *sources, *extra)

    sent_first = sums(table_first, size_first, 0, 1)
    held_first = exchange(sent_first)
    sent_rest = sums(table_rest, size_rest, 1, slots - 1)
    back_first = exchange(applied(held_first, 0, 1))
    held_rest = exchange(sent_rest)
    back_rest = exchange(applied(held_rest, 1, slots - 1))

    own_first = back_first.reshape(columns, band, width)
    below_first, above_first, half_first = spread(own_first)
    far_low_first = lax.ppermute(below_first[:half_first], "rep", up_pairs)
    far_high_first = lax.ppermute(above_first[half_first:], "rep", down_pairs)

    own_rest = pl.pallas_call(
        functools.partial(pack_kernel, size_rest, 1, last),
        out_shape=piece(size_rest),
        in_specs=[SMEM, SMEM, ANY],
        out_specs=ANY,
        scratch_shapes=[pltpu.SemaphoreType.DMA],
        compiler_params=params(),
        cost_estimate=cost(nbytes(2 * size_rest)),
    )(table_rest, place, back_rest)
    below_rest, above_rest, half_rest = spread(own_rest)
    far_low_rest = lax.ppermute(below_rest[:half_rest], "rep", up_pairs)
    far_high_rest = lax.ppermute(above_rest[half_rest:], "rep", down_pairs)

    order = factor_left.shape[1]
    matrix = pl.BlockSpec((1, order, order), lambda s: (s, 0, 0))
    new_left, new_right = pl.pallas_call(
        gram_kernel,
        grid=(slots,),
        out_shape=(
            jax.ShapeDtypeStruct(factor_left.shape, F32),
            jax.ShapeDtypeStruct(factor_right.shape, F32),
        ),
        in_specs=[
            pl.BlockSpec((columns, 1, band, width), lambda s: (0, 0, 0, 0)),
            pl.BlockSpec((columns, 1, band, width), lambda s: (0, jnp.maximum(s - 1, 0), 0, 0)),
            matrix,
            matrix,
        ],
        out_specs=(matrix, matrix),
        compiler_params=params(),
        cost_estimate=cost(slots * 18 * order * order, slots * 4 * order**3),
    )(held_first, held_rest, factor_left, factor_right)

    def all_plan(size):
        half = size // 2
        return [(0, size, 0), (size, size, 0), (3 * size, size, 0), (2 * size, half, 0), (2 * size + half, half, 0)]

    plan_first, plan_rest = all_plan(size_first), all_plan(size_rest)
    direction = placed(
        table_first, plan_first, [own_first, above_first, below_first, far_low_first, far_high_first], None
    )
    direction = placed(table_rest, plan_rest[:3], [own_rest, above_rest, below_rest], direction)
    direction = placed(table_rest, plan_rest[3:], [far_low_rest, far_high_rest], direction)
    return (new_left, new_right, direction)


def solution(mesh):
    placed = (
        P("rep", None, "fsdp", None),
        P(),
        P(("rep", "fsdp"), None, None),
        P(("rep", "fsdp"), None, None),
        P(("rep", "fsdp"), None, None),
        P(("rep", "fsdp"), None, None),
    )
    return jax.shard_map(
        local,
        mesh=mesh,
        in_specs=placed,
        out_specs=(
            P(("rep", "fsdp"), None, None),
            P(("rep", "fsdp"), None, None),
            P(None, "fsdp", None),
        ),
        check_vma=False,
    )
```

time: 262 us -> 270 us (1.031)
  Pallas kernels: 0 us -> 110 us
  waiting for transfers between devices: 151 us -> 61.7 us
  starting transfers between devices: 0.08 us -> 37.2 us
  between operations: 14.2 us -> 0.88 us
  matrix products: 12.7 us -> 0 us
  blocking collectives: 56.4 us -> 44.1 us
  local copies, waits for them, and re-layouts: 17.4 us -> 9.67 us
  other arithmetic: 8.91 us -> 2.07 us
    pallas_call x0 -> x13, Pallas kernels: none -> 110 us  [the longest x3 56.2 us: placed(): pl.pallas_call(kernel, out_shape=piece(blocks), in_specs=[SMEM] + [ANY] *...]
    psum x1 -> x0, waiting for transfers between devices: 95.9 us -> none  [local(): lax.psum(grads[0].astype(jnp.float32).astype(jnp.bfloat16), 'rep')]
    ppermute x0 -> x16, waiting for transfers between devices: none -> 61.7 us  [the longest x2 30.8 us: sums(): from_up = lax.ppermute(up, 'rep', up_pairs)]
    all_gather x1 -> x0, waiting for transfers between devices: 54.4 us -> none  [local(): everyone = lax.all_gather(returned, 'rep', axis=0, tiled=True)]
    ppermute x0 -> x16, starting transfers between devices: none -> 25.3 us  [the longest x2 6.26 us: spread(): above = lax.ppermute(chunk, 'rep', down_pairs)]
    dot_general x3 -> x0, matrix products: 12.7 us -> none  [the longest x1 5.06 us: local(): jnp.einsum('sik,skj->sij', left_applied, precond_right, preferred_element...]
    all_to_all x2, blocking collectives: 56.4 us -> 44.1 us  [exchange(): return lax.all_to_all(x, 'fsdp', split_axis=0, concat_axis=0, tiled=True)]
    all_to_all x0 -> x2, starting transfers between devices: none -> 12 us  [exchange(): return lax.all_to_all(x, 'fsdp', split_axis=0, concat_axis=0, tiled=True)]
  transfers between devices with their start and end apart: 2 -> 18, of which waited for: 2 -> 6; matrix products, arithmetic and copies ran while one was open for 4% -> 1% of each run, Pallas kernels for 0% -> 37%
where the time goes in v1:
time: 270 us; the launch traced here: 266 us
  Pallas kernels  110 us (41%)
  waiting for transfers between devices  61.7 us (23%)
  blocking collectives  44.1 us (16%)
  starting transfers between devices  37.2 us (14%)
  local copies, waits for them, and re-layouts  9.67 us (4%)
    pallas_call x3, Pallas kernels, placed(): pl.pallas_call(kernel, out_shape=piece(blocks), in_specs=[SMEM] + [ANY] *...  56.2 us
    all_to_all x2, blocking collectives, exchange(): return lax.all_to_all(x, 'fsdp', split_axis=0, concat_axis=0, tiled=True)  44.1 us
    ppermute x2, waiting for transfers between devices, sums(): from_up = lax.ppermute(up, 'rep', up_pairs)  30.8 us
    pallas_call x1, Pallas kernels, local(): pl.pallas_call(functools.partial(pack_kernel, size_rest, 1, last), out_sh...  29.5 us
    ppermute x2, waiting for transfers between devices, sums(): got_low = lax.ppermute(low, 'rep', up_pairs)  16.9 us
    all_to_all x2, starting transfers between devices, exchange(): return lax.all_to_all(x, 'fsdp', split_axis=0, concat_axis=0, tiled=True)  12 us
    ppermute x2, waiting for transfers between devices, spread(): below = lax.ppermute(chunk, 'rep', up_pairs)  8.43 us
    unnamed x16, local copies, waits for them, and re-layouts  7.54 us
  transfers between devices with their start and end apart: 18, of which 6 were waited for; matrix products, arithmetic and copies ran while one was open for 1% of the time, Pallas kernels for 37%

profile of v1, /device:TPU:0, one launch (start us, length us, event | category | flops | bytes accessed | tf_op | source)
XLA Modules:
  0.0 266.1 jit_solution(14576324598660826485)
XLA Ops:
  2.6 2.2 copy-done
  4.8 2.2 shard_map.88
  7.0 1.7 collective-permute-start.4
  8.7 1.6 collective-permute-start.5
  10.3 10.4 %collective-permute-done.4.got_low = bf16[28,16,512]{2,1,0:T(8,128)(2,1)S(1)} collective-permute-done((bf16[28,16,512]{2,1,0:T(8,128)(2,1)S(1)}, bf16[28,16,512]{2,1,0:T(8,128)(2,1)S(1)}, u32[]{:S(2)}, u32[]{:S(2)}) %collective-permute-start.4) | collective-permute-done | bytes 458784 | tf_op jit(solution)/shard_map/ppermute | solution.py:197
  20.7 3.7 %shard_map.89 = (bf16[56,16,512]{2,1,0:T(8,128)(2,1)S(1)}, bf16[56,16,512]{2,1,0:T(8,128)(2,1)S(1)}) custom-call(s32[224]{0:T(256)S(1)} %select_reduce_fusion.table.refs_0_, bf16[256,16,512]{2,1,0:T(8,128)(2,1)} %bitcast.2, bf16[28,16,512]{2,1,0:T(8,128)(2,1)S(1)} %collective-permute-done.4.got_low, bf16[28,16,512]{2,1,0:T(8,128)(2,1)S(1)} %collective-permute-done.5.got_high), custom_call_target="tpu_custom_call" | custom-call | bytes 4587520 | tf_op jit(solution)/shard_map/pallas_call | solution.py:199
  25.6 2.0 collective-permute-start.7
  27.7 19.3 %collective-permute-done.6.from_up = bf16[56,16,512]{2,1,0:T(8,128)(2,1)S(1)} collective-permute-done((bf16[56,16,512]{2,1,0:T(8,128)(2,1)S(1)}, bf16[56,16,512]{2,1,0:T(8,128)(2,1)S(1)}, u32[]{:S(2)}, u32[]{:S(2)}) %collective-permute-start.6) | collective-permute-done | bytes 917536 | tf_op jit(solution)/shard_map/ppermute | solution.py:208
  47.0 3.1 %shard_map.90 = bf16[32,2,16,512]{3,2,1,0:T(8,128)(2,1)S(1)} custom-call(s32[224]{0:T(256)S(1)} %select_reduce_fusion.table.refs_0_, s32[256]{0:T(256)S(1)} %get-tuple-element.27.place, bf16[256,16,512]{2,1,0:T(8,128)(2,1)} %bitcast.3, bf16[56,16,512]{2,1,0:T(8,128)(2,1)S(1)} %collective-permute-done.6.from_up, ...), custom_call_target="tpu_custom_call" | custom-call | bytes 4587520 | tf_op jit(solution)/shard_map/pallas_call | solution.py:210
  50.1 25.2 %all_to_all.20.held_rest.held = bf16[32,2,16,512]{3,2,1,0:T(8,128)(2,1)S(1)} all-to-all(bf16[32,2,16,512]{3,2,1,0:T(8,128)(2,1)S(1)} %shard_map.90), channel_id=1, replica_groups=mesh['rep'=4,'fsdp'=32] {'fsdp'}, dimensions={0} | all-to-all | bytes 2097152 | tf_op jit(solution)/shard_map/all_to_all | solution.py:221
  75.3 2.5 shard_map.92
  78.8 4.7 %all-to-all-start.2 = ((bf16[32,2,16,512]{3,2,1,0:T(8,128)(2,1)}), bf16[32,2,16,512]{3,2,1,0:T(8,128)(2,1)}, u32[]{:S(2)}, u32[]{:S(2)}) async-start(bf16[32,2,16,512]{3,2,1,0:T(8,128)(2,1)} %copy-done.5), calls=%async_computation.2 | async-start | bytes 2097152 | tf_op jit(solution)/shard_map/all_to_all | solution.py:221
  83.6 2.2 copy-done.1
  88.5 2.3 collective-permute-start.1
  90.8 6.5 %collective-permute-done.got_low = bf16[16,16,512]{2,1,0:T(8,128)(2,1)S(1)} collective-permute-done((bf16[16,16,512]{2,1,0:T(8,128)(2,1)S(1)}, bf16[16,16,512]{2,1,0:T(8,128)(2,1)S(1)}, u32[]{:S(2)}, u32[]{:S(2)}) %collective-permute-start) | collective-permute-done | bytes 262176 | tf_op jit(solution)/shard_map/ppermute | solution.py:197
  97.3 2.5 shard_map.86
  101.1 2.1 collective-permute-start.3
  103.2 11.5 %collective-permute-done.2.from_up = bf16[32,16,512]{2,1,0:T(8,128)(2,1)S(1)} collective-permute-done((bf16[32,16,512]{2,1,0:T(8,128)(2,1)S(1)}, bf16[32,16,512]{2,1,0:T(8,128)(2,1)S(1)}, u32[]{:S(2)}, u32[]{:S(2)}) %collective-permute-start.2) | collective-permute-done | bytes 524320 | tf_op jit(solution)/shard_map/ppermute | solution.py:208
  114.6 2.2 shard_map.87
  117.6 7.3 %all-to-all-start = ((bf16[32,1,16,512]{3,2,1,0:T(8,128)(2,1)}), bf16[32,1,16,512]{3,2,1,0:T(8,128)(2,1)S(1)}, u32[]{:S(2)}, u32[]{:S(2)}) async-start(bf16[32,1,16,512]{3,2,1,0:T(8,128)(2,1)} %copy-done.7), calls=%async_computation | async-start | bytes 1048576 | tf_op jit(solution)/shard_map/all_to_all | solution.py:221
  125.0 29.5 %shard_map.93.refs_1_ = bf16[56,16,512]{2,1,0:T(8,128)(2,1)} custom-call(s32[224]{0:T(256)S(1)} %select_reduce_fusion.table.refs_0_, s32[256]{0:T(256)S(1)} %get-tuple-element.27.place, bf16[32,2,16,512]{3,2,1,0:T(8,128)(2,1)} %all-to-all-done.2.returned), custom_call_target="tpu_custom_call" | custom-call | bytes 1835008 | tf_op jit(solution)/shard_map/pallas_call | solution.py:272
  154.5 3.0 %collective-permute-start.10 = (bf16[56,16,512]{2,1,0:T(8,128)(2,1)}, bf16[56,16,512]{2,1,0:T(8,128)(2,1)}, u32[]{:S(2)}, u32[]{:S(2)}) collective-permute-start(bf16[56,16,512]{2,1,0:T(8,128)(2,1)} %shard_map.93.refs_1_), channel_id=1, source_target_pairs={{0,96},{32,0},{64,32},{96,64},{1,97},{33,1},{65,33},{97,65},{2,98}... | collective-permute-start | bytes 2752520 | tf_op jit(solution)/shard_map/ppermute | solution.py:240
  160.1 18.9 %all_to_all.21 = bf16[32,1,16,512]{3,2,1,0:T(8,128)(2,1)S(1)} all-to-all(bf16[32,1,16,512]{3,2,1,0:T(8,128)(2,1)S(1)} %shard_map.94), channel_id=1, replica_groups=mesh['rep'=4,'fsdp'=32] {'fsdp'}, dimensions={0} | all-to-all | bytes 1048576 | tf_op jit(solution)/shard_map/all_to_all | solution.py:221
  179.0 3.2 %collective-permute-start.12 = (bf16[32,16,512]{2,1,0:T(8,128)(2,1)S(1)}, bf16[32,16,512]{2,1,0:T(8,128)(2,1)S(1)}, u32[]{:S(2)}, u32[]{:S(2)}) collective-permute-start(bf16[32,16,512]{2,1,0:T(8,128)(2,1)S(1)} %bitcast.9), channel_id=1, source_target_pairs={{0,96},{32,0},{64,32},{96,64},{1,97},{33,1},{65,33},{97,65},{2,98}... | collective-permute-start | bytes 1572872 | tf_op jit(solution)/shard_map/ppermute | solution.py:240
  183.3 2.1 collective-permute-start.11
  186.6 8.4 %collective-permute-done.13.refs_3_ = bf16[32,16,512]{2,1,0:T(8,128)(2,1)S(1)} collective-permute-done((bf16[32,16,512]{2,1,0:T(8,128)(2,1)S(1)}, bf16[32,16,512]{2,1,0:T(8,128)(2,1)S(1)}, u32[]{:S(2)}, u32[]{:S(2)}) %collective-permute-start.13) | collective-permute-done | bytes 524320 | tf_op jit(solution)/shard_map/ppermute | solution.py:239
  195.1 3.3 %collective-permute-start.15 = (bf16[16,16,512]{2,1,0:T(8,128)(2,1)S(1)}, bf16[16,16,512]{2,1,0:T(8,128)(2,1)S(1)}, u32[]{:S(2)}, u32[]{:S(2)}) collective-permute-start(bf16[16,16,512]{2,1,0:T(8,128)(2,1)S(1)} %slice.19), channel_id=1, source_target_pairs={{0,96},{32,0},{64,32},{96,64},{1,97},{33,1},{65,33},{97,65},{2,98}... | collective-permute-start | bytes 786440 | tf_op jit(solution)/shard_map/ppermute | solution.py:270
  198.4 5.9 %shard_map.91 = (f32[3,512,512]{2,1,0:T(8,128)}, f32[3,512,512]{2,1,0:T(8,128)}) custom-call(bf16[32,1,16,512]{3,2,1,0:T(8,128)(2,1)S(1)} %all-to-all-done.held_first.held, bf16[32,2,16,512]{3,2,1,0:T(8,128)(2,1)S(1)} %all_to_all.20.held_rest.held, f32[3,512,512]{2,1,0:T(8,128)S(1)} %copy-done.6, f32[3,512,512]{2,1,0:T(8,128)} %right.3), custom_call_target="tpu_custom_call" | custom-call | flops 1610612736 | bytes 14155776 | tf_op jit(solution)/shard_map/pallas_call | solution.py:287
  204.3 5.5 %collective-permute-done.14.refs_4_ = bf16[16,16,512]{2,1,0:T(8,128)(2,1)S(1)} collective-permute-done((bf16[16,16,512]{2,1,0:T(8,128)(2,1)S(1)}, bf16[16,16,512]{2,1,0:T(8,128)(2,1)S(1)}, u32[]{:S(2)}, u32[]{:S(2)}) %collective-permute-start.14) | collective-permute-done | bytes 262176 | tf_op jit(solution)/shard_map/ppermute | solution.py:269
  209.9 2.7 %shard_map.95.refs_4_ = bf16[256,16,512]{2,1,0:T(8,128)(2,1)} custom-call(s32[128]{0:T(128)S(1)} %select_reduce_fusion.1.table.refs_0_, bf16[32,16,512]{2,1,0:T(8,128)(2,1)S(1)} %bitcast.10, bf16[32,16,512]{2,1,0:T(8,128)(2,1)S(1)} %collective-permute-done.12.refs_2_, bf16[32,16,512]{2,1,0:T(8,128)(2,1)S(1)} %collective-permute-done.13.refs_3_, ...), custom_call_target="tpu_custom_call" | custom-call | bytes 4194304 | tf_op jit(solution)/shard_map/pallas_call | solution.py:249
  212.6 51.8 %shard_map.96.refs_3_ = bf16[256,16,512]{2,1,0:T(8,128)(2,1)} custom-call(s32[224]{0:T(256)S(1)} %select_reduce_fusion.table.refs_0_, bf16[56,16,512]{2,1,0:T(8,128)(2,1)} %shard_map.93.refs_1_, bf16[56,16,512]{2,1,0:T(8,128)(2,1)} %collective-permute-done.10.refs_2_, ...), custom_call_target="tpu_custom_call", output_to_operand_aliasing={{}: (4, {})} | custom-call | bytes 5505024 | tf_op jit(solution)/shard_map/pallas_call | solution.py:249
  264.4 1.6 shard_map.97
  (46 shorter events, 13.9 us)
Async XLA Ops:
  2.6 2.2 copy-start
  7.0 13.7 %collective-permute-start.4 = (bf16[28,16,512]{2,1,0:T(8,128)(2,1)S(1)}, bf16[28,16,512]{2,1,0:T(8,128)(2,1)S(1)}, u32[]{:S(2)}, u32[]{:S(2)}) collective-permute-start(bf16[28,16,512]{2,1,0:T(8,128)(2,1)S(1)} %get-tuple-element.17), channel_id=1, source_target_pairs={{0,32},{32,64},{64,96},{96,0},{1,33},{33,65},{65,97},{97,1},{2,34}... | collective-permute-start | bytes 1376264 | tf_op jit(solution)/shard_map/ppermute | solution.py:197
  8.7 12.0 %collective-permute-start.5 = (bf16[28,16,512]{2,1,0:T(8,128)(2,1)S(1)}, bf16[28,16,512]{2,1,0:T(8,128)(2,1)S(1)}, u32[]{:S(2)}, u32[]{:S(2)}) collective-permute-start(bf16[28,16,512]{2,1,0:T(8,128)(2,1)S(1)} %get-tuple-element.18), channel_id=1, source_target_pairs={{0,96},{32,0},{64,32},{96,64},{1,97},{33,1},{65,33},{97,65},{2,98}... | collective-permute-start | bytes 1376264 | tf_op jit(solution)/shard_map/ppermute | solution.py:198
  24.4 22.6 %collective-permute-start.6 = (bf16[56,16,512]{2,1,0:T(8,128)(2,1)S(1)}, bf16[56,16,512]{2,1,0:T(8,128)(2,1)S(1)}, u32[]{:S(2)}, u32[]{:S(2)}) collective-permute-start(bf16[56,16,512]{2,1,0:T(8,128)(2,1)S(1)} %get-tuple-element.19), channel_id=1, source_target_pairs={{0,32},{32,64},{64,96},{96,0},{1,33},{33,65},{65,97},{97,1},{2,34}... | collective-permute-start | bytes 2752520 | tf_op jit(solution)/shard_map/ppermute | solution.py:208
  25.6 21.4 %collective-permute-start.7 = (bf16[56,16,512]{2,1,0:T(8,128)(2,1)S(1)}, bf16[56,16,512]{2,1,0:T(8,128)(2,1)S(1)}, u32[]{:S(2)}, u32[]{:S(2)}) collective-permute-start(bf16[56,16,512]{2,1,0:T(8,128)(2,1)S(1)} %get-tuple-element.20), channel_id=1, source_target_pairs={{0,96},{32,0},{64,32},{96,64},{1,97},{33,1},{65,33},{97,65},{2,98}... | collective-permute-start | bytes 2752520 | tf_op jit(solution)/shard_map/ppermute | solution.py:209
  47.0 28.3 %copy-start.2 = (bf16[3,512,512]{2,1,0:T(8,128)(2,1)S(1)}, bf16[3,512,512]{2,1,0:T(8,128)(2,1)}, u32[]{:S(2)}) copy-start(bf16[3,512,512]{2,1,0:T(8,128)(2,1)} %left.5) | copy-start | bytes 4718596
  47.0 28.3 %copy-start.3 = (bf16[3,512,512]{2,1,0:T(8,128)(2,1)S(1)}, bf16[3,512,512]{2,1,0:T(8,128)(2,1)}, u32[]{:S(2)}) copy-start(bf16[3,512,512]{2,1,0:T(8,128)(2,1)} %right.5) | copy-start | bytes 4718596
  77.9 1.0 copy-start.5
  78.8 38.8 %all-to-all-start.2 = ((bf16[32,2,16,512]{3,2,1,0:T(8,128)(2,1)}), bf16[32,2,16,512]{3,2,1,0:T(8,128)(2,1)}, u32[]{:S(2)}, u32[]{:S(2)}) async-start(bf16[32,2,16,512]{3,2,1,0:T(8,128)(2,1)} %copy-done.5), calls=%async_computation.2 | async-start | bytes 2097152 | tf_op jit(solution)/shard_map/all_to_all | solution.py:221
  83.6 2.2 copy-start.1
  87.3 10.0 %collective-permute-start = (bf16[16,16,512]{2,1,0:T(8,128)(2,1)S(1)}, bf16[16,16,512]{2,1,0:T(8,128)(2,1)S(1)}, u32[]{:S(2)}, u32[]{:S(2)}) collective-permute-start(bf16[16,16,512]{2,1,0:T(8,128)(2,1)S(1)} %get-tuple-element.13), channel_id=1, source_target_pairs={{0,32},{32,64},{64,96},{96,0},{1,33},{33,65},{65,97},{97,1},{2,34}... | collective-permute-start | bytes 786440 | tf_op jit(solution)/shard_map/ppermute | solution.py:197
  88.5 8.8 %collective-permute-start.1 = (bf16[16,16,512]{2,1,0:T(8,128)(2,1)S(1)}, bf16[16,16,512]{2,1,0:T(8,128)(2,1)S(1)}, u32[]{:S(2)}, u32[]{:S(2)}) collective-permute-start(bf16[16,16,512]{2,1,0:T(8,128)(2,1)S(1)} %get-tuple-element.14), channel_id=1, source_target_pairs={{0,96},{32,0},{64,32},{96,64},{1,97},{33,1},{65,33},{97,65},{2,98}... | collective-permute-start | bytes 786440 | tf_op jit(solution)/shard_map/ppermute | solution.py:198
  99.9 14.8 %collective-permute-start.2 = (bf16[32,16,512]{2,1,0:T(8,128)(2,1)S(1)}, bf16[32,16,512]{2,1,0:T(8,128)(2,1)S(1)}, u32[]{:S(2)}, u32[]{:S(2)}) collective-permute-start(bf16[32,16,512]{2,1,0:T(8,128)(2,1)S(1)} %get-tuple-element.15), channel_id=1, source_target_pairs={{0,32},{32,64},{64,96},{96,0},{1,33},{33,65},{65,97},{97,1},{2,34}... | collective-permute-start | bytes 1572872 | tf_op jit(solution)/shard_map/ppermute | solution.py:208
  101.1 13.6 %collective-permute-start.3 = (bf16[32,16,512]{2,1,0:T(8,128)(2,1)S(1)}, bf16[32,16,512]{2,1,0:T(8,128)(2,1)S(1)}, u32[]{:S(2)}, u32[]{:S(2)}) collective-permute-start(bf16[32,16,512]{2,1,0:T(8,128)(2,1)S(1)} %get-tuple-element.16), channel_id=1, source_target_pairs={{0,96},{32,0},{64,32},{96,64},{1,97},{33,1},{65,33},{97,65},{2,98}... | collective-permute-start | bytes 1572872 | tf_op jit(solution)/shard_map/ppermute | solution.py:209
  116.8 0.8 copy-start.7
  117.6 39.9 %all-to-all-start = ((bf16[32,1,16,512]{3,2,1,0:T(8,128)(2,1)}), bf16[32,1,16,512]{3,2,1,0:T(8,128)(2,1)S(1)}, u32[]{:S(2)}, u32[]{:S(2)}) async-start(bf16[32,1,16,512]{3,2,1,0:T(8,128)(2,1)} %copy-done.7), calls=%async_computation | async-start | bytes 1048576 | tf_op jit(solution)/shard_map/all_to_all | solution.py:221
  154.5 27.8 %collective-permute-start.10 = (bf16[56,16,512]{2,1,0:T(8,128)(2,1)}, bf16[56,16,512]{2,1,0:T(8,128)(2,1)}, u32[]{:S(2)}, u32[]{:S(2)}) collective-permute-start(bf16[56,16,512]{2,1,0:T(8,128)(2,1)} %shard_map.93.refs_1_), channel_id=1, source_target_pairs={{0,96},{32,0},{64,32},{96,64},{1,97},{33,1},{65,33},{97,65},{2,98}... | collective-permute-start | bytes 2752520 | tf_op jit(solution)/shard_map/ppermute | solution.py:240
  157.5 27.9 %collective-permute-start.8 = (bf16[56,16,512]{2,1,0:T(8,128)(2,1)}, bf16[56,16,512]{2,1,0:T(8,128)(2,1)}, u32[]{:S(2)}, u32[]{:S(2)}) collective-permute-start(bf16[56,16,512]{2,1,0:T(8,128)(2,1)} %shard_map.93.refs_1_), channel_id=1, source_target_pairs={{0,32},{32,64},{64,96},{96,0},{1,33},{33,65},{65,97},{97,1},{2,34}... | collective-permute-start | bytes 2752520 | tf_op jit(solution)/shard_map/ppermute | solution.py:239
  157.5 1.4 copy-start.4
  158.9 39.5 %copy-start.6 = (f32[3,512,512]{2,1,0:T(8,128)S(1)}, f32[3,512,512]{2,1,0:T(8,128)}, u32[]{:S(2)}) copy-start(f32[3,512,512]{2,1,0:T(8,128)} %left.3) | copy-start | bytes 9437188
  179.0 16.0 %collective-permute-start.13 = (bf16[32,16,512]{2,1,0:T(8,128)(2,1)S(1)}, bf16[32,16,512]{2,1,0:T(8,128)(2,1)S(1)}, u32[]{:S(2)}, u32[]{:S(2)}) collective-permute-start(bf16[32,16,512]{2,1,0:T(8,128)(2,1)S(1)} %bitcast.8), channel_id=1, source_target_pairs={{0,32},{32,64},{64,96},{96,0},{1,33},{33,65},{65,97},{97,1},{2,34}... | collective-permute-start | bytes 1572872 | tf_op jit(solution)/shard_map/ppermute | solution.py:239
  179.0 16.1 %collective-permute-start.12 = (bf16[32,16,512]{2,1,0:T(8,128)(2,1)S(1)}, bf16[32,16,512]{2,1,0:T(8,128)(2,1)S(1)}, u32[]{:S(2)}, u32[]{:S(2)}) collective-permute-start(bf16[32,16,512]{2,1,0:T(8,128)(2,1)S(1)} %bitcast.9), channel_id=1, source_target_pairs={{0,96},{32,0},{64,32},{96,64},{1,97},{33,1},{65,33},{97,65},{2,98}... | collective-permute-start | bytes 1572872 | tf_op jit(solution)/shard_map/ppermute | solution.py:240
  183.3 81.1 %collective-permute-start.11 = (bf16[28,16,512]{2,1,0:T(8,128)(2,1)S(1)}, bf16[28,16,512]{2,1,0:T(8,128)(2,1)S(1)}, u32[]{:S(2)}, u32[]{:S(2)}) collective-permute-start(bf16[28,16,512]{2,1,0:T(8,128)(2,1)S(1)} %slice.17), channel_id=1, source_target_pairs={{0,96},{32,0},{64,32},{96,64},{1,97},{33,1},{65,33},{97,65},{2,98}... | collective-permute-start | bytes 1376264 | tf_op jit(solution)/shard_map/ppermute | solution.py:283
  186.5 77.9 %collective-permute-start.9 = (bf16[28,16,512]{2,1,0:T(8,128)(2,1)S(1)}, bf16[28,16,512]{2,1,0:T(8,128)(2,1)S(1)}, u32[]{:S(2)}, u32[]{:S(2)}) collective-permute-start(bf16[28,16,512]{2,1,0:T(8,128)(2,1)S(1)} %slice.16), channel_id=1, source_target_pairs={{0,32},{32,64},{64,96},{96,0},{1,33},{33,65},{65,97},{97,1},{2,34}... | collective-permute-start | bytes 1376264 | tf_op jit(solution)/shard_map/ppermute | solution.py:282
  195.0 14.9 %collective-permute-start.14 = (bf16[16,16,512]{2,1,0:T(8,128)(2,1)S(1)}, bf16[16,16,512]{2,1,0:T(8,128)(2,1)S(1)}, u32[]{:S(2)}, u32[]{:S(2)}) collective-permute-start(bf16[16,16,512]{2,1,0:T(8,128)(2,1)S(1)} %slice.18), channel_id=1, source_target_pairs={{0,32},{32,64},{64,96},{96,0},{1,33},{33,65},{65,97},{97,1},{2,34}... | collective-permute-start | bytes 786440 | tf_op jit(solution)/shard_map/ppermute | solution.py:269
  195.1 14.7 %collective-permute-start.15 = (bf16[16,16,512]{2,1,0:T(8,128)(2,1)S(1)}, bf16[16,16,512]{2,1,0:T(8,128)(2,1)S(1)}, u32[]{:S(2)}, u32[]{:S(2)}) collective-permute-start(bf16[16,16,512]{2,1,0:T(8,128)(2,1)S(1)} %slice.19), channel_id=1, source_target_pairs={{0,96},{32,0},{64,32},{96,64},{1,97},{33,1},{65,33},{97,65},{2,98}... | collective-permute-start | bytes 786440 | tf_op jit(solution)/shard_map/ppermute | solution.py:270

commit v2 on v0

v2 whole, which is shorter than its diff:
```python
import functools

import jax
import jax.numpy as jnp
from jax import lax
from jax.experimental import pallas as pl
from jax.experimental.pallas import tpu as pltpu
from jax.sharding import PartitionSpec as P

epsilon = 1e-06
decay_rate = 0.9

ANY = pl.BlockSpec(memory_space=pl.ANY)
HBM = pl.BlockSpec(memory_space=pltpu.HBM)
SMEM = pl.BlockSpec(memory_space=pltpu.SMEM)
VMEM = pl.BlockSpec(memory_space=pltpu.VMEM)
F32 = jnp.float32
MIB = 1024 * 1024


def cost(nbytes, flops=0):
    return pl.CostEstimate(flops=flops, bytes_accessed=nbytes, transcendentals=0)


def fetch(rows, table, start, count, into, sem, last):
    def one(j, _):
        block = jnp.minimum(table[start + j], last)
        pltpu.make_async_copy(rows.at[block], into.at[j], sem).start()
        return 0

    lax.fori_loop(0, count, one, 0, unroll=4)


def first_kernel(size, table, rows, low, high, sems):
    last = rows.shape[0] - 1
    half = size // 2
    fetch(rows, table, 2 * size, half, low, sems.at[0], last)
    fetch(rows, table, 2 * size + half, half, high, sems.at[1], last)
    pltpu.make_async_copy(low, low, sems.at[0]).wait()
    pltpu.make_async_copy(high, high, sems.at[1]).wait()


def lay_kernel(plan, table, rows):
    last = rows.shape[0] - 1
    for start, out in plan:

        def one(j, _, start=start, out=out):
            out[j] = rows[jnp.minimum(table[start + j], last)]
            return 0

        lax.fori_loop(0, out.shape[0], one, 0, unroll=4)


def second_kernel(got_low, got_high, low_rows, high_rows, low, high):
    def one(j, _):
        low[j] = (low_rows[j].astype(F32) + got_low[j].astype(F32)).astype(low.dtype)
        high[j] = (high_rows[j].astype(F32) + got_high[j].astype(F32)).astype(high.dtype)
        return 0

    lax.fori_loop(0, low.shape[0], one, 0, unroll=4)


def second_whole_kernel(got_low, got_high, up_rows, down_rows, up, down):
    half = got_low.shape[0]

    def one(j, _):
        k = half + j
        up[j] = (up_rows[j].astype(F32) + got_low[j].astype(F32)).astype(up.dtype)
        down[k] = (down_rows[k].astype(F32) + got_high[j].astype(F32)).astype(down.dtype)
        return 0

    lax.fori_loop(0, half, one, 0, unroll=4)


def third_first_kernel(size, last, table, own, up_low, up_high, down_low, down_high, out):
    half = size // 2
    for first, from_up, from_down in ((0, up_low, down_low), (half, up_high, down_high)):

        def one(k, _, first=first, from_up=from_up, from_down=from_down):
            j = first + k
            total = own[j].astype(F32) + from_up[k].astype(F32) + from_down[k].astype(F32)
            out[j, 0] = jnp.where(table[j] <= last, total, 0.0).astype(out.dtype)
            return 0

        lax.fori_loop(0, half, one, 0, unroll=4)


def third_kernel(size, base, last, table, place, own, from_up, from_down, back, out):
    depth = out.shape[1]

    def clear(j, _):
        for part in range(depth - 1):
            out[j, part] = jnp.zeros_like(out[j, part])
        out[j, depth - 1] = back[j, 0]
        return 0

    lax.fori_loop(0, out.shape[0], clear, 0, unroll=4)
    count = lax.fori_loop(0, size, lambda j, n: n + jnp.where(table[j] <= last, 1, 0), 0, unroll=8)

    def some(i, _):
        for lane in range(4):
            j = jnp.minimum(4 * i + lane, count - 1)
            where = place[table[j]]
            total = own[j].astype(F32) + from_up[j].astype(F32) + from_down[j].astype(F32)
            out[where & 31, (where >> 5) - base] = total.astype(out.dtype)
        return 0

    lax.fori_loop(0, (count + 3) // 4, some, 0)


def pack_kernel(half, base, last, table, place, returned, low, high):
    for first, out in ((0, low), (half, high)):

        def one(j, _, first=first, out=out):
            where = place[jnp.minimum(table[first + j], last)]
            layer = jnp.maximum((where >> 5) - base, 0)
            out[j] = returned[where & 31, layer]
            return 0

        lax.fori_loop(0, half, one, 0, unroll=4)


def take_kernel(part, mixed, low, high):
    half = low.shape[0]

    def one(j, _):
        low[j] = mixed[j, part]
        high[j] = mixed[half + j, part]
        return 0

    lax.fori_loop(0, half, one, 0, unroll=4)


def place_kernel(plan, last, table, *refs):
    sources, out, sem = refs[: len(plan)], refs[-2], refs[-1]

    def each(act):
        for source, (start, count, shift) in zip(sources, plan):

            def one(j, _, source=source, start=start, shift=shift):
                block = table[start + j]

                @pl.when(block <= last)
                def _():
                    act(pltpu.make_async_copy(source.at[shift + j], out.at[block], sem))

                return 0

            lax.fori_loop(0, count, one, 0)

    each(lambda copy: copy.start())
    each(lambda copy: copy.wait())


def apply_kernel(held, left, right, shaped):
    order = left.shape[-1]
    block = held[...].reshape(order, order)
    applied = jnp.dot(left[0], block, preferred_element_type=F32).astype(jnp.bfloat16)
    product = jnp.dot(applied, right[0], preferred_element_type=F32)
    wide = block.astype(F32)
    count = order * order
    held_power = jnp.sum(wide * wide) / count
    power = jnp.sum(product * product) / count
    scale = jnp.sqrt((held_power + epsilon) / (power + epsilon))
    shaped[...] = (product * scale).astype(jnp.bfloat16).reshape(shaped.shape)


def gram_kernel(held_first, held_rest, left, right, new_left, new_right):
    order = left.shape[-1]
    block = jnp.where(pl.program_id(0) == 0, held_first[...], held_rest[...]).reshape(order, order)
    weight = (1.0 - decay_rate) / order
    left_gram = lax.dot_general(block, block, (((1,), (1,)), ((), ())), preferred_element_type=F32)
    right_gram = lax.dot_general(block, block, (((0,), (0,)), ((), ())), preferred_element_type=F32)
    new_left[0] = decay_rate * left[0] + weight * left_gram
    new_right[0] = decay_rate * right[0] + weight * right_gram


def local(grads, owner, factor_left, factor_right, precond_left, precond_right):
    rows = grads[0]
    blocks, band, width = rows.shape
    columns = lax.axis_size("fsdp")
    replicas = lax.axis_size("rep")
    my_rep = lax.axis_index("rep")
    slots = factor_left.shape[0]
    last = blocks - 1
    up_pairs = [(i, (i + 1) % replicas) for i in range(replicas)]
    down_pairs = [(i, (i - 1) % replicas) for i in range(replicas)]
    far_pairs = [(i, (i + 2) % replicas) for i in range(replicas)]

    position = jnp.arange(blocks, dtype=jnp.int32)
    earlier = position[None, :] < position[:, None]
    same_owner = (owner[:, None] == owner[None, :]) & earlier
    col_rank = jnp.sum(same_owner.astype(jnp.int32), axis=1)
    rep_of = col_rank % replicas
    local_slot = col_rank // replicas
    relative = (rep_of - my_rep) % replicas
    place = local_slot * columns + owner

    def listed(key, size):
        hits = key[None, :] == jnp.arange(size, dtype=jnp.int32)[:, None]
        return jnp.min(jnp.where(hits, position[None, :], blocks), axis=1)

    size_first = columns
    by_column = relative * columns + owner
    table_first = listed(jnp.where(local_slot == 0, by_column, -1), replicas * columns)

    def packed(member, size):
        same_list = (rep_of[:, None] == rep_of[None, :]) & member[None, :] & earlier
        in_list = jnp.sum(same_list.astype(jnp.int32), axis=1)
        return listed(jnp.where(member, relative * size + in_list, -1), replicas * size)

    size_rest = 56
    table_rest = packed(local_slot > 0, size_rest)

    def piece(*count):
        return jax.ShapeDtypeStruct((*count, band, width), jnp.bfloat16)

    def nbytes(count):
        return count * band * width * 2

    token = jax.ShapeDtypeStruct((8, 128), F32)

    def call(kernel, results, operands, specs, out_specs, scratch=(), after=(), moved=0, flops=0, grid=None, aliases=None, limit=16):
        count, late = len(operands), len(after)
        n_out = len(results)
        small = pl.BlockSpec((8, 128), lambda *_: (0, 0)) if grid else VMEM

        def body(*refs):
            outs = refs[count + late : count + late + n_out]
            mark = refs[count + late + n_out]
            mark[...] = jnp.zeros_like(mark)
            kernel(*refs[:count], *outs, *refs[count + late + n_out + 1 :])

        extra = {} if grid is None else {"grid": grid}
        return pl.pallas_call(
            body,
            out_shape=(*results, token),
            in_specs=list(specs) + [ANY] * late,
            out_specs=(*out_specs, small),
            scratch_shapes=list(scratch),
            input_output_aliases=aliases or {},
            compiler_params=pltpu.CompilerParams(vmem_limit_bytes=limit * MIB),
            cost_estimate=pl.CostEstimate(flops=flops, bytes_accessed=moved, transcendentals=0),
            **extra,
        )(*operands, *after)

    def tip(x):
        return x[0, :16, :128]

    def both_ways(up, down):
        return lax.ppermute(up, "rep", up_pairs), lax.ppermute(down, "rep", down_pairs)

    def half_plan(size):
        return [(relative * size + first, size // 2, 0) for relative in (0, 1, 3, 2) for first in (0, size // 2)]

    def tip(x):
        return x[0, :16, :128]

    def both_ways(up, down):
        return lax.ppermute(up, "rep", up_pairs), lax.ppermute(down, "rep", down_pairs)

    def half_plan(size):
        return [(relative * size + first, size // 2, 0) for relative in (0, 1, 3, 2) for first in (0, size // 2)]

    def far_plan(size):
        half = size // 2
        return [(2 * size, half, 0), (2 * size + half, half, 0)]

    def exchange(x):
        return lax.all_to_all(x, "fsdp", split_axis=0, concat_axis=0, tiled=True)

    def applied(held, base, depth, order_after):
        strip = pl.BlockSpec((columns, 1, band, width), lambda s: (0, s, 0, 0))
        matrix = pl.BlockSpec((1, order, order), lambda s: (s + base, 0, 0))
        return call(
            apply_kernel,
            (piece(columns, depth),),
            (held, precond_left, precond_right),
            (strip, matrix, matrix),
            (strip,),
            after=order_after,
            grid=(depth,),
            limit=24,
        )

    def placed(table, plan, sources, out, after=()):
        operands = (table, *sources) if out is None else (table, *sources, out)
        specs = [SMEM] + [VMEM] * len(sources) + ([] if out is None else [HBM])

        def kernel(*refs):
            place_kernel(plan, last, *refs[: 1 + len(plan)], *refs[-2:])

        return call(
            kernel,
            (piece(blocks),),
            operands,
            specs,
            (HBM,),
            [pltpu.SemaphoreType.DMA],
            after,
            nbytes(2 * sum(p[1] for p in plan)),
            aliases=None if out is None else {1 + len(sources): 0},
        )

    order = factor_left.shape[1]
    depth_rest = slots - 1
    half_first, half_rest = size_first // 2, size_rest // 2
    low_first, high_first, mark = call(
        functools.partial(first_kernel, size_first),
        (piece(half_first), piece(half_first)),
        (table_first, rows),
        (SMEM, HBM),
        (VMEM, VMEM),
        [pltpu.SemaphoreType.DMA((2,))],
        moved=nbytes(2 * size_first),
        limit=60,
    )
    got_low_first, got_high_first = both_ways(low_first, high_first)

    def lay(table, size, parts, marks):
        def kernel(table, rows, *outs):
            lay_kernel([(p[0] * size + p[1], out) for p, out in zip(parts, outs)], table, rows)

        return call(
            kernel,
            tuple(piece(p[-1]) for p in parts),
            (table, rows),
            (SMEM, VMEM),
            (VMEM,) * len(parts),
            after=marks,
            moved=nbytes(2 * sum(p[-1] for p in parts)),
        )

    plain_up, plain_down, near_low, near_high, mine_first, mark = lay(
        table_first,
        size_first,
        [
            (1, half_first, half_first),
            (3, 0, half_first),
            (1, 0, half_first),
            (3, half_first, half_first),
            (0, 0, size_first),
        ],
        (mark,),
    )
    up_high, down_low = both_ways(plain_up, plain_down)
    low, high, mark = call(
        second_kernel,
        (piece(half_first), piece(half_first)),
        (got_low_first, got_high_first, near_low, near_high),
        (VMEM,) * 4,
        (VMEM, VMEM),
        moved=nbytes(3 * size_first),
    )
    up_low, down_high = both_ways(low, high)
    low_rest, high_rest, up_rest, down_rest, mine_rest, mark = lay(
        table_rest,
        size_rest,
        [
            (2, 0, half_rest),
            (2, half_rest, half_rest),
            (1, 0, size_rest),
            (3, 0, size_rest),
            (0, 0, size_rest),
        ],
        (mark,),
    )
    got_low_rest, got_high_rest = both_ways(low_rest, high_rest)
    sent_first, mark = call(
        functools.partial(third_first_kernel, size_first, last),
        (piece(columns, 1),),
        (table_first, mine_first, up_low, up_high, down_low, down_high),
        (SMEM,) + (VMEM,) * 5,
        (VMEM,),
        after=(mark,),
        moved=nbytes(4 * size_first),
    )
    held_first = exchange(sent_first)
    up, down, mark = call(
        second_whole_kernel,
        (piece(size_rest), piece(size_rest)),
        (got_low_rest, got_high_rest, up_rest, down_rest),
        (VMEM,) * 4,
        (VMEM, VMEM),
        after=(mark,),
        moved=nbytes(3 * size_rest),
        aliases={2: 0, 3: 1},
    )
    from_up, from_down = both_ways(up, down)
    shaped_first, mark = applied(held_first, 0, 1, ())
    sent_rest, mark = call(
        functools.partial(third_kernel, size_rest, 1, last),
        (piece(columns, slots),),
        (table_rest, place, mine_rest, from_up, from_down, shaped_first),
        (SMEM, SMEM, VMEM, VMEM, VMEM, VMEM),
        (VMEM,),
        moved=nbytes(5 * size_rest),
    )
    mixed = exchange(sent_rest)
    own_low, own_high, mark = call(
        functools.partial(take_kernel, slots - 1),
        (piece(half_first), piece(half_first)),
        (mixed,),
        (VMEM,),
        (VMEM, VMEM),
        moved=nbytes(2 * size_first),
    )
    below_low, above_high = both_ways(own_low, own_high)
    below_high, above_low = both_ways(own_high, own_low)
    far_low, far_high = both_ways(below_low, above_high)
    shaped_rest, mark = applied(mixed, 1, depth_rest, (mark,))
    back_rest = exchange(shaped_rest)
    direction, mark_placed = placed(
        table_first,
        half_plan(size_first),
        [own_low, own_high, above_low, above_high, below_low, below_high, far_low, far_high],
        None,
    )

    low, high, mark = call(
        functools.partial(pack_kernel, half_rest, 1, last),
        (piece(half_rest), piece(half_rest)),
        (table_rest, place, back_rest),
        (SMEM, SMEM, VMEM),
        (VMEM, VMEM),
        after=(mark_placed,),
        moved=nbytes(2 * size_rest),
    )
    below_low, above_high = both_ways(low, high)
    below_high, above_low = both_ways(high, low)
    far_low, far_high = both_ways(below_low, above_high)

    matrix = pl.BlockSpec((1, order, order), lambda s: (s, 0, 0))
    new_left, new_right, mark_gram = call(
        gram_kernel,
        (
            jax.ShapeDtypeStruct(factor_left.shape, F32),
            jax.ShapeDtypeStruct(factor_right.shape, F32),
        ),
        (held_first, mixed, factor_left, factor_right),
        (
            pl.BlockSpec((columns, 1, band, width), lambda s: (0, 0, 0, 0)),
            pl.BlockSpec((columns, 1, band, width), lambda s: (0, jnp.maximum(s - 1, 0), 0, 0)),
            matrix,
            matrix,
        ),
        (matrix, matrix),
        after=(mark,),
        moved=slots * 18 * order * order,
        flops=slots * 4 * order**3,
        grid=(slots,),
        limit=32,
    )

    plan = half_plan(size_rest)
    direction, _ = placed(
        table_rest, plan[:6], [low, high, above_low, above_high, below_low, below_high], direction
    )
    direction, _ = placed(table_rest, plan[6:], [far_low, far_high], direction)
    return (new_left, new_right, direction)


def solution(mesh):
    placed = (
        P("rep", None, "fsdp", None),
        P(),
        P(("rep", "fsdp"), None, None),
        P(("rep", "fsdp"), None, None),
        P(("rep", "fsdp"), None, None),
        P(("rep", "fsdp"), None, None),
    )
    return jax.shard_map(
        local,
        mesh=mesh,
        in_specs=placed,
        out_specs=(
            P(("rep", "fsdp"), None, None),
            P(("rep", "fsdp"), None, None),
            P(None, "fsdp", None),
        ),
        check_vma=False,
    )
```

time: 262 us -> 167 us (0.64)
  waiting for transfers between devices: 151 us -> 43.1 us
  starting transfers between devices: 0.08 us -> 35 us
  Pallas kernels: 0 us -> 26.8 us
  between operations: 14.2 us -> 0.81 us
  matrix products: 12.7 us -> 0 us
  blocking collectives: 56.4 us -> 47.7 us
  local copies, waits for them, and re-layouts: 17.4 us -> 9.29 us
  other arithmetic: 8.91 us -> 3.33 us
    psum x1 -> x0, waiting for transfers between devices: 95.9 us -> none  [local(): lax.psum(grads[0].astype(jnp.float32).astype(jnp.bfloat16), 'rep')]
    all_gather x1 -> x0, waiting for transfers between devices: 54.4 us -> none  [local(): everyone = lax.all_gather(returned, 'rep', axis=0, tiled=True)]
    ppermute x0 -> x22, waiting for transfers between devices: none -> 43.1 us  [the longest x11 25.5 us: both_ways(): lax.ppermute(up, 'rep', up_pairs)]
    ppermute x0 -> x22, starting transfers between devices: none -> 31.1 us  [the longest x11 22.1 us: both_ways(): lax.ppermute(down, 'rep', down_pairs)]
    pallas_call x0 -> x15, Pallas kernels: none -> 26.8 us  [call(): pl.pallas_call(body, out_shape=(*results, token), in_specs=list(specs) +...]
    dot_general x3 -> x0, matrix products: 12.7 us -> none  [the longest x1 5.06 us: local(): jnp.einsum('sik,skj->sij', left_applied, precond_right, preferred_element...]
    all_to_all x2, blocking collectives: 56.4 us -> 47.7 us  [exchange(): return lax.all_to_all(x, 'fsdp', split_axis=0, concat_axis=0, tiled=True)]
    gather x2 -> x0, local copies, waits for them, and re-layouts: 8.52 us -> none  [the longest x1 5.62 us: local(): direction = jnp.take(all_rows, pick_index, axis=0)]
  transfers between devices with their start and end apart: 2 -> 23, of which waited for: 2 -> 11; matrix products, arithmetic and copies ran while one was open for 4% -> 0% of each run, Pallas kernels for 0% -> 9%
where the time goes in v2:
time: 167 us; the launch traced here: 166 us
  blocking collectives  47.7 us (29%)
  waiting for transfers between devices  43.1 us (26%)
  starting transfers between devices  35 us (21%)
  Pallas kernels  26.8 us (16%)
  local copies, waits for them, and re-layouts  9.29 us (6%)
  other arithmetic  3.33 us (2%)
    all_to_all x2, blocking collectives, exchange(): return lax.all_to_all(x, 'fsdp', split_axis=0, concat_axis=0, tiled=True)  47.7 us
    pallas_call x15, Pallas kernels, call(): pl.pallas_call(body, out_shape=(*results, token), in_specs=list(specs) +...  26.8 us
    ppermute x11, waiting for transfers between devices, both_ways(): lax.ppermute(up, 'rep', up_pairs)  25.5 us
    ppermute x11, starting transfers between devices, both_ways(): lax.ppermute(down, 'rep', down_pairs)  22.1 us
    ppermute x11, waiting for transfers between devices, both_ways(): lax.ppermute(down, 'rep', down_pairs)  17.6 us
    unnamed x22, local copies, waits for them, and re-layouts  9.29 us
    ppermute x11, starting transfers between devices, both_ways(): lax.ppermute(up, 'rep', up_pairs)  8.94 us
    all_to_all x1, starting transfers between devices, exchange(): return lax.all_to_all(x, 'fsdp', split_axis=0, concat_axis=0, tiled=True)  3.93 us
  transfers between devices with their start and end apart: 23, of which 11 were waited for; matrix products, arithmetic and copies ran while one was open for 0% of the time, Pallas kernels for 9%

profile of v2, /device:TPU:0, one launch (start us, length us, event | category | flops | bytes accessed | tf_op | source)
XLA Modules:
  0.0 166.1 jit_solution(5203554310756960021)
XLA Ops:
  3.6 2.6 %shard_map.85 = (bf16[16,16,512]{2,1,0:T(8,128)(2,1)}, bf16[16,16,512]{2,1,0:T(8,128)(2,1)}, f32[8,128]{1,0:T(8,128)}) custom-call(s32[128]{0:T(128)} %select_reduce_fusion.1.refs_0_, bf16[256,16,512]{2,1,0:T(8,128)(2,1)} %bitcast.1), custom_call_target="tpu_custom_call" | custom-call | bytes 1048576 | tf_op jit(solution)/shard_map/pallas_call | solution.py:235
  6.3 1.7 %collective-permute-start = (bf16[16,16,512]{2,1,0:T(8,128)(2,1)}, bf16[16,16,512]{2,1,0:T(8,128)(2,1)S(1)}, u32[]{:S(2)}, u32[]{:S(2)}) collective-permute-start(bf16[16,16,512]{2,1,0:T(8,128)(2,1)} %get-tuple-element.41), channel_id=1, source_target_pairs={{0,32},{32,64},{64,96},{96,0},{1,33},{33,65},{65,97},{97,1},{2,34}... | collective-permute-start | bytes 786440 | tf_op jit(solution)/shard_map/ppermute | solution.py:260
  9.6 2.2 %copy-done = bf16[1,256,16,512]{3,2,1,0:T(8,128)(2,1)S(1)} copy-done((bf16[1,256,16,512]{3,2,1,0:T(8,128)(2,1)S(1)}, bf16[1,256,16,512]{3,2,1,0:T(8,128)(2,1)}, u32[]{:S(2)}) %copy-start) | copy-done | bytes 4194328
  17.3 1.6 collective-permute-start.6
  19.0 1.7 collective-permute-start.7
  20.6 1.8 %collective-permute-start.4 = (bf16[16,16,512]{2,1,0:T(8,128)(2,1)S(1)}, bf16[16,16,512]{2,1,0:T(8,128)(2,1)S(1)}, u32[]{:S(2)}, u32[]{:S(2)}) collective-permute-start(bf16[16,16,512]{2,1,0:T(8,128)(2,1)S(1)} %get-tuple-element.47), channel_id=1, source_target_pairs={{0,96},{32,0},{64,32},{96,64},{1,97},{33,1},{65,33},{97,65},{2,98}... | collective-permute-start | bytes 786440 | tf_op jit(solution)/shard_map/ppermute | solution.py:260
  22.7 1.6 collective-permute-done.3.refs_3_
  25.7 12.3 %collective-permute-done.4.refs_4_ = bf16[16,16,512]{2,1,0:T(8,128)(2,1)S(1)} collective-permute-done((bf16[16,16,512]{2,1,0:T(8,128)(2,1)S(1)}, bf16[16,16,512]{2,1,0:T(8,128)(2,1)S(1)}, u32[]{:S(2)}, u32[]{:S(2)}) %collective-permute-start.4) | collective-permute-done | bytes 262176 | tf_op jit(solution)/shard_map/ppermute | solution.py:260
  38.2 2.8 %collective-permute-done.5.refs_5_ = bf16[16,16,512]{2,1,0:T(8,128)(2,1)S(1)} collective-permute-done((bf16[16,16,512]{2,1,0:T(8,128)(2,1)S(1)}, bf16[16,16,512]{2,1,0:T(8,128)(2,1)S(1)}, u32[]{:S(2)}, u32[]{:S(2)}) %collective-permute-start.5) | collective-permute-done | bytes 262176 | tf_op jit(solution)/shard_map/ppermute | solution.py:260
  44.0 2.0 %collective-permute-start.9 = (bf16[56,16,512]{2,1,0:T(8,128)(2,1)S(1)}, bf16[56,16,512]{2,1,0:T(8,128)(2,1)S(1)}, u32[]{:S(2)}, u32[]{:S(2)}) collective-permute-start(bf16[56,16,512]{2,1,0:T(8,128)(2,1)S(1)} %get-tuple-element.59), channel_id=1, source_target_pairs={{0,96},{32,0},{64,32},{96,64},{1,97},{33,1},{65,33},{97,65},{2,98}... | collective-permute-start | bytes 2752520 | tf_op jit(solution)/shard_map/ppermute | solution.py:260
  46.0 19.6 %all_to_all.15.refs_0_ = bf16[32,1,16,512]{3,2,1,0:T(8,128)(2,1)S(1)} all-to-all(bf16[32,1,16,512]{3,2,1,0:T(8,128)(2,1)S(1)} %get-tuple-element.51), channel_id=1, replica_groups=mesh['rep'=4,'fsdp'=32] {'fsdp'}, dimensions={0} | all-to-all | bytes 1048576 | tf_op jit(solution)/shard_map/all_to_all | solution.py:270
  67.1 1.7 %shard_map.92 = (bf16[32,3,16,512]{3,2,1,0:T(8,128)(2,1)S(1)}, f32[8,128]{1,0:T(8,128)}) custom-call(s32[224]{0:T(256)S(1)} %select_reduce_fusion.refs_0_, s32[256]{0:T(256)S(1)} %get-tuple-element.75.refs_1_, bf16[56,16,512]{2,1,0:T(8,128)(2,1)S(1)} %get-tuple-element.52.refs_2_, bf16[56,16,512]{2,1,0:T(8,128)(2,1)S(1)} %collective-permute-done.8.refs_3_, ...), custom_call_target="tpu_custom_call" | custom-call | bytes 4587520 | tf_op jit(solution)/shard_map/pallas_call | solution.py:235
  68.8 28.1 %all_to_all.16.refs_0_.refs_1_ = bf16[32,3,16,512]{3,2,1,0:T(8,128)(2,1)S(1)} all-to-all(bf16[32,3,16,512]{3,2,1,0:T(8,128)(2,1)S(1)} %get-tuple-element.61), channel_id=1, replica_groups=mesh['rep'=4,'fsdp'=32] {'fsdp'}, dimensions={0} | all-to-all | bytes 3145728 | tf_op jit(solution)/shard_map/all_to_all | solution.py:270
  97.7 3.1 %shard_map.94 = (bf16[32,2,16,512]{3,2,1,0:T(8,128)(2,1)S(1)}, f32[8,128]{1,0:T(8,128)}) custom-call(bf16[32,3,16,512]{3,2,1,0:T(8,128)(2,1)S(1)} %all_to_all.16.refs_0_.refs_1_, bf16[3,512,512]{2,1,0:T(8,128)(2,1)S(1)} %copy-done.2, bf16[3,512,512]{2,1,0:T(8,128)(2,1)S(1)} %copy-done.3, f32[8,128]{1,0:T(8,128)S(1)} %get-tuple-element.62.refs_3_), custom_call_target="tpu_custom_call" | custom-call | tf_op jit(solution)/shard_map/pallas_call | solution.py:235
  101.7 3.9 %all-to-all-start.2 = ((bf16[32,2,16,512]{3,2,1,0:T(8,128)(2,1)}), bf16[32,2,16,512]{3,2,1,0:T(8,128)(2,1)S(1)}, u32[]{:S(2)}, u32[]{:S(2)}) async-start(bf16[32,2,16,512]{3,2,1,0:T(8,128)(2,1)} %copy-done.6), calls=%async_computation.2 | async-start | bytes 2097152 | tf_op jit(solution)/shard_map/all_to_all | solution.py:270
  106.9 2.1 %collective-permute-start.11 = (bf16[16,16,512]{2,1,0:T(8,128)(2,1)}, bf16[16,16,512]{2,1,0:T(8,128)(2,1)S(1)}, u32[]{:S(2)}, u32[]{:S(2)}) collective-permute-start(bf16[16,16,512]{2,1,0:T(8,128)(2,1)} %copy-done.7), channel_id=1, source_target_pairs={{0,96},{32,0},{64,32},{96,64},{1,97},{33,1},{65,33},{97,65},{2,98}... | collective-permute-start | bytes 786440 | tf_op jit(solution)/shard_map/ppermute | solution.py:260
  109.0 1.6 collective-permute-start.10
  111.0 5.1 %collective-permute-done.12.refs_5_ = bf16[16,16,512]{2,1,0:T(8,128)(2,1)S(1)} collective-permute-done((bf16[16,16,512]{2,1,0:T(8,128)(2,1)S(1)}, bf16[16,16,512]{2,1,0:T(8,128)(2,1)S(1)}, u32[]{:S(2)}, u32[]{:S(2)}) %collective-permute-start.12) | collective-permute-done | bytes 262176 | tf_op jit(solution)/shard_map/ppermute | solution.py:260
  116.3 3.3 %collective-permute-start.15 = (bf16[16,16,512]{2,1,0:T(8,128)(2,1)S(1)}, bf16[16,16,512]{2,1,0:T(8,128)(2,1)S(1)}, u32[]{:S(2)}, u32[]{:S(2)}) collective-permute-start(bf16[16,16,512]{2,1,0:T(8,128)(2,1)S(1)} %collective-permute-done.11.refs_4_), channel_id=1, source_target_pairs={{0,96},{32,0},{64,32},{96,64},{1,97},{33,1},{65,33},{97,65},{2,98}... | collective-permute-start | bytes 786440 | tf_op jit(solution)/shard_map/ppermute | solution.py:260
  119.6 2.3 %collective-permute-done.10.refs_3_ = bf16[16,16,512]{2,1,0:T(8,128)(2,1)S(1)} collective-permute-done((bf16[16,16,512]{2,1,0:T(8,128)(2,1)S(1)}, bf16[16,16,512]{2,1,0:T(8,128)(2,1)S(1)}, u32[]{:S(2)}, u32[]{:S(2)}) %collective-permute-start.10) | collective-permute-done | bytes 262176 | tf_op jit(solution)/shard_map/ppermute | solution.py:260
  121.9 4.7 %collective-permute-done.14.refs_7_ = bf16[16,16,512]{2,1,0:T(8,128)(2,1)S(1)} collective-permute-done((bf16[16,16,512]{2,1,0:T(8,128)(2,1)S(1)}, bf16[16,16,512]{2,1,0:T(8,128)(2,1)S(1)}, u32[]{:S(2)}, u32[]{:S(2)}) %collective-permute-start.14) | collective-permute-done | bytes 262176 | tf_op jit(solution)/shard_map/ppermute | solution.py:260
  127.5 2.7 %shard_map.95 = (bf16[256,16,512]{2,1,0:T(8,128)(2,1)}, f32[8,128]{1,0:T(8,128)S(1)}) custom-call(s32[128]{0:T(128)S(1)} %copy-done.9, bf16[16,16,512]{2,1,0:T(8,128)(2,1)S(1)} %get-tuple-element.64.refs_1_, bf16[16,16,512]{2,1,0:T(8,128)(2,1)S(1)} %copy-done.8, bf16[16,16,512]{2,1,0:T(8,128)(2,1)S(1)} %collective-permute-done.10.refs_3_, ...), custom_call_target="tpu_custom_call" | custom-call | bytes 4194304 | tf_op jit(solution)/shard_map/pallas_call | solution.py:235
  132.7 1.7 %collective-permute-start.18 = (bf16[28,16,512]{2,1,0:T(8,128)(2,1)S(1)}, bf16[28,16,512]{2,1,0:T(8,128)(2,1)S(1)}, u32[]{:S(2)}, u32[]{:S(2)}) collective-permute-start(bf16[28,16,512]{2,1,0:T(8,128)(2,1)S(1)} %get-tuple-element.71.refs_2_), channel_id=1, source_target_pairs={{0,96},{32,0},{64,32},{96,64},{1,97},{33,1},{65,33},{97,65},{2,98}... | collective-permute-start | bytes 1376264 | tf_op jit(solution)/shard_map/ppermute | solution.py:260
  134.5 1.9 %collective-permute-start.20 = (bf16[28,16,512]{2,1,0:T(8,128)(2,1)S(1)}, bf16[28,16,512]{2,1,0:T(8,128)(2,1)S(1)}, u32[]{:S(2)}, u32[]{:S(2)}) collective-permute-start(bf16[28,16,512]{2,1,0:T(8,128)(2,1)S(1)} %get-tuple-element.70.refs_1_), channel_id=1, source_target_pairs={{0,96},{32,0},{64,32},{96,64},{1,97},{33,1},{65,33},{97,65},{2,98}... | collective-permute-start | bytes 1376264 | tf_op jit(solution)/shard_map/ppermute | solution.py:260
  136.5 9.4 %collective-permute-done.16.refs_5_ = bf16[28,16,512]{2,1,0:T(8,128)(2,1)S(1)} collective-permute-done((bf16[28,16,512]{2,1,0:T(8,128)(2,1)S(1)}, bf16[28,16,512]{2,1,0:T(8,128)(2,1)S(1)}, u32[]{:S(2)}, u32[]{:S(2)}) %collective-permute-start.16) | collective-permute-done | bytes 458784 | tf_op jit(solution)/shard_map/ppermute | solution.py:260
  146.2 3.0 %collective-permute-start.19 = (bf16[28,16,512]{2,1,0:T(8,128)(2,1)S(1)}, bf16[28,16,512]{2,1,0:T(8,128)(2,1)S(1)}, u32[]{:S(2)}, u32[]{:S(2)}) collective-permute-start(bf16[28,16,512]{2,1,0:T(8,128)(2,1)S(1)} %collective-permute-done.18.refs_4_), channel_id=1, source_target_pairs={{0,96},{32,0},{64,32},{96,64},{1,97},{33,1},{65,33},{97,65},{2,98}... | collective-permute-start | bytes 1376264 | tf_op jit(solution)/shard_map/ppermute | solution.py:260
  149.1 1.9 %copy-done.4 = f32[3,512,512]{2,1,0:T(8,128)S(1)} copy-done((f32[3,512,512]{2,1,0:T(8,128)S(1)}, f32[3,512,512]{2,1,0:T(8,128)}, u32[]{:S(2)}) %copy-start.4) | copy-done | bytes 3145752
  151.0 1.9 %copy-done.5 = f32[3,512,512]{2,1,0:T(8,128)S(1)} copy-done((f32[3,512,512]{2,1,0:T(8,128)S(1)}, f32[3,512,512]{2,1,0:T(8,128)}, u32[]{:S(2)}) %copy-start.5) | copy-done | bytes 3145752
  152.9 3.7 %shard_map.97 = (f32[3,512,512]{2,1,0:T(8,128)}, f32[3,512,512]{2,1,0:T(8,128)}, f32[8,128]{1,0:T(8,128)}) custom-call(bf16[32,1,16,512]{3,2,1,0:T(8,128)(2,1)S(1)} %all_to_all.15.refs_0_, bf16[32,3,16,512]{3,2,1,0:T(8,128)(2,1)S(1)} %all_to_all.16.refs_0_.refs_1_, f32[3,512,512]{2,1,0:T(8,128)S(1)} %copy-done.4, f32[3,512,512]{2,1,0:T(8,128)S(1)} %copy-done.5, ...), custom_call_target="tpu_custom_call" | custom-call | flops 1610612736 | bytes 14155776 | tf_op jit(solution)/shard_map/pallas_call | solution.py:235
  156.6 4.0 %shard_map.98 = (bf16[256,16,512]{2,1,0:T(8,128)(2,1)}, f32[8,128]{1,0:T(8,128)}) custom-call(s32[224]{0:T(256)S(1)} %select_reduce_fusion.refs_0_, bf16[28,16,512]{2,1,0:T(8,128)(2,1)S(1)} %get-tuple-element.70.refs_1_, bf16[28,16,512]{2,1,0:T(8,128)(2,1)S(1)} %get-tuple-element.71.refs_2_, ...), custom_call_target="tpu_custom_call", output_to_operand_aliasing={{0}: (7, {})} | custom-call | bytes 5505024 | tf_op jit(solution)/shard_map/pallas_call | solution.py:235
  160.6 3.2 %collective-permute-done.17.refs_1_ = bf16[28,16,512]{2,1,0:T(8,128)(2,1)S(1)} collective-permute-done((bf16[28,16,512]{2,1,0:T(8,128)(2,1)S(1)}, bf16[28,16,512]{2,1,0:T(8,128)(2,1)S(1)}, u32[]{:S(2)}, u32[]{:S(2)}) %collective-permute-start.17) | collective-permute-done | bytes 458784 | tf_op jit(solution)/shard_map/ppermute | solution.py:260
  163.8 2.3 %shard_map.99 = (bf16[256,16,512]{2,1,0:T(8,128)(2,1)}, f32[8,128]{1,0:T(8,128)}) custom-call(s32[224]{0:T(256)S(1)} %select_reduce_fusion.refs_0_, bf16[28,16,512]{2,1,0:T(8,128)(2,1)S(1)} %collective-permute-done.17.refs_1_, bf16[28,16,512]{2,1,0:T(8,128)(2,1)S(1)} %collective-permute-done.19.refs_2_, ...), custom_call_target="tpu_custom_call", output_to_operand_aliasing={{0}: (3, {})} | custom-call | bytes 1835008 | tf_op jit(solution)/shard_map/pallas_call | solution.py:235
  (61 shorter events, 23.6 us)
Async XLA Ops:
  3.6 5.9 %copy-start.9 = (s32[128]{0:T(128)S(1)}, s32[128]{0:T(128)}, u32[]{:S(2)}) copy-start(s32[128]{0:T(128)} %select_reduce_fusion.1.refs_0_) | copy-start | bytes 1540
  6.3 9.7 %collective-permute-start = (bf16[16,16,512]{2,1,0:T(8,128)(2,1)}, bf16[16,16,512]{2,1,0:T(8,128)(2,1)S(1)}, u32[]{:S(2)}, u32[]{:S(2)}) collective-permute-start(bf16[16,16,512]{2,1,0:T(8,128)(2,1)} %get-tuple-element.41), channel_id=1, source_target_pairs={{0,32},{32,64},{64,96},{96,0},{1,33},{33,65},{65,97},{97,1},{2,34}... | collective-permute-start | bytes 786440 | tf_op jit(solution)/shard_map/ppermute | solution.py:260
  8.0 8.0 %collective-permute-start.1 = (bf16[16,16,512]{2,1,0:T(8,128)(2,1)}, bf16[16,16,512]{2,1,0:T(8,128)(2,1)S(1)}, u32[]{:S(2)}, u32[]{:S(2)}) collective-permute-start(bf16[16,16,512]{2,1,0:T(8,128)(2,1)} %get-tuple-element.42), channel_id=1, source_target_pairs={{0,96},{32,0},{64,32},{96,64},{1,97},{33,1},{65,33},{97,65},{2,98}... | collective-permute-start | bytes 786440 | tf_op jit(solution)/shard_map/ppermute | solution.py:260
  9.6 2.2 %copy-start = (bf16[1,256,16,512]{3,2,1,0:T(8,128)(2,1)S(1)}, bf16[1,256,16,512]{3,2,1,0:T(8,128)(2,1)}, u32[]{:S(2)}) copy-start(bf16[1,256,16,512]{3,2,1,0:T(8,128)(2,1)} %param.6) | copy-start | bytes 12582916
  12.4 3.7 %copy-start.1 = (bf16[1,256,16,512]{3,2,1,0:T(8,128)(2,1)S(1)}, bf16[1,256,16,512]{3,2,1,0:T(8,128)(2,1)}, u32[]{:S(2)}) copy-start(bf16[1,256,16,512]{3,2,1,0:T(8,128)(2,1)} %param.6) | copy-start | bytes 12582916
  13.9 10.5 %collective-permute-start.3 = (bf16[16,16,512]{2,1,0:T(8,128)(2,1)S(1)}, bf16[16,16,512]{2,1,0:T(8,128)(2,1)S(1)}, u32[]{:S(2)}, u32[]{:S(2)}) collective-permute-start(bf16[16,16,512]{2,1,0:T(8,128)(2,1)S(1)} %get-tuple-element.46), channel_id=1, source_target_pairs={{0,32},{32,64},{64,96},{96,0},{1,33},{33,65},{65,97},{97,1},{2,34}... | collective-permute-start | bytes 786440 | tf_op jit(solution)/shard_map/ppermute | solution.py:260
  17.3 48.3 %copy-start.2 = (bf16[3,512,512]{2,1,0:T(8,128)(2,1)S(1)}, bf16[3,512,512]{2,1,0:T(8,128)(2,1)}, u32[]{:S(2)}) copy-start(bf16[3,512,512]{2,1,0:T(8,128)(2,1)} %refs_1_.3) | copy-start | bytes 4718596
  17.3 48.3 %copy-start.3 = (bf16[3,512,512]{2,1,0:T(8,128)(2,1)S(1)}, bf16[3,512,512]{2,1,0:T(8,128)(2,1)}, u32[]{:S(2)}) copy-start(bf16[3,512,512]{2,1,0:T(8,128)(2,1)} %refs_2_.4) | copy-start | bytes 4718596
  17.3 24.5 %collective-permute-start.6 = (bf16[28,16,512]{2,1,0:T(8,128)(2,1)S(1)}, bf16[28,16,512]{2,1,0:T(8,128)(2,1)S(1)}, u32[]{:S(2)}, u32[]{:S(2)}) collective-permute-start(bf16[28,16,512]{2,1,0:T(8,128)(2,1)S(1)} %get-tuple-element.53), channel_id=1, source_target_pairs={{0,32},{32,64},{64,96},{96,0},{1,33},{33,65},{65,97},{97,1},{2,34}... | collective-permute-start | bytes 1376264 | tf_op jit(solution)/shard_map/ppermute | solution.py:260
  19.0 22.8 %collective-permute-start.7 = (bf16[28,16,512]{2,1,0:T(8,128)(2,1)S(1)}, bf16[28,16,512]{2,1,0:T(8,128)(2,1)S(1)}, u32[]{:S(2)}, u32[]{:S(2)}) collective-permute-start(bf16[28,16,512]{2,1,0:T(8,128)(2,1)S(1)} %get-tuple-element.54), channel_id=1, source_target_pairs={{0,96},{32,0},{64,32},{96,64},{1,97},{33,1},{65,33},{97,65},{2,98}... | collective-permute-start | bytes 1376264 | tf_op jit(solution)/shard_map/ppermute | solution.py:260
  20.6 17.4 %collective-permute-start.4 = (bf16[16,16,512]{2,1,0:T(8,128)(2,1)S(1)}, bf16[16,16,512]{2,1,0:T(8,128)(2,1)S(1)}, u32[]{:S(2)}, u32[]{:S(2)}) collective-permute-start(bf16[16,16,512]{2,1,0:T(8,128)(2,1)S(1)} %get-tuple-element.47), channel_id=1, source_target_pairs={{0,96},{32,0},{64,32},{96,64},{1,97},{33,1},{65,33},{97,65},{2,98}... | collective-permute-start | bytes 786440 | tf_op jit(solution)/shard_map/ppermute | solution.py:260
  22.5 15.7 %collective-permute-start.2 = (bf16[16,16,512]{2,1,0:T(8,128)(2,1)S(1)}, bf16[16,16,512]{2,1,0:T(8,128)(2,1)S(1)}, u32[]{:S(2)}, u32[]{:S(2)}) collective-permute-start(bf16[16,16,512]{2,1,0:T(8,128)(2,1)S(1)} %get-tuple-element.45), channel_id=1, source_target_pairs={{0,32},{32,64},{64,96},{96,0},{1,33},{33,65},{65,97},{97,1},{2,34}... | collective-permute-start | bytes 786440 | tf_op jit(solution)/shard_map/ppermute | solution.py:260
  24.3 16.7 %collective-permute-start.5 = (bf16[16,16,512]{2,1,0:T(8,128)(2,1)S(1)}, bf16[16,16,512]{2,1,0:T(8,128)(2,1)S(1)}, u32[]{:S(2)}, u32[]{:S(2)}) collective-permute-start(bf16[16,16,512]{2,1,0:T(8,128)(2,1)S(1)} %get-tuple-element.48), channel_id=1, source_target_pairs={{0,96},{32,0},{64,32},{96,64},{1,97},{33,1},{65,33},{97,65},{2,98}... | collective-permute-start | bytes 786440 | tf_op jit(solution)/shard_map/ppermute | solution.py:260
  42.7 24.4 %collective-permute-start.8 = (bf16[56,16,512]{2,1,0:T(8,128)(2,1)S(1)}, bf16[56,16,512]{2,1,0:T(8,128)(2,1)S(1)}, u32[]{:S(2)}, u32[]{:S(2)}) collective-permute-start(bf16[56,16,512]{2,1,0:T(8,128)(2,1)S(1)} %get-tuple-element.58), channel_id=1, source_target_pairs={{0,32},{32,64},{64,96},{96,0},{1,33},{33,65},{65,97},{97,1},{2,34}... | collective-permute-start | bytes 2752520 | tf_op jit(solution)/shard_map/ppermute | solution.py:260
  44.0 23.1 %collective-permute-start.9 = (bf16[56,16,512]{2,1,0:T(8,128)(2,1)S(1)}, bf16[56,16,512]{2,1,0:T(8,128)(2,1)S(1)}, u32[]{:S(2)}, u32[]{:S(2)}) collective-permute-start(bf16[56,16,512]{2,1,0:T(8,128)(2,1)S(1)} %get-tuple-element.59), channel_id=1, source_target_pairs={{0,96},{32,0},{64,32},{96,64},{1,97},{33,1},{65,33},{97,65},{2,98}... | collective-permute-start | bytes 2752520 | tf_op jit(solution)/shard_map/ppermute | solution.py:260
  100.8 1.0 copy-start.6
  101.7 28.5 %all-to-all-start.2 = ((bf16[32,2,16,512]{3,2,1,0:T(8,128)(2,1)}), bf16[32,2,16,512]{3,2,1,0:T(8,128)(2,1)S(1)}, u32[]{:S(2)}, u32[]{:S(2)}) async-start(bf16[32,2,16,512]{3,2,1,0:T(8,128)(2,1)} %copy-done.6), calls=%async_computation.2 | async-start | bytes 2097152 | tf_op jit(solution)/shard_map/all_to_all | solution.py:270
  105.7 10.4 %collective-permute-start.12 = (bf16[16,16,512]{2,1,0:T(8,128)(2,1)S(1)}, bf16[16,16,512]{2,1,0:T(8,128)(2,1)S(1)}, u32[]{:S(2)}, u32[]{:S(2)}) collective-permute-start(bf16[16,16,512]{2,1,0:T(8,128)(2,1)S(1)} %get-tuple-element.64.refs_1_), channel_id=1, source_target_pairs={{0,32},{32,64},{64,96},{96,0},{1,33},{33,65},{65,97},{97,1},{2,34}... | collective-permute-start | bytes 786440 | tf_op jit(solution)/shard_map/ppermute | solution.py:260
  106.9 9.4 %collective-permute-start.11 = (bf16[16,16,512]{2,1,0:T(8,128)(2,1)}, bf16[16,16,512]{2,1,0:T(8,128)(2,1)S(1)}, u32[]{:S(2)}, u32[]{:S(2)}) collective-permute-start(bf16[16,16,512]{2,1,0:T(8,128)(2,1)} %copy-done.7), channel_id=1, source_target_pairs={{0,96},{32,0},{64,32},{96,64},{1,97},{33,1},{65,33},{97,65},{2,98}... | collective-permute-start | bytes 786440 | tf_op jit(solution)/shard_map/ppermute | solution.py:260
  109.0 12.9 %collective-permute-start.10 = (bf16[16,16,512]{2,1,0:T(8,128)(2,1)S(1)}, bf16[16,16,512]{2,1,0:T(8,128)(2,1)S(1)}, u32[]{:S(2)}, u32[]{:S(2)}) collective-permute-start(bf16[16,16,512]{2,1,0:T(8,128)(2,1)S(1)} %get-tuple-element.64.refs_1_), channel_id=1, source_target_pairs={{0,96},{32,0},{64,32},{96,64},{1,97},{33,1},{65,33},{97,65},{2,98}... | collective-permute-start | bytes 786440 | tf_op jit(solution)/shard_map/ppermute | solution.py:260
  110.6 11.3 %collective-permute-start.13 = (bf16[16,16,512]{2,1,0:T(8,128)(2,1)}, bf16[16,16,512]{2,1,0:T(8,128)(2,1)S(1)}, u32[]{:S(2)}, u32[]{:S(2)}) collective-permute-start(bf16[16,16,512]{2,1,0:T(8,128)(2,1)} %copy-done.7), channel_id=1, source_target_pairs={{0,32},{32,64},{64,96},{96,0},{1,33},{33,65},{65,97},{97,1},{2,34}... | collective-permute-start | bytes 786440 | tf_op jit(solution)/shard_map/ppermute | solution.py:260
  116.1 10.5 %collective-permute-start.14 = (bf16[16,16,512]{2,1,0:T(8,128)(2,1)S(1)}, bf16[16,16,512]{2,1,0:T(8,128)(2,1)S(1)}, u32[]{:S(2)}, u32[]{:S(2)}) collective-permute-start(bf16[16,16,512]{2,1,0:T(8,128)(2,1)S(1)} %collective-permute-done.12.refs_5_), channel_id=1, source_target_pairs={{0,32},{32,64},{64,96},{96,0},{1,33},{33,65},{65,97},{97,1},{2,34}... | collective-permute-start | bytes 786440 | tf_op jit(solution)/shard_map/ppermute | solution.py:260
  116.3 10.3 %collective-permute-start.15 = (bf16[16,16,512]{2,1,0:T(8,128)(2,1)S(1)}, bf16[16,16,512]{2,1,0:T(8,128)(2,1)S(1)}, u32[]{:S(2)}, u32[]{:S(2)}) collective-permute-start(bf16[16,16,512]{2,1,0:T(8,128)(2,1)S(1)} %collective-permute-done.11.refs_4_), channel_id=1, source_target_pairs={{0,96},{32,0},{64,32},{96,64},{1,97},{33,1},{65,33},{97,65},{2,98}... | collective-permute-start | bytes 786440 | tf_op jit(solution)/shard_map/ppermute | solution.py:260
  126.6 1.0 copy-start.8
  131.1 14.7 %collective-permute-start.16 = (bf16[28,16,512]{2,1,0:T(8,128)(2,1)S(1)}, bf16[28,16,512]{2,1,0:T(8,128)(2,1)S(1)}, u32[]{:S(2)}, u32[]{:S(2)}) collective-permute-start(bf16[28,16,512]{2,1,0:T(8,128)(2,1)S(1)} %get-tuple-element.70.refs_1_), channel_id=1, source_target_pairs={{0,32},{32,64},{64,96},{96,0},{1,33},{33,65},{65,97},{97,1},{2,34}... | collective-permute-start | bytes 1376264 | tf_op jit(solution)/shard_map/ppermute | solution.py:260
  132.7 13.5 %collective-permute-start.18 = (bf16[28,16,512]{2,1,0:T(8,128)(2,1)S(1)}, bf16[28,16,512]{2,1,0:T(8,128)(2,1)S(1)}, u32[]{:S(2)}, u32[]{:S(2)}) collective-permute-start(bf16[28,16,512]{2,1,0:T(8,128)(2,1)S(1)} %get-tuple-element.71.refs_2_), channel_id=1, source_target_pairs={{0,96},{32,0},{64,32},{96,64},{1,97},{33,1},{65,33},{97,65},{2,98}... | collective-permute-start | bytes 1376264 | tf_op jit(solution)/shard_map/ppermute | solution.py:260
  134.5 22.1 %collective-permute-start.20 = (bf16[28,16,512]{2,1,0:T(8,128)(2,1)S(1)}, bf16[28,16,512]{2,1,0:T(8,128)(2,1)S(1)}, u32[]{:S(2)}, u32[]{:S(2)}) collective-permute-start(bf16[28,16,512]{2,1,0:T(8,128)(2,1)S(1)} %get-tuple-element.70.refs_1_), channel_id=1, source_target_pairs={{0,96},{32,0},{64,32},{96,64},{1,97},{33,1},{65,33},{97,65},{2,98}... | collective-permute-start | bytes 1376264 | tf_op jit(solution)/shard_map/ppermute | solution.py:260
  136.4 20.2 %collective-permute-start.21 = (bf16[28,16,512]{2,1,0:T(8,128)(2,1)S(1)}, bf16[28,16,512]{2,1,0:T(8,128)(2,1)S(1)}, u32[]{:S(2)}, u32[]{:S(2)}) collective-permute-start(bf16[28,16,512]{2,1,0:T(8,128)(2,1)S(1)} %get-tuple-element.71.refs_2_), channel_id=1, source_target_pairs={{0,32},{32,64},{64,96},{96,0},{1,33},{33,65},{65,97},{97,1},{2,34}... | collective-permute-start | bytes 1376264 | tf_op jit(solution)/shard_map/ppermute | solution.py:260
  145.9 18.0 %collective-permute-start.17 = (bf16[28,16,512]{2,1,0:T(8,128)(2,1)S(1)}, bf16[28,16,512]{2,1,0:T(8,128)(2,1)S(1)}, u32[]{:S(2)}, u32[]{:S(2)}) collective-permute-start(bf16[28,16,512]{2,1,0:T(8,128)(2,1)S(1)} %collective-permute-done.16.refs_5_), channel_id=1, source_target_pairs={{0,32},{32,64},{64,96},{96,0},{1,33},{33,65},{65,97},{97,1},{2,34}... | collective-permute-start | bytes 1376264 | tf_op jit(solution)/shard_map/ppermute | solution.py:260
  146.2 17.7 %collective-permute-start.19 = (bf16[28,16,512]{2,1,0:T(8,128)(2,1)S(1)}, bf16[28,16,512]{2,1,0:T(8,128)(2,1)S(1)}, u32[]{:S(2)}, u32[]{:S(2)}) collective-permute-start(bf16[28,16,512]{2,1,0:T(8,128)(2,1)S(1)} %collective-permute-done.18.refs_4_), channel_id=1, source_target_pairs={{0,96},{32,0},{64,32},{96,64},{1,97},{33,1},{65,33},{97,65},{2,98}... | collective-permute-start | bytes 1376264 | tf_op jit(solution)/shard_map/ppermute | solution.py:260
  149.1 1.9 %copy-start.4 = (f32[3,512,512]{2,1,0:T(8,128)S(1)}, f32[3,512,512]{2,1,0:T(8,128)}, u32[]{:S(2)}) copy-start(f32[3,512,512]{2,1,0:T(8,128)} %refs_2_.5) | copy-start | bytes 9437188
  151.0 1.9 %copy-start.5 = (f32[3,512,512]{2,1,0:T(8,128)S(1)}, f32[3,512,512]{2,1,0:T(8,128)}, u32[]{:S(2)}) copy-start(f32[3,512,512]{2,1,0:T(8,128)} %refs_3_.1) | copy-start | bytes 9437188
  (2 other events, 1.4 us)

commit v3 on v2

--- a/solution.py
+++ b/solution.py
@@ -22,86 +22,82 @@
     return pl.CostEstimate(flops=flops, bytes_accessed=nbytes, transcendentals=0)
 
 
-def fetch(rows, table, start, count, into, sem, last):
-    def one(j, _):
-        block = jnp.minimum(table[start + j], last)
-        pltpu.make_async_copy(rows.at[block], into.at[j], sem).start()
+def batched(count, read, write, batch=4):
+    def some(i, _):
+        pieces = [read(batch * i + lane) for lane in range(batch)]
+        for lane in range(batch):
+            write(batch * i + lane, pieces[lane])
         return 0
 
-    lax.fori_loop(0, count, one, 0, unroll=4)
-
-
-def first_kernel(size, table, rows, low, high, sems):
-    last = rows.shape[0] - 1
-    half = size // 2
-    fetch(rows, table, 2 * size, half, low, sems.at[0], last)
-    fetch(rows, table, 2 * size + half, half, high, sems.at[1], last)
-    pltpu.make_async_copy(low, low, sems.at[0]).wait()
-    pltpu.make_async_copy(high, high, sems.at[1]).wait()
-
-
-def lay_kernel(plan, table, rows):
+    lax.fori_loop(0, count // batch, some, 0)
+
+
+def put(out, *where):
+    def write(j, piece):
+        out[(j, *where)] = piece.astype(out.dtype)
+
+    return write
+
+
+def lay_kernel(plan, table, rows, zeros):
     last = rows.shape[0] - 1
     for start, out in plan:
 
-        def one(j, _, start=start, out=out):
-            out[j] = rows[jnp.minimum(table[start + j], last)]
-            return 0
-
-        lax.fori_loop(0, out.shape[0], one, 0, unroll=4)
+        def read(j, start=start):
+            block = table[start + j]
+            piece = rows[jnp.minimum(block, last)]
+            return jnp.where(block <= last, piece, jnp.zeros_like(piece)) if zeros else piece
+
+        batched(out.shape[0], read, put(out))
 
 
 def second_kernel(got_low, got_high, low_rows, high_rows, low, high):
-    def one(j, _):
-        low[j] = (low_rows[j].astype(F32) + got_low[j].astype(F32)).astype(low.dtype)
-        high[j] = (high_rows[j].astype(F32) + got_high[j].astype(F32)).astype(high.dtype)
-        return 0
-
-    lax.fori_loop(0, low.shape[0], one, 0, unroll=4)
+    for got, own, out in ((got_low, low_rows, low), (got_high, high_rows, high)):
+        batched(
+            out.shape[0],
+            lambda j, got=got, own=own: own[j].astype(F32) + got[j].astype(F32),
+            put(out),
+        )
 
 
 def second_whole_kernel(got_low, got_high, up_rows, down_rows, up, down):
     half = got_low.shape[0]
 
-    def one(j, _):
-        k = half + j
-        up[j] = (up_rows[j].astype(F32) + got_low[j].astype(F32)).astype(up.dtype)
-        down[k] = (down_rows[k].astype(F32) + got_high[j].astype(F32)).astype(down.dtype)
-        return 0
-
-    lax.fori_loop(0, half, one, 0, unroll=4)
-
-
-def third_first_kernel(size, last, table, own, up_low, up_high, down_low, down_high, out):
-    half = size // 2
+    def write_up(j, piece):
+        up[half + j] = piece
+
+    def write_down(j, piece):
+        down[half + j] = piece.astype(down.dtype)
+
+    batched(half, lambda j: up_rows[j].astype(F32) + got_low[j].astype(F32), put(up))
+    batched(half, lambda j: up_rows[half + j], write_up)
+    batched(half, lambda j: down_rows[j], put(down))
+    batched(half, lambda j: down_rows[half + j].astype(F32) + got_high[j].astype(F32), write_down)
+
+
+def third_first_kernel(own, up_low, up_high, down_low, down_high, out):
+    half = up_low.shape[0]
     for first, from_up, from_down in ((0, up_low, down_low), (half, up_high, down_high)):
 
-        def one(k, _, first=first, from_up=from_up, from_down=from_down):
-            j = first + k
-            total = own[j].astype(F32) + from_up[k].astype(F32) + from_down[k].astype(F32)
-            out[j, 0] = jnp.where(table[j] <= last, total, 0.0).astype(out.dtype)
-            return 0
-
-        lax.fori_loop(0, half, one, 0, unroll=4)
-
-
-def third_kernel(size, base, last, table, place, own, from_up, from_down, back, out):
-    depth = out.shape[1]
-
-    def clear(j, _):
-        for part in range(depth - 1):
-            out[j, part] = jnp.zeros_like(out[j, part])
-        out[j, depth - 1] = back[j, 0]
-        return 0
-
-    lax.fori_loop(0, out.shape[0], clear, 0, unroll=4)
+        def read(k, first=first, from_up=from_up, from_down=from_down):
+            return own[first + k].astype(F32) + from_up[k].astype(F32) + from_down[k].astype(F32)
+
+        def write(k, piece, first=first):
+            out[first + k, 0] = piece.astype(out.dtype)
+
+        batched(half, read, write)
+
+
+def third_kernel(size, base, last, table, place, own, from_up, from_down, out):
+    for part in range(out.shape[1]):
+        batched(out.shape[0], lambda j: jnp.zeros(out.shape[2:], F32), put(out, part))
     count = lax.fori_loop(0, size, lambda j, n: n + jnp.where(table[j] <= last, 1, 0), 0, unroll=8)
 
     def some(i, _):
-        for lane in range(4):
-            j = jnp.minimum(4 * i + lane, count - 1)
+        entries = [jnp.minimum(4 * i + lane, count - 1) for lane in range(4)]
+        totals = [own[j].astype(F32) + from_up[j].astype(F32) + from_down[j].astype(F32) for j in entries]
+        for j, total in zip(entries, totals):
             where = place[table[j]]
-            total = own[j].astype(F32) + from_up[j].astype(F32) + from_down[j].astype(F32)
             out[where & 31, (where >> 5) - base] = total.astype(out.dtype)
         return 0
 
@@ -111,24 +107,17 @@
 def pack_kernel(half, base, last, table, place, returned, low, high):
     for first, out in ((0, low), (half, high)):
 
-        def one(j, _, first=first, out=out):
+        def read(j, first=first):
             where = place[jnp.minimum(table[first + j], last)]
-            layer = jnp.maximum((where >> 5) - base, 0)
-            out[j] = returned[where & 31, layer]
-            return 0
-
-        lax.fori_loop(0, half, one, 0, unroll=4)
+            return returned[where & 31, jnp.maximum((where >> 5) - base, 0)]
+
+        batched(half, read, put(out))
 
 
 def take_kernel(part, mixed, low, high):
     half = low.shape[0]
-
-    def one(j, _):
-        low[j] = mixed[j, part]
-        high[j] = mixed[half + j, part]
-        return 0
-
-    lax.fori_loop(0, half, one, 0, unroll=4)
+    batched(half, lambda j: mixed[j, part], put(low))
+    batched(half, lambda j: mixed[half + j, part], put(high))
 
 
 def place_kernel(plan, last, table, *refs):
@@ -175,7 +164,7 @@
     new_right[0] = decay_rate * right[0] + weight * right_gram
 
 
-def local(grads, owner, factor_left, factor_right, precond_left, precond_right):
+def step(size_rest, grads, owner, factor_left, factor_right, precond_left, precond_right):
     rows = grads[0]
     blocks, band, width = rows.shape
     columns = lax.axis_size("fsdp")
@@ -209,7 +198,6 @@
         in_list = jnp.sum(same_list.astype(jnp.int32), axis=1)
         return listed(jnp.where(member, relative * size + in_list, -1), replicas * size)
 
-    size_rest = 56
     table_rest = packed(local_slot > 0, size_rest)
 
     def piece(*count):
@@ -247,6 +235,16 @@
     def tip(x):
         return x[0, :16, :128]
 
+    def gate(values, *marks):
+        shapes = tuple(jax.ShapeDtypeStruct(v.shape, v.dtype) for v in values)
+        return pl.pallas_call(
+            lambda *refs: None,
+            out_shape=shapes,
+            in_specs=[ANY] * (len(values) + len(marks)),
+            out_specs=(ANY,) * len(values),
+            input_output_aliases={i: i for i in range(len(values))},
+        )(*values, *marks)
+
     def both_ways(up, down):
         return lax.ppermute(up, "rep", up_pairs), lax.ppermute(down, "rep", down_pairs)
 
@@ -269,7 +267,7 @@
     def exchange(x):
         return lax.all_to_all(x, "fsdp", split_axis=0, concat_axis=0, tiled=True)
 
-    def applied(held, base, depth, order_after):
+    def applied(held, base, depth, order_after, moved=0):
         strip = pl.BlockSpec((columns, 1, band, width), lambda s: (0, s, 0, 0))
         matrix = pl.BlockSpec((1, order, order), lambda s: (s + base, 0, 0))
         return call(
@@ -279,11 +277,12 @@
             (strip, matrix, matrix),
             (strip,),
             after=order_after,
+            moved=moved,
             grid=(depth,),
-            limit=24,
+            limit=16,
         )
 
-    def placed(table, plan, sources, out, after=()):
+    def placed(table, plan, sources, out, after=(), limit=16):
         operands = (table, *sources) if out is None else (table, *sources, out)
         specs = [SMEM] + [VMEM] * len(sources) + ([] if out is None else [HBM])
 
@@ -300,26 +299,15 @@
             after,
             nbytes(2 * sum(p[1] for p in plan)),
             aliases=None if out is None else {1 + len(sources): 0},
+            limit=limit,
         )
 
     order = factor_left.shape[1]
     depth_rest = slots - 1
     half_first, half_rest = size_first // 2, size_rest // 2
-    low_first, high_first, mark = call(
-        functools.partial(first_kernel, size_first),
-        (piece(half_first), piece(half_first)),
-        (table_first, rows),
-        (SMEM, HBM),
-        (VMEM, VMEM),
-        [pltpu.SemaphoreType.DMA((2,))],
-        moved=nbytes(2 * size_first),
-        limit=60,
-    )
-    got_low_first, got_high_first = both_ways(low_first, high_first)
-
-    def lay(table, size, parts, marks):
+    def lay(table, size, parts, marks, zeros):
         def kernel(table, rows, *outs):
-            lay_kernel([(p[0] * size + p[1], out) for p, out in zip(parts, outs)], table, rows)
+            lay_kernel([(p[0] * size + p[1], out) for p, out in zip(parts, outs)], table, rows, zeros)
 
         return call(
             kernel,
@@ -331,18 +319,22 @@
             moved=nbytes(2 * sum(p[-1] for p in parts)),
         )
 
-    plain_up, plain_down, near_low, near_high, mine_first, mark = lay(
+    low_first, high_first, plain_up, plain_down, near_low, near_high, mine_first, mark = lay(
         table_first,
         size_first,
         [
+            (2, 0, half_first),
+            (2, half_first, half_first),
             (1, half_first, half_first),
             (3, 0, half_first),
             (1, 0, half_first),
             (3, half_first, half_first),
             (0, 0, size_first),
         ],
-        (mark,),
-    )
+        (),
+        True,
+    )
+    got_low_first, got_high_first = both_ways(low_first, high_first)
     up_high, down_low = both_ways(plain_up, plain_down)
     low, high, mark = call(
         second_kernel,
@@ -356,25 +348,21 @@
     low_rest, high_rest, up_rest, down_rest, mine_rest, mark = lay(
         table_rest,
         size_rest,
-        [
-            (2, 0, half_rest),
-            (2, half_rest, half_rest),
-            (1, 0, size_rest),
-            (3, 0, size_rest),
-            (0, 0, size_rest),
-        ],
+        [(2, 0, half_rest), (2, half_rest, half_rest), (1, 0, size_rest), (3, 0, size_rest), (0, 0, size_rest)],
         (mark,),
-    )
-    got_low_rest, got_high_rest = both_ways(low_rest, high_rest)
+        False,
+    )
     sent_first, mark = call(
-        functools.partial(third_first_kernel, size_first, last),
+        third_first_kernel,
         (piece(columns, 1),),
-        (table_first, mine_first, up_low, up_high, down_low, down_high),
-        (SMEM,) + (VMEM,) * 5,
+        (mine_first, up_low, up_high, down_low, down_high),
+        (VMEM,) * 5,
         (VMEM,),
         after=(mark,),
         moved=nbytes(4 * size_first),
     )
+    low_rest, high_rest = gate((low_rest, high_rest), mark)
+    got_low_rest, got_high_rest = both_ways(low_rest, high_rest)
     held_first = exchange(sent_first)
     up, down, mark = call(
         second_whole_kernel,
@@ -384,46 +372,48 @@
         (VMEM, VMEM),
         after=(mark,),
         moved=nbytes(3 * size_rest),
-        aliases={2: 0, 3: 1},
     )
     from_up, from_down = both_ways(up, down)
-    shaped_first, mark = applied(held_first, 0, 1, ())
-    sent_rest, mark = call(
-        functools.partial(third_kernel, size_rest, 1, last),
-        (piece(columns, slots),),
-        (table_rest, place, mine_rest, from_up, from_down, shaped_first),
-        (SMEM, SMEM, VMEM, VMEM, VMEM, VMEM),
-        (VMEM,),
-        moved=nbytes(5 * size_rest),
-    )
-    mixed = exchange(sent_rest)
+    shaped_first, mark = applied(held_first, 0, 1, (mark,))
+    back_first = exchange(shaped_first)
     own_low, own_high, mark = call(
-        functools.partial(take_kernel, slots - 1),
+        functools.partial(take_kernel, 0),
         (piece(half_first), piece(half_first)),
-        (mixed,),
+        (back_first,),
         (VMEM,),
         (VMEM, VMEM),
         moved=nbytes(2 * size_first),
     )
+    sent_rest, _ = call(
+        functools.partial(third_kernel, size_rest, 1, last),
+        (piece(columns, depth_rest),),
+        (table_rest, place, mine_rest, from_up, from_down),
+        (SMEM, SMEM, VMEM, VMEM, VMEM),
+        (VMEM,),
+        moved=nbytes(5 * size_rest),
+    )
+    [sent_rest] = gate((sent_rest,), mark)
+    held_rest = exchange(sent_rest)
     below_low, above_high = both_ways(own_low, own_high)
     below_high, above_low = both_ways(own_high, own_low)
     far_low, far_high = both_ways(below_low, above_high)
-    shaped_rest, mark = applied(mixed, 1, depth_rest, (mark,))
+    far_first = [far_low, far_high]
+    shaped_rest, mark = applied(held_rest, 1, depth_rest, (tip(below_low), tip(above_high)))
     back_rest = exchange(shaped_rest)
+    plan_first = half_plan(size_first)
     direction, mark_placed = placed(
         table_first,
-        half_plan(size_first),
-        [own_low, own_high, above_low, above_high, below_low, below_high, far_low, far_high],
+        plan_first[:6],
+        [own_low, own_high, above_low, above_high, below_low, below_high],
         None,
     )
-
     low, high, mark = call(
         functools.partial(pack_kernel, half_rest, 1, last),
         (piece(half_rest), piece(half_rest)),
         (table_rest, place, back_rest),
         (SMEM, SMEM, VMEM),
         (VMEM, VMEM),
-        after=(mark_placed,),
+        after=(mark_placed, tip(far_first[0]), tip(far_first[1])),
         moved=nbytes(2 * size_rest),
     )
     below_low, above_high = both_ways(low, high)
@@ -431,13 +421,13 @@
     far_low, far_high = both_ways(below_low, above_high)
 
     matrix = pl.BlockSpec((1, order, order), lambda s: (s, 0, 0))
-    new_left, new_right, mark_gram = call(
+    new_left, new_right, _ = call(
         gram_kernel,
         (
             jax.ShapeDtypeStruct(factor_left.shape, F32),
             jax.ShapeDtypeStruct(factor_right.shape, F32),
         ),
-        (held_first, mixed, factor_left, factor_right),
+        (held_first, held_rest, factor_left, factor_right),
         (
             pl.BlockSpec((columns, 1, band, width), lambda s: (0, 0, 0, 0)),
             pl.BlockSpec((columns, 1, band, width), lambda s: (0, jnp.maximum(s - 1, 0), 0, 0)),
@@ -449,15 +439,30 @@
         moved=slots * 18 * order * order,
         flops=slots * 4 * order**3,
         grid=(slots,),
-        limit=32,
-    )
-
+        limit=24,
+    )
+
+    direction, _ = placed(table_first, plan_first[6:], far_first, direction)
     plan = half_plan(size_rest)
     direction, _ = placed(
-        table_rest, plan[:6], [low, high, above_low, above_high, below_low, below_high], direction
-    )
-    direction, _ = placed(table_rest, plan[6:], [far_low, far_high], direction)
+        table_rest, plan[:6], [low, high, above_low, above_high, below_low, below_high], direction, (), 59
+    )
+    direction, _ = placed(table_rest, plan[6:], [far_low, far_high], direction, (), 59)
     return (new_left, new_right, direction)
+
+
+def local(grads, owner, *others):
+    columns = jnp.arange(lax.axis_size("fsdp"), dtype=jnp.int32)
+    counts = jnp.sum((owner[None, :] == columns[:, None]).astype(jnp.int32), axis=1)
+    longest = jnp.sum((counts > 4).astype(jnp.int32) + (counts > 8).astype(jnp.int32))
+    return lax.cond(
+        longest <= 48,
+        functools.partial(step, 48),
+        functools.partial(step, 56),
+        grads,
+        owner,
+        *others,
+    )
 
 
 def solution(mesh):

time: 167 us -> 159 us (0.952)
  blocking collectives: 47.7 us -> 15.2 us
  starting transfers between devices: 35 us -> 49.5 us
  Pallas kernels: 26.8 us -> 36.3 us
  local copies, waits for them, and re-layouts: 9.29 us -> 6.57 us
    all_to_all x2 -> x1, blocking collectives: 47.7 us -> 15.2 us  [exchange(): return lax.all_to_all(x, 'fsdp', split_axis=0, concat_axis=0, tiled=True)]
    all_to_all x1 -> x3, waiting for transfers between devices: 0.01 us -> 13.3 us  [exchange(): return lax.all_to_all(x, 'fsdp', split_axis=0, concat_axis=0, tiled=True)]
    ppermute x11, waiting for transfers between devices: 17.6 us -> 4.73 us  [both_ways(): lax.ppermute(down, 'rep', down_pairs)]
    all_to_all x1 -> x3, starting transfers between devices: 3.93 us -> 16 us  [exchange(): return lax.all_to_all(x, 'fsdp', split_axis=0, concat_axis=0, tiled=True)]
    pallas_call x15, Pallas kernels: 26.8 us -> 36.3 us  [call(): pl.pallas_call(body, out_shape=(*results, token), in_specs=list(specs) +...]
    unnamed x22 -> x0, local copies, waits for them, and re-layouts: 9.29 us -> none
    cond x0 -> x38, local copies, waits for them, and re-layouts: none -> 6.56 us
  transfers between devices with their start and end apart: 23 -> 25, of which waited for: 11 -> 13; matrix products, arithmetic and copies ran while one was open for 0% -> 0% of each run, Pallas kernels for 9% -> 14%
where the time goes in v3:
time: 159 us; the launch traced here: 158 us
  starting transfers between devices  49.5 us (31%)
  waiting for transfers between devices  44.2 us (28%)
  Pallas kernels  36.3 us (23%)
  blocking collectives  15.2 us (10%)
  local copies, waits for them, and re-layouts  6.57 us (4%)
  other arithmetic  4.53 us (3%)
    pallas_call x15, Pallas kernels, call(): pl.pallas_call(body, out_shape=(*results, token), in_specs=list(specs) +...  36.3 us
    ppermute x11, waiting for transfers between devices, both_ways(): lax.ppermute(up, 'rep', up_pairs)  26.1 us
    ppermute x11, starting transfers between devices, both_ways(): lax.ppermute(down, 'rep', down_pairs)  23.8 us
    all_to_all x3, starting transfers between devices, exchange(): return lax.all_to_all(x, 'fsdp', split_axis=0, concat_axis=0, tiled=True)  16 us
    all_to_all x1, blocking collectives, exchange(): return lax.all_to_all(x, 'fsdp', split_axis=0, concat_axis=0, tiled=True)  15.2 us
    all_to_all x3, waiting for transfers between devices, exchange(): return lax.all_to_all(x, 'fsdp', split_axis=0, concat_axis=0, tiled=True)  13.3 us
    ppermute x11, starting transfers between devices, both_ways(): lax.ppermute(up, 'rep', up_pairs)  9.68 us
    cond x38, local copies, waits for them, and re-layouts  6.56 us
  transfers between devices with their start and end apart: 25, of which 13 were waited for; matrix products, arithmetic and copies ran while one was open for 0% of the time, Pallas kernels for 14%

profile of v3, /device:TPU:0, one launch (start us, length us, event | category | flops | bytes accessed | tf_op | source)
XLA Modules:
  0.0 158.3 jit_solution(10498932442577041526)
XLA Ops:
  2.7 155.4 %conditional.1 = (f32[3,512,512]{2,1,0:T(8,128)}, f32[3,512,512]{2,1,0:T(8,128)}, bf16[256,16,512]{2,1,0:T(8,128)(2,1)}) conditional(s32[]{:T(128)} %convert_element_type.27, (s32[256]{0:T(256)}, bf16[1,256,16,512]{3,2,1,0:T(8,128)(2,1)}, bf16[3,512,512]{2,1,0:T(8,128)(2,1)}, bf16[3,512,512]{2,1,0:T(8,128)(2,1)}, f32[3,512,512]{2,1,0:T(8,128)}, ...), branch_computations={%region_2.7_spmd, %region_7.12_spmd} | conditional | flops 1611618688 | bytes 151366592 | solution.py:458
  5.7 3.3 %branch_1_fun.17 = (bf16[16,16,512]{2,1,0:T(8,128)(2,1)S(1)}, bf16[16,16,512]{2,1,0:T(8,128)(2,1)S(1)}, bf16[16,16,512]{2,1,0:T(8,128)(2,1)S(1)}, bf16[16,16,512...) custom-call(s32[128]{0:T(128)S(1)} %select_reduce_fusion.3.refs_0_, ...), custom_call_target="tpu_custom_call" | custom-call | bytes 4194304 | tf_op jit(solution)/shard_map/cond/branch_1_fun/pallas_call | solution.py:223
  12.7 2.8 %collective-permute-start.26 = (bf16[16,16,512]{2,1,0:T(8,128)(2,1)S(1)}, bf16[16,16,512]{2,1,0:T(8,128)(2,1)S(1)}, u32[]{:S(2)}, u32[]{:S(2)}) collective-permute-start(bf16[16,16,512]{2,1,0:T(8,128)(2,1)S(1)} %get-tuple-element.78), channel_id=1, source_target_pairs={{0,96},{32,0},{64,32},{96,64},{1,97},{33,1},{65,33},{97,65},{2,98}... | collective-permute-start | bytes 786440 | tf_op jit(solution)/shard_map/cond/branch_1_fun/ppermute | solution.py:258
  15.7 3.7 %collective-permute-done.22.refs_0_ = bf16[16,16,512]{2,1,0:T(8,128)(2,1)S(1)} collective-permute-done((bf16[16,16,512]{2,1,0:T(8,128)(2,1)S(1)}, bf16[16,16,512]{2,1,0:T(8,128)(2,1)S(1)}, u32[]{:S(2)}, u32[]{:S(2)}) %collective-permute-start.22) | collective-permute-done | bytes 262176 | tf_op jit(solution)/shard_map/cond/branch_1_fun/ppermute | solution.py:258
  21.7 1.7 %collective-permute-start.27 = (bf16[16,16,512]{2,1,0:T(8,128)(2,1)S(1)}, bf16[16,16,512]{2,1,0:T(8,128)(2,1)S(1)}, u32[]{:S(2)}, u32[]{:S(2)}) collective-permute-start(bf16[16,16,512]{2,1,0:T(8,128)(2,1)S(1)} %get-tuple-element.79), channel_id=1, source_target_pairs={{0,96},{32,0},{64,32},{96,64},{1,97},{33,1},{65,33},{97,65},{2,98}... | collective-permute-start | bytes 786440 | tf_op jit(solution)/shard_map/cond/branch_1_fun/ppermute | solution.py:258
  25.5 4.1 %collective-permute-done.24.refs_1_ = bf16[16,16,512]{2,1,0:T(8,128)(2,1)S(1)} collective-permute-done((bf16[16,16,512]{2,1,0:T(8,128)(2,1)S(1)}, bf16[16,16,512]{2,1,0:T(8,128)(2,1)S(1)}, u32[]{:S(2)}, u32[]{:S(2)}) %collective-permute-start.24) | collective-permute-done | bytes 262176 | tf_op jit(solution)/shard_map/cond/branch_1_fun/ppermute | solution.py:258
  32.9 1.7 %collective-permute-start.29 = (bf16[24,16,512]{2,1,0:T(8,128)(2,1)}, bf16[24,16,512]{2,1,0:T(8,128)(2,1)}, u32[]{:S(2)}, u32[]{:S(2)}) collective-permute-start(bf16[24,16,512]{2,1,0:T(8,128)(2,1)} %get-tuple-element.88), channel_id=1, source_target_pairs={{0,96},{32,0},{64,32},{96,64},{1,97},{33,1},{65,33},{97,65},{2,98}... | collective-permute-start | bytes 1179656 | tf_op jit(solution)/shard_map/cond/branch_1_fun/ppermute | solution.py:258
  34.5 8.2 %all-to-all-start.4 = ((bf16[32,1,16,512]{3,2,1,0:T(8,128)(2,1)}), bf16[32,1,16,512]{3,2,1,0:T(8,128)(2,1)S(1)}, u32[]{:S(2)}, u32[]{:S(2)}) async-start(bf16[32,1,16,512]{3,2,1,0:T(8,128)(2,1)} %get-tuple-element.82), calls=%async_computation.4 | async-start | bytes 1048576 | tf_op jit(solution)/shard_map/cond/branch_1_fun/all_to_all | solution.py:268
  43.5 2.4 %branch_1_fun.22 = (bf16[48,16,512]{2,1,0:T(8,128)(2,1)}, bf16[48,16,512]{2,1,0:T(8,128)(2,1)}, f32[8,128]{1,0:T(8,128)S(1)}) custom-call(bf16[24,16,512]{2,1,0:T(8,128)(2,1)S(1)} %collective-permute-done.28.refs_0_, bf16[24,16,512]{2,1,0:T(8,128)(2,1)} %collective-permute-done.29.refs_1_, bf16[48,16,512]{2,1,0:T(8,128)(2,1)S(1)} %get-tuple-element.89.refs_2_, ...), custom_call_target="tpu_custom_call" | custom-call | bytes 2359296 | tf_op jit(solution)/shard_map/cond/branch_1_fun/pallas_call | solution.py:223
  47.0 2.2 %collective-permute-start.31 = (bf16[48,16,512]{2,1,0:T(8,128)(2,1)}, bf16[48,16,512]{2,1,0:T(8,128)(2,1)S(1)}, u32[]{:S(2)}, u32[]{:S(2)}) collective-permute-start(bf16[48,16,512]{2,1,0:T(8,128)(2,1)} %get-tuple-element.92), channel_id=1, source_target_pairs={{0,96},{32,0},{64,32},{96,64},{1,97},{33,1},{65,33},{97,65},{2,98}... | collective-permute-start | bytes 2359304 | tf_op jit(solution)/shard_map/cond/branch_1_fun/ppermute | solution.py:258
  49.2 5.3 %all-to-all-done.4.refs_0_ = bf16[32,1,16,512]{3,2,1,0:T(8,128)(2,1)S(1)} async-done(((bf16[32,1,16,512]{3,2,1,0:T(8,128)(2,1)}), bf16[32,1,16,512]{3,2,1,0:T(8,128)(2,1)S(1)}, u32[]{:S(2)}, u32[]{:S(2)}) %all-to-all-start.4) | async-done | bytes 524320 | tf_op jit(solution)/shard_map/cond/branch_1_fun/all_to_all | solution.py:268
  54.5 2.6 %branch_1_fun.24 = (bf16[32,1,16,512]{3,2,1,0:T(8,128)(2,1)S(1)}, f32[8,128]{1,0:T(8,128)}) custom-call(bf16[32,1,16,512]{3,2,1,0:T(8,128)(2,1)S(1)} %all-to-all-done.4.refs_0_, bf16[3,512,512]{2,1,0:T(8,128)(2,1)} %get-tuple-element.94.refs_1_, bf16[3,512,512]{2,1,0:T(8,128)(2,1)} %get-tuple-element.95.refs_2_, f32[8,128]{1,0:T(8,128)S(1)} %get-tuple-element.96.refs_3_), custom_call_target="tpu_custom_call" | custom-call | tf_op jit(solution)/shard_map/cond/branch_1_fun/pallas_call | solution.py:223
  57.1 15.2 %all_to_all.33.refs_0_ = bf16[32,1,16,512]{3,2,1,0:T(8,128)(2,1)S(1)} all-to-all(bf16[32,1,16,512]{3,2,1,0:T(8,128)(2,1)S(1)} %get-tuple-element.97), channel_id=1, replica_groups=mesh['rep'=4,'fsdp'=32] {'fsdp'}, dimensions={0} | all-to-all | bytes 1048576 | tf_op jit(solution)/shard_map/cond/branch_1_fun/all_to_all | solution.py:268
  73.2 1.7 %branch_1_fun.23 = (bf16[32,2,16,512]{3,2,1,0:T(8,128)(2,1)S(1)}, f32[8,128]{1,0:T(8,128)}) custom-call(s32[192]{0:T(256)S(1)} %select_reduce_fusion.2.refs_0_, s32[256]{0:T(256)S(1)} %get-tuple-element.121.refs_1_, bf16[48,16,512]{2,1,0:T(8,128)(2,1)S(1)} %get-tuple-element.83.refs_2_, bf16[48,16,512]{2,1,0:T(8,128)(2,1)S(1)} %collective-permute-done.30.refs_3_, ...), custom_call_target="tpu_custom_call" | custom-call | bytes 3932160 | tf_op jit(solution)/shard_map/cond/branch_1_fun/pallas_call | solution.py:223
  75.9 3.9 %all-to-all-start.6 = ((bf16[32,2,16,512]{3,2,1,0:T(8,128)(2,1)}), bf16[32,2,16,512]{3,2,1,0:T(8,128)(2,1)S(1)}, u32[]{:S(2)}, u32[]{:S(2)}) async-start(bf16[32,2,16,512]{3,2,1,0:T(8,128)(2,1)} %branch_1_fun.26), calls=%async_computation.6 | async-start | bytes 2097152 | tf_op jit(solution)/shard_map/cond/branch_1_fun/all_to_all | solution.py:268
  80.2 2.9 %collective-permute-start.33 = (bf16[16,16,512]{2,1,0:T(8,128)(2,1)}, bf16[16,16,512]{2,1,0:T(8,128)(2,1)S(1)}, u32[]{:S(2)}, u32[]{:S(2)}) collective-permute-start(bf16[16,16,512]{2,1,0:T(8,128)(2,1)} %get-tuple-element.102.refs_2_), channel_id=1, source_target_pairs={{0,96},{32,0},{64,32},{96,64},{1,97},{33,1},{65,33},{97,65},{2,98}... | collective-permute-start | bytes 786440 | tf_op jit(solution)/shard_map/cond/branch_1_fun/ppermute | solution.py:258
  83.1 6.6 %collective-permute-done.32.refs_5_ = bf16[16,16,512]{2,1,0:T(8,128)(2,1)S(1)} collective-permute-done((bf16[16,16,512]{2,1,0:T(8,128)(2,1)}, bf16[16,16,512]{2,1,0:T(8,128)(2,1)S(1)}, u32[]{:S(2)}, u32[]{:S(2)}) %collective-permute-start.32) | collective-permute-done | bytes 262176 | tf_op jit(solution)/shard_map/cond/branch_1_fun/ppermute | solution.py:258
  89.7 7.5 %all-to-all-done.6.refs_0_.refs_1_ = bf16[32,2,16,512]{3,2,1,0:T(8,128)(2,1)S(1)} async-done(((bf16[32,2,16,512]{3,2,1,0:T(8,128)(2,1)}), bf16[32,2,16,512]{3,2,1,0:T(8,128)(2,1)S(1)}, u32[]{:S(2)}, u32[]{:S(2)}) %all-to-all-start.6) | async-done | bytes 1048608 | tf_op jit(solution)/shard_map/cond/branch_1_fun/all_to_all | solution.py:268
  97.1 4.3 %branch_1_fun.27 = (bf16[32,2,16,512]{3,2,1,0:T(8,128)(2,1)S(1)}, f32[8,128]{1,0:T(8,128)}) custom-call(bf16[32,2,16,512]{3,2,1,0:T(8,128)(2,1)S(1)} %all-to-all-done.6.refs_0_.refs_1_, bf16[3,512,512]{2,1,0:T(8,128)(2,1)} %get-tuple-element.94.refs_1_, bf16[3,512,512]{2,1,0:T(8,128)(2,1)} %get-tuple-element.95.refs_2_, ...), custom_call_target="tpu_custom_call" | custom-call | tf_op jit(solution)/shard_map/cond/branch_1_fun/pallas_call | solution.py:223
  102.4 3.9 %all-to-all-start.7 = ((bf16[32,2,16,512]{3,2,1,0:T(8,128)(2,1)}), bf16[32,2,16,512]{3,2,1,0:T(8,128)(2,1)S(1)}, u32[]{:S(2)}, u32[]{:S(2)}) async-start(bf16[32,2,16,512]{3,2,1,0:T(8,128)(2,1)} %copy-done.3), calls=%async_computation.7 | async-start | bytes 2097152 | tf_op jit(solution)/shard_map/cond/branch_1_fun/all_to_all | solution.py:268
  108.7 2.9 %collective-permute-start.37 = (bf16[16,16,512]{2,1,0:T(8,128)(2,1)}, bf16[16,16,512]{2,1,0:T(8,128)(2,1)S(1)}, u32[]{:S(2)}, u32[]{:S(2)}) collective-permute-start(bf16[16,16,512]{2,1,0:T(8,128)(2,1)} %copy-done.15), channel_id=1, source_target_pairs={{0,96},{32,0},{64,32},{96,64},{1,97},{33,1},{65,33},{97,65},{2,98}... | collective-permute-start | bytes 786440 | tf_op jit(solution)/shard_map/cond/branch_1_fun/ppermute | solution.py:258
  111.6 4.1 %collective-permute-done.34.refs_3_ = bf16[16,16,512]{2,1,0:T(8,128)(2,1)S(1)} collective-permute-done((bf16[16,16,512]{2,1,0:T(8,128)(2,1)}, bf16[16,16,512]{2,1,0:T(8,128)(2,1)S(1)}, u32[]{:S(2)}, u32[]{:S(2)}) %collective-permute-start.34) | collective-permute-done | bytes 262176 | tf_op jit(solution)/shard_map/cond/branch_1_fun/ppermute | solution.py:258
  115.7 2.8 %collective-permute-done.35.refs_6_ = bf16[16,16,512]{2,1,0:T(8,128)(2,1)S(1)} collective-permute-done((bf16[16,16,512]{2,1,0:T(8,128)(2,1)}, bf16[16,16,512]{2,1,0:T(8,128)(2,1)S(1)}, u32[]{:S(2)}, u32[]{:S(2)}) %collective-permute-start.35) | collective-permute-done | bytes 262176 | tf_op jit(solution)/shard_map/cond/branch_1_fun/ppermute | solution.py:258
  119.5 2.7 %branch_1_fun.28 = (bf16[256,16,512]{2,1,0:T(8,128)(2,1)}, f32[8,128]{1,0:T(8,128)S(1)}) custom-call(s32[128]{0:T(128)S(1)} %select_reduce_fusion.3.refs_0_, bf16[16,16,512]{2,1,0:T(8,128)(2,1)} %get-tuple-element.101.refs_1_, bf16[16,16,512]{2,1,0:T(8,128)(2,1)} %get-tuple-element.102.refs_2_, bf16[16,16,512]{2,1,0:T(8,128)(2,1)S(1)} %collective-permute-done.34.refs_3_, ...), custom_call_target="tpu_custom_call" | custom-call | bytes 3145728 | tf_op jit(solution)/shard_map/cond/branch_1_fun/pallas_call | solution.py:223
  124.9 2.9 %collective-permute-start.40 = (bf16[24,16,512]{2,1,0:T(8,128)(2,1)S(1)}, bf16[24,16,512]{2,1,0:T(8,128)(2,1)S(1)}, u32[]{:S(2)}, u32[]{:S(2)}) collective-permute-start(bf16[24,16,512]{2,1,0:T(8,128)(2,1)S(1)} %get-tuple-element.109.refs_2_), channel_id=1, source_target_pairs={{0,96},{32,0},{64,32},{96,64},{1,97},{33,1},{65,33},{97,65},{2,98}... | collective-permute-start | bytes 1179656 | tf_op jit(solution)/shard_map/cond/branch_1_fun/ppermute | solution.py:258
  128.1 1.7 %collective-permute-start.43 = (bf16[24,16,512]{2,1,0:T(8,128)(2,1)S(1)}, bf16[24,16,512]{2,1,0:T(8,128)(2,1)S(1)}, u32[]{:S(2)}, u32[]{:S(2)}) collective-permute-start(bf16[24,16,512]{2,1,0:T(8,128)(2,1)S(1)} %get-tuple-element.109.refs_2_), channel_id=1, source_target_pairs={{0,32},{32,64},{64,96},{96,0},{1,33},{33,65},{65,97},{97,1},{2,34}... | collective-permute-start | bytes 1179656 | tf_op jit(solution)/shard_map/cond/branch_1_fun/ppermute | solution.py:258
  129.8 7.9 %collective-permute-done.38.refs_5_ = bf16[24,16,512]{2,1,0:T(8,128)(2,1)S(1)} collective-permute-done((bf16[24,16,512]{2,1,0:T(8,128)(2,1)S(1)}, bf16[24,16,512]{2,1,0:T(8,128)(2,1)S(1)}, u32[]{:S(2)}, u32[]{:S(2)}) %collective-permute-start.38) | collective-permute-done | bytes 393248 | tf_op jit(solution)/shard_map/cond/branch_1_fun/ppermute | solution.py:258
  137.8 3.3 %collective-permute-start.41 = (bf16[24,16,512]{2,1,0:T(8,128)(2,1)S(1)}, bf16[24,16,512]{2,1,0:T(8,128)(2,1)}, u32[]{:S(2)}, u32[]{:S(2)}) collective-permute-start(bf16[24,16,512]{2,1,0:T(8,128)(2,1)S(1)} %collective-permute-done.40.refs_4_), channel_id=1, source_target_pairs={{0,96},{32,0},{64,32},{96,64},{1,97},{33,1},{65,33},{97,65},{2,98}... | collective-permute-start | bytes 1179656 | tf_op jit(solution)/shard_map/cond/branch_1_fun/ppermute | solution.py:258
  141.0 2.0 %branch_1_fun.31 = (bf16[256,16,512]{2,1,0:T(8,128)(2,1)}, f32[8,128]{1,0:T(8,128)}) custom-call(s32[128]{0:T(128)S(1)} %select_reduce_fusion.3.refs_0_, bf16[16,16,512]{2,1,0:T(8,128)(2,1)S(1)} %collective-permute-done.36.refs_1_, bf16[16,16,512]{2,1,0:T(8,128)(2,1)S(1)} %collective-permute-done.37.refs_2_, ...), custom_call_target="tpu_custom_call", output_to_operand_aliasing={{0}: (3, {})} | custom-call | bytes 1048576 | tf_op jit(solution)/shard_map/cond/branch_1_fun/pallas_call | solution.py:223
  143.0 6.0 %branch_1_fun.30 = (f32[3,512,512]{2,1,0:T(8,128)}, f32[3,512,512]{2,1,0:T(8,128)}, f32[8,128]{1,0:T(8,128)}) custom-call(bf16[32,1,16,512]{3,2,1,0:T(8,128)(2,1)S(1)} %all-to-all-done.4.refs_0_, bf16[32,2,16,512]{3,2,1,0:T(8,128)(2,1)S(1)} %all-to-all-done.6.refs_0_.refs_1_, f32[3,512,512]{2,1,0:T(8,128)S(1)} %copy-done.28, ...), custom_call_target="tpu_custom_call" | custom-call | flops 1610612736 | bytes 14155776 | tf_op jit(solution)/shard_map/cond/branch_1_fun/pallas_call | solution.py:223
  149.9 4.7 %branch_1_fun.32 = (bf16[256,16,512]{2,1,0:T(8,128)(2,1)}, f32[8,128]{1,0:T(8,128)}) custom-call(s32[192]{0:T(256)} %copy-done.18, bf16[24,16,512]{2,1,0:T(8,128)(2,1)} %copy-done.11, bf16[24,16,512]{2,1,0:T(8,128)(2,1)} %copy-done.12, bf16[24,16,512]{2,1,0:T(8,128)(2,1)} %copy-done.36, ...), custom_call_target="tpu_custom_call", output_to_operand_aliasing={{0}: (7, {})} | custom-call | bytes 4718592 | tf_op jit(solution)/shard_map/cond/branch_1_fun/pallas_call | solution.py:223
  155.4 2.7 %branch_1_fun.33 = (bf16[256,16,512]{2,1,0:T(8,128)(2,1)}, f32[8,128]{1,0:T(8,128)}) custom-call(s32[192]{0:T(256)} %copy-done.18, bf16[24,16,512]{2,1,0:T(8,128)(2,1)} %copy-done.35, bf16[24,16,512]{2,1,0:T(8,128)(2,1)} %collective-permute-done.41.refs_2_, bf16[256,16,512]{2,1,0:T(8,128)(2,1)} %get-tuple-element.112.refs_3_), custom_call_target="tpu_custom_call", output_to_operand_aliasing={{0}: (3, {})} | custom-call | bytes 1572864 | tf_op jit(solution)/shard_map/cond/branch_1_fun/pallas_call | solution.py:223
  (89 shorter events, 28.8 us)
Async XLA Ops:
  2.9 20.6 %copy-start.26 = (bf16[1,256,16,512]{3,2,1,0:T(8,128)(2,1)S(1)}, bf16[1,256,16,512]{3,2,1,0:T(8,128)(2,1)}, u32[]{:S(2)}) copy-start(bf16[1,256,16,512]{3,2,1,0:T(8,128)(2,1)} %get-tuple-element.70) | copy-start | bytes 12582916 | tf_op jit(solution)/shard_map/cond
  9.0 10.4 %collective-permute-start.22 = (bf16[16,16,512]{2,1,0:T(8,128)(2,1)S(1)}, bf16[16,16,512]{2,1,0:T(8,128)(2,1)S(1)}, u32[]{:S(2)}, u32[]{:S(2)}) collective-permute-start(bf16[16,16,512]{2,1,0:T(8,128)(2,1)S(1)} %get-tuple-element.72), channel_id=1, source_target_pairs={{0,32},{32,64},{64,96},{96,0},{1,33},{33,65},{65,97},{97,1},{2,34}... | collective-permute-start | bytes 786440 | tf_op jit(solution)/shard_map/cond/branch_1_fun/ppermute | solution.py:258
  10.7 9.2 %collective-permute-start.23 = (bf16[16,16,512]{2,1,0:T(8,128)(2,1)S(1)}, bf16[16,16,512]{2,1,0:T(8,128)(2,1)S(1)}, u32[]{:S(2)}, u32[]{:S(2)}) collective-permute-start(bf16[16,16,512]{2,1,0:T(8,128)(2,1)S(1)} %get-tuple-element.73), channel_id=1, source_target_pairs={{0,96},{32,0},{64,32},{96,64},{1,97},{33,1},{65,33},{97,65},{2,98}... | collective-permute-start | bytes 786440 | tf_op jit(solution)/shard_map/cond/branch_1_fun/ppermute | solution.py:258
  12.3 13.2 %collective-permute-start.25 = (bf16[16,16,512]{2,1,0:T(8,128)(2,1)S(1)}, bf16[16,16,512]{2,1,0:T(8,128)(2,1)S(1)}, u32[]{:S(2)}, u32[]{:S(2)}) collective-permute-start(bf16[16,16,512]{2,1,0:T(8,128)(2,1)S(1)} %get-tuple-element.77), channel_id=1, source_target_pairs={{0,32},{32,64},{64,96},{96,0},{1,33},{33,65},{65,97},{97,1},{2,34}... | collective-permute-start | bytes 786440 | tf_op jit(solution)/shard_map/cond/branch_1_fun/ppermute | solution.py:258
  12.7 12.8 %collective-permute-start.26 = (bf16[16,16,512]{2,1,0:T(8,128)(2,1)S(1)}, bf16[16,16,512]{2,1,0:T(8,128)(2,1)S(1)}, u32[]{:S(2)}, u32[]{:S(2)}) collective-permute-start(bf16[16,16,512]{2,1,0:T(8,128)(2,1)S(1)} %get-tuple-element.78), channel_id=1, source_target_pairs={{0,96},{32,0},{64,32},{96,64},{1,97},{33,1},{65,33},{97,65},{2,98}... | collective-permute-start | bytes 786440 | tf_op jit(solution)/shard_map/cond/branch_1_fun/ppermute | solution.py:258
  20.1 9.6 %collective-permute-start.24 = (bf16[16,16,512]{2,1,0:T(8,128)(2,1)S(1)}, bf16[16,16,512]{2,1,0:T(8,128)(2,1)S(1)}, u32[]{:S(2)}, u32[]{:S(2)}) collective-permute-start(bf16[16,16,512]{2,1,0:T(8,128)(2,1)S(1)} %get-tuple-element.76), channel_id=1, source_target_pairs={{0,32},{32,64},{64,96},{96,0},{1,33},{33,65},{65,97},{97,1},{2,34}... | collective-permute-start | bytes 786440 | tf_op jit(solution)/shard_map/cond/branch_1_fun/ppermute | solution.py:258
  21.7 8.0 %collective-permute-start.27 = (bf16[16,16,512]{2,1,0:T(8,128)(2,1)S(1)}, bf16[16,16,512]{2,1,0:T(8,128)(2,1)S(1)}, u32[]{:S(2)}, u32[]{:S(2)}) collective-permute-start(bf16[16,16,512]{2,1,0:T(8,128)(2,1)S(1)} %get-tuple-element.79), channel_id=1, source_target_pairs={{0,96},{32,0},{64,32},{96,64},{1,97},{33,1},{65,33},{97,65},{2,98}... | collective-permute-start | bytes 786440 | tf_op jit(solution)/shard_map/cond/branch_1_fun/ppermute | solution.py:258
  23.5 100.1 %copy-start.18 = (s32[192]{0:T(256)}, s32[192]{0:T(256)S(1)}, u32[]{:S(2)}) copy-start(s32[192]{0:T(256)S(1)} %select_reduce_fusion.2.refs_0_) | copy-start | bytes 2308 | tf_op jit(solution)/shard_map/cond
  31.3 11.5 %collective-permute-start.28 = (bf16[24,16,512]{2,1,0:T(8,128)(2,1)}, bf16[24,16,512]{2,1,0:T(8,128)(2,1)S(1)}, u32[]{:S(2)}, u32[]{:S(2)}) collective-permute-start(bf16[24,16,512]{2,1,0:T(8,128)(2,1)} %get-tuple-element.87), channel_id=1, source_target_pairs={{0,32},{32,64},{64,96},{96,0},{1,33},{33,65},{65,97},{97,1},{2,34}... | collective-permute-start | bytes 1179656 | tf_op jit(solution)/shard_map/cond/branch_1_fun/ppermute | solution.py:258
  32.9 10.0 %collective-permute-start.29 = (bf16[24,16,512]{2,1,0:T(8,128)(2,1)}, bf16[24,16,512]{2,1,0:T(8,128)(2,1)}, u32[]{:S(2)}, u32[]{:S(2)}) collective-permute-start(bf16[24,16,512]{2,1,0:T(8,128)(2,1)} %get-tuple-element.88), channel_id=1, source_target_pairs={{0,96},{32,0},{64,32},{96,64},{1,97},{33,1},{65,33},{97,65},{2,98}... | collective-permute-start | bytes 1179656 | tf_op jit(solution)/shard_map/cond/branch_1_fun/ppermute | solution.py:258
  34.5 19.9 %all-to-all-start.4 = ((bf16[32,1,16,512]{3,2,1,0:T(8,128)(2,1)}), bf16[32,1,16,512]{3,2,1,0:T(8,128)(2,1)S(1)}, u32[]{:S(2)}, u32[]{:S(2)}) async-start(bf16[32,1,16,512]{3,2,1,0:T(8,128)(2,1)} %get-tuple-element.82), calls=%async_computation.4 | async-start | bytes 1048576 | tf_op jit(solution)/shard_map/cond/branch_1_fun/all_to_all | solution.py:268
  46.0 27.2 %collective-permute-start.30 = (bf16[48,16,512]{2,1,0:T(8,128)(2,1)}, bf16[48,16,512]{2,1,0:T(8,128)(2,1)S(1)}, u32[]{:S(2)}, u32[]{:S(2)}) collective-permute-start(bf16[48,16,512]{2,1,0:T(8,128)(2,1)} %get-tuple-element.91), channel_id=1, source_target_pairs={{0,32},{32,64},{64,96},{96,0},{1,33},{33,65},{65,97},{97,1},{2,34}... | collective-permute-start | bytes 2359304 | tf_op jit(solution)/shard_map/cond/branch_1_fun/ppermute | solution.py:258
  47.0 26.2 %collective-permute-start.31 = (bf16[48,16,512]{2,1,0:T(8,128)(2,1)}, bf16[48,16,512]{2,1,0:T(8,128)(2,1)S(1)}, u32[]{:S(2)}, u32[]{:S(2)}) collective-permute-start(bf16[48,16,512]{2,1,0:T(8,128)(2,1)} %get-tuple-element.92), channel_id=1, source_target_pairs={{0,96},{32,0},{64,32},{96,64},{1,97},{33,1},{65,33},{97,65},{2,98}... | collective-permute-start | bytes 2359304 | tf_op jit(solution)/shard_map/cond/branch_1_fun/ppermute | solution.py:258
  75.9 21.3 %all-to-all-start.6 = ((bf16[32,2,16,512]{3,2,1,0:T(8,128)(2,1)}), bf16[32,2,16,512]{3,2,1,0:T(8,128)(2,1)S(1)}, u32[]{:S(2)}, u32[]{:S(2)}) async-start(bf16[32,2,16,512]{3,2,1,0:T(8,128)(2,1)} %branch_1_fun.26), calls=%async_computation.6 | async-start | bytes 2097152 | tf_op jit(solution)/shard_map/cond/branch_1_fun/all_to_all | solution.py:268
  79.8 9.9 %collective-permute-start.32 = (bf16[16,16,512]{2,1,0:T(8,128)(2,1)}, bf16[16,16,512]{2,1,0:T(8,128)(2,1)S(1)}, u32[]{:S(2)}, u32[]{:S(2)}) collective-permute-start(bf16[16,16,512]{2,1,0:T(8,128)(2,1)} %get-tuple-element.101.refs_1_), channel_id=1, source_target_pairs={{0,32},{32,64},{64,96},{96,0},{1,33},{33,65},{65,97},{97,1},{2,34}... | collective-permute-start | bytes 786440 | tf_op jit(solution)/shard_map/cond/branch_1_fun/ppermute | solution.py:258
  80.2 9.5 %collective-permute-start.33 = (bf16[16,16,512]{2,1,0:T(8,128)(2,1)}, bf16[16,16,512]{2,1,0:T(8,128)(2,1)S(1)}, u32[]{:S(2)}, u32[]{:S(2)}) collective-permute-start(bf16[16,16,512]{2,1,0:T(8,128)(2,1)} %get-tuple-element.102.refs_2_), channel_id=1, source_target_pairs={{0,96},{32,0},{64,32},{96,64},{1,97},{33,1},{65,33},{97,65},{2,98}... | collective-permute-start | bytes 786440 | tf_op jit(solution)/shard_map/cond/branch_1_fun/ppermute | solution.py:258
  89.7 12.7 %copy-start.15 = (bf16[16,16,512]{2,1,0:T(8,128)(2,1)}, bf16[16,16,512]{2,1,0:T(8,128)(2,1)S(1)}, u32[]{:S(2)}) copy-start(bf16[16,16,512]{2,1,0:T(8,128)(2,1)S(1)} %collective-permute-done.33.refs_4_) | copy-start | bytes 786436 | tf_op jit(solution)/shard_map/cond
  102.4 21.3 %all-to-all-start.7 = ((bf16[32,2,16,512]{3,2,1,0:T(8,128)(2,1)}), bf16[32,2,16,512]{3,2,1,0:T(8,128)(2,1)S(1)}, u32[]{:S(2)}, u32[]{:S(2)}) async-start(bf16[32,2,16,512]{3,2,1,0:T(8,128)(2,1)} %copy-done.3), calls=%async_computation.7 | async-start | bytes 2097152 | tf_op jit(solution)/shard_map/cond/branch_1_fun/all_to_all | solution.py:268
  106.3 9.4 %collective-permute-start.34 = (bf16[16,16,512]{2,1,0:T(8,128)(2,1)}, bf16[16,16,512]{2,1,0:T(8,128)(2,1)S(1)}, u32[]{:S(2)}, u32[]{:S(2)}) collective-permute-start(bf16[16,16,512]{2,1,0:T(8,128)(2,1)} %get-tuple-element.101.refs_1_), channel_id=1, source_target_pairs={{0,96},{32,0},{64,32},{96,64},{1,97},{33,1},{65,33},{97,65},{2,98}... | collective-permute-start | bytes 786440 | tf_op jit(solution)/shard_map/cond/branch_1_fun/ppermute | solution.py:258
  107.9 10.6 %collective-permute-start.35 = (bf16[16,16,512]{2,1,0:T(8,128)(2,1)}, bf16[16,16,512]{2,1,0:T(8,128)(2,1)S(1)}, u32[]{:S(2)}, u32[]{:S(2)}) collective-permute-start(bf16[16,16,512]{2,1,0:T(8,128)(2,1)} %get-tuple-element.102.refs_2_), channel_id=1, source_target_pairs={{0,32},{32,64},{64,96},{96,0},{1,33},{33,65},{65,97},{97,1},{2,34}... | collective-permute-start | bytes 786440 | tf_op jit(solution)/shard_map/cond/branch_1_fun/ppermute | solution.py:258
  108.4 14.6 %collective-permute-start.36 = (bf16[16,16,512]{2,1,0:T(8,128)(2,1)S(1)}, bf16[16,16,512]{2,1,0:T(8,128)(2,1)S(1)}, u32[]{:S(2)}, u32[]{:S(2)}) collective-permute-start(bf16[16,16,512]{2,1,0:T(8,128)(2,1)S(1)} %collective-permute-done.32.refs_5_), channel_id=1, source_target_pairs={{0,32},{32,64},{64,96},{96,0},{1,33},{33,65},{65,97},{97,1},{2,34}... | collective-permute-start | bytes 786440 | tf_op jit(solution)/shard_map/cond/branch_1_fun/ppermute | solution.py:258
  108.7 14.3 %collective-permute-start.37 = (bf16[16,16,512]{2,1,0:T(8,128)(2,1)}, bf16[16,16,512]{2,1,0:T(8,128)(2,1)S(1)}, u32[]{:S(2)}, u32[]{:S(2)}) collective-permute-start(bf16[16,16,512]{2,1,0:T(8,128)(2,1)} %copy-done.15), channel_id=1, source_target_pairs={{0,96},{32,0},{64,32},{96,64},{1,97},{33,1},{65,33},{97,65},{2,98}... | collective-permute-start | bytes 786440 | tf_op jit(solution)/shard_map/cond/branch_1_fun/ppermute | solution.py:258
  123.6 19.4 %copy-start.28 = (f32[3,512,512]{2,1,0:T(8,128)S(1)}, f32[3,512,512]{2,1,0:T(8,128)}, u32[]{:S(2)}) copy-start(f32[3,512,512]{2,1,0:T(8,128)} %get-tuple-element.99.refs_2_) | copy-start | bytes 9437188 | tf_op jit(solution)/shard_map/cond
  124.5 24.5 %copy-start.11 = (bf16[24,16,512]{2,1,0:T(8,128)(2,1)}, bf16[24,16,512]{2,1,0:T(8,128)(2,1)S(1)}, u32[]{:S(2)}) copy-start(bf16[24,16,512]{2,1,0:T(8,128)(2,1)S(1)} %get-tuple-element.108.refs_1_) | copy-start | bytes 1179652 | tf_op jit(solution)/shard_map/cond
  124.5 24.5 %copy-start.12 = (bf16[24,16,512]{2,1,0:T(8,128)(2,1)}, bf16[24,16,512]{2,1,0:T(8,128)(2,1)S(1)}, u32[]{:S(2)}) copy-start(bf16[24,16,512]{2,1,0:T(8,128)(2,1)S(1)} %get-tuple-element.109.refs_2_) | copy-start | bytes 1179652 | tf_op jit(solution)/shard_map/cond
  124.5 13.2 %collective-permute-start.38 = (bf16[24,16,512]{2,1,0:T(8,128)(2,1)S(1)}, bf16[24,16,512]{2,1,0:T(8,128)(2,1)S(1)}, u32[]{:S(2)}, u32[]{:S(2)}) collective-permute-start(bf16[24,16,512]{2,1,0:T(8,128)(2,1)S(1)} %get-tuple-element.108.refs_1_), channel_id=1, source_target_pairs={{0,32},{32,64},{64,96},{96,0},{1,33},{33,65},{65,97},{97,1},{2,34}... | collective-permute-start | bytes 1179656 | tf_op jit(solution)/shard_map/cond/branch_1_fun/ppermute | solution.py:258
  124.9 12.8 %collective-permute-start.40 = (bf16[24,16,512]{2,1,0:T(8,128)(2,1)S(1)}, bf16[24,16,512]{2,1,0:T(8,128)(2,1)S(1)}, u32[]{:S(2)}, u32[]{:S(2)}) collective-permute-start(bf16[24,16,512]{2,1,0:T(8,128)(2,1)S(1)} %get-tuple-element.109.refs_2_), channel_id=1, source_target_pairs={{0,96},{32,0},{64,32},{96,64},{1,97},{33,1},{65,33},{97,65},{2,98}... | collective-permute-start | bytes 1179656 | tf_op jit(solution)/shard_map/cond/branch_1_fun/ppermute | solution.py:258
  127.8 21.2 %collective-permute-start.42 = (bf16[24,16,512]{2,1,0:T(8,128)(2,1)S(1)}, bf16[24,16,512]{2,1,0:T(8,128)(2,1)S(1)}, u32[]{:S(2)}, u32[]{:S(2)}) collective-permute-start(bf16[24,16,512]{2,1,0:T(8,128)(2,1)S(1)} %get-tuple-element.108.refs_1_), channel_id=1, source_target_pairs={{0,96},{32,0},{64,32},{96,64},{1,97},{33,1},{65,33},{97,65},{2,98}... | collective-permute-start | bytes 1179656 | tf_op jit(solution)/shard_map/cond/branch_1_fun/ppermute | solution.py:258
  128.1 20.9 %collective-permute-start.43 = (bf16[24,16,512]{2,1,0:T(8,128)(2,1)S(1)}, bf16[24,16,512]{2,1,0:T(8,128)(2,1)S(1)}, u32[]{:S(2)}, u32[]{:S(2)}) collective-permute-start(bf16[24,16,512]{2,1,0:T(8,128)(2,1)S(1)} %get-tuple-element.109.refs_2_), channel_id=1, source_target_pairs={{0,32},{32,64},{64,96},{96,0},{1,33},{33,65},{65,97},{97,1},{2,34}... | collective-permute-start | bytes 1179656 | tf_op jit(solution)/shard_map/cond/branch_1_fun/ppermute | solution.py:258
  137.7 11.3 %copy-start.33 = (bf16[24,16,512]{2,1,0:T(8,128)(2,1)}, bf16[24,16,512]{2,1,0:T(8,128)(2,1)S(1)}, u32[]{:S(2)}) copy-start(bf16[24,16,512]{2,1,0:T(8,128)(2,1)S(1)} %collective-permute-done.38.refs_5_) | copy-start | bytes 1179652 | tf_op jit(solution)/shard_map/cond
  137.7 16.8 %collective-permute-start.39 = (bf16[24,16,512]{2,1,0:T(8,128)(2,1)S(1)}, bf16[24,16,512]{2,1,0:T(8,128)(2,1)S(1)}, u32[]{:S(2)}, u32[]{:S(2)}) collective-permute-start(bf16[24,16,512]{2,1,0:T(8,128)(2,1)S(1)} %collective-permute-done.38.refs_5_), channel_id=1, source_target_pairs={{0,32},{32,64},{64,96},{96,0},{1,33},{33,65},{65,97},{97,1},{2,34}... | collective-permute-start | bytes 1179656 | tf_op jit(solution)/shard_map/cond/branch_1_fun/ppermute | solution.py:258
  137.8 16.8 %collective-permute-start.41 = (bf16[24,16,512]{2,1,0:T(8,128)(2,1)S(1)}, bf16[24,16,512]{2,1,0:T(8,128)(2,1)}, u32[]{:S(2)}, u32[]{:S(2)}) collective-permute-start(bf16[24,16,512]{2,1,0:T(8,128)(2,1)S(1)} %collective-permute-done.40.refs_4_), channel_id=1, source_target_pairs={{0,96},{32,0},{64,32},{96,64},{1,97},{33,1},{65,33},{97,65},{2,98}... | collective-permute-start | bytes 1179656 | tf_op jit(solution)/shard_map/cond/branch_1_fun/ppermute | solution.py:258
  (12 other events, 26.6 us)

commit v4 on v3

--- a/solution.py
+++ b/solution.py
@@ -418,10 +418,8 @@
     )
     below_low, above_high = both_ways(low, high)
     below_high, above_low = both_ways(high, low)
-    far_low, far_high = both_ways(below_low, above_high)
-
     matrix = pl.BlockSpec((1, order, order), lambda s: (s, 0, 0))
-    new_left, new_right, _ = call(
+    new_left, new_right, mark = call(
         gram_kernel,
         (
             jax.ShapeDtypeStruct(factor_left.shape, F32),
@@ -442,6 +440,9 @@
         limit=24,
     )
 
+    below_low, above_high = gate((below_low, above_high), mark)
+    far_low, far_high = both_ways(below_low, above_high)
+
     direction, _ = placed(table_first, plan_first[6:], far_first, direction)
     plan = half_plan(size_rest)
     direction, _ = placed(

time: 159 us -> 158 us (level)
  waiting for transfers between devices: 44.2 us -> 40.9 us
  local copies, waits for them, and re-layouts: 6.57 us -> 8.72 us
    ppermute x11, waiting for transfers between devices: 26.1 us -> 21.6 us  [both_ways(): lax.ppermute(up, 'rep', up_pairs)]
    cond x38 -> x44, local copies, waits for them, and re-layouts: 6.56 us -> 8.71 us
    ppermute x11, waiting for transfers between devices: 4.73 us -> 6.34 us  [both_ways(): lax.ppermute(down, 'rep', down_pairs)]
  transfers between devices with their start and end apart: 25 -> 25, of which waited for: 13 -> 15; matrix products, arithmetic and copies ran while one was open for 0% -> 0% of each run, Pallas kernels for 14% -> 14%
where the time goes in v4:
time: 158 us; the launch traced here: 157 us
  starting transfers between devices  49.5 us (31%)
  waiting for transfers between devices  40.9 us (26%)
  Pallas kernels  36.1 us (23%)
  blocking collectives  15.2 us (10%)
  local copies, waits for them, and re-layouts  8.72 us (6%)
  other arithmetic  4.53 us (3%)
    pallas_call x15, Pallas kernels, call(): pl.pallas_call(body, out_shape=(*results, token), in_specs=list(specs) +...  36.1 us
    ppermute x11, starting transfers between devices, both_ways(): lax.ppermute(down, 'rep', down_pairs)  23.9 us
    ppermute x11, waiting for transfers between devices, both_ways(): lax.ppermute(up, 'rep', up_pairs)  21.6 us
    all_to_all x3, starting transfers between devices, exchange(): return lax.all_to_all(x, 'fsdp', split_axis=0, concat_axis=0, tiled=True)  16 us
    all_to_all x1, blocking collectives, exchange(): return lax.all_to_all(x, 'fsdp', split_axis=0, concat_axis=0, tiled=True)  15.2 us
    all_to_all x3, waiting for transfers between devices, exchange(): return lax.all_to_all(x, 'fsdp', split_axis=0, concat_axis=0, tiled=True)  13 us
    ppermute x11, starting transfers between devices, both_ways(): lax.ppermute(up, 'rep', up_pairs)  9.55 us
    cond x44, local copies, waits for them, and re-layouts  8.71 us
  transfers between devices with their start and end apart: 25, of which 15 were waited for; matrix products, arithmetic and copies ran while one was open for 0% of the time, Pallas kernels for 14%

profile of v4, /device:TPU:0, one launch (start us, length us, event | category | flops | bytes accessed | tf_op | source)
XLA Modules:
  0.0 156.8 jit_solution(4764240382721592317)
XLA Ops:
  2.7 153.9 %conditional.1 = (f32[3,512,512]{2,1,0:T(8,128)}, f32[3,512,512]{2,1,0:T(8,128)}, bf16[256,16,512]{2,1,0:T(8,128)(2,1)}) conditional(s32[]{:T(128)} %convert_element_type.27, (s32[256]{0:T(256)}, bf16[1,256,16,512]{3,2,1,0:T(8,128)(2,1)}, bf16[3,512,512]{2,1,0:T(8,128)(2,1)}, bf16[3,512,512]{2,1,0:T(8,128)(2,1)}, f32[3,512,512]{2,1,0:T(8,128)}, ...), branch_computations={%region_2.7_spmd, %region_7.12_spmd} | conditional | flops 1611618688 | bytes 144080064 | solution.py:459
  5.7 3.3 %branch_1_fun.18 = (bf16[16,16,512]{2,1,0:T(8,128)(2,1)S(1)}, bf16[16,16,512]{2,1,0:T(8,128)(2,1)S(1)}, bf16[16,16,512]{2,1,0:T(8,128)(2,1)S(1)}, bf16[16,16,512...) custom-call(s32[128]{0:T(128)S(1)} %select_reduce_fusion.3.refs_0_, ...), custom_call_target="tpu_custom_call" | custom-call | bytes 4194304 | tf_op jit(solution)/shard_map/cond/branch_1_fun/pallas_call | solution.py:223
  12.7 2.8 %collective-permute-start.26 = (bf16[16,16,512]{2,1,0:T(8,128)(2,1)S(1)}, bf16[16,16,512]{2,1,0:T(8,128)(2,1)S(1)}, u32[]{:S(2)}, u32[]{:S(2)}) collective-permute-start(bf16[16,16,512]{2,1,0:T(8,128)(2,1)S(1)} %get-tuple-element.81), channel_id=1, source_target_pairs={{0,96},{32,0},{64,32},{96,64},{1,97},{33,1},{65,33},{97,65},{2,98}... | collective-permute-start | bytes 786440 | tf_op jit(solution)/shard_map/cond/branch_1_fun/ppermute | solution.py:258
  15.7 3.7 %collective-permute-done.22.refs_0_ = bf16[16,16,512]{2,1,0:T(8,128)(2,1)S(1)} collective-permute-done((bf16[16,16,512]{2,1,0:T(8,128)(2,1)S(1)}, bf16[16,16,512]{2,1,0:T(8,128)(2,1)S(1)}, u32[]{:S(2)}, u32[]{:S(2)}) %collective-permute-start.22) | collective-permute-done | bytes 262176 | tf_op jit(solution)/shard_map/cond/branch_1_fun/ppermute | solution.py:258
  21.7 1.7 %collective-permute-start.27 = (bf16[16,16,512]{2,1,0:T(8,128)(2,1)S(1)}, bf16[16,16,512]{2,1,0:T(8,128)(2,1)S(1)}, u32[]{:S(2)}, u32[]{:S(2)}) collective-permute-start(bf16[16,16,512]{2,1,0:T(8,128)(2,1)S(1)} %get-tuple-element.82), channel_id=1, source_target_pairs={{0,96},{32,0},{64,32},{96,64},{1,97},{33,1},{65,33},{97,65},{2,98}... | collective-permute-start | bytes 786440 | tf_op jit(solution)/shard_map/cond/branch_1_fun/ppermute | solution.py:258
  25.5 4.1 %collective-permute-done.24.refs_1_ = bf16[16,16,512]{2,1,0:T(8,128)(2,1)S(1)} collective-permute-done((bf16[16,16,512]{2,1,0:T(8,128)(2,1)S(1)}, bf16[16,16,512]{2,1,0:T(8,128)(2,1)S(1)}, u32[]{:S(2)}, u32[]{:S(2)}) %collective-permute-start.24) | collective-permute-done | bytes 262176 | tf_op jit(solution)/shard_map/cond/branch_1_fun/ppermute | solution.py:258
  34.5 8.2 %all-to-all-start.4 = ((bf16[32,1,16,512]{3,2,1,0:T(8,128)(2,1)}), bf16[32,1,16,512]{3,2,1,0:T(8,128)(2,1)S(1)}, u32[]{:S(2)}, u32[]{:S(2)}) async-start(bf16[32,1,16,512]{3,2,1,0:T(8,128)(2,1)} %get-tuple-element.85), calls=%async_computation.4 | async-start | bytes 1048576 | tf_op jit(solution)/shard_map/cond/branch_1_fun/all_to_all | solution.py:268
  43.5 2.4 %branch_1_fun.23 = (bf16[48,16,512]{2,1,0:T(8,128)(2,1)}, bf16[48,16,512]{2,1,0:T(8,128)(2,1)}, f32[8,128]{1,0:T(8,128)S(1)}) custom-call(bf16[24,16,512]{2,1,0:T(8,128)(2,1)S(1)} %collective-permute-done.28.refs_0_, bf16[24,16,512]{2,1,0:T(8,128)(2,1)} %collective-permute-done.29.refs_1_, bf16[48,16,512]{2,1,0:T(8,128)(2,1)S(1)} %get-tuple-element.92.refs_2_, ...), custom_call_target="tpu_custom_call" | custom-call | bytes 2359296 | tf_op jit(solution)/shard_map/cond/branch_1_fun/pallas_call | solution.py:223
  47.0 2.2 %collective-permute-start.31 = (bf16[48,16,512]{2,1,0:T(8,128)(2,1)}, bf16[48,16,512]{2,1,0:T(8,128)(2,1)S(1)}, u32[]{:S(2)}, u32[]{:S(2)}) collective-permute-start(bf16[48,16,512]{2,1,0:T(8,128)(2,1)} %get-tuple-element.95), channel_id=1, source_target_pairs={{0,96},{32,0},{64,32},{96,64},{1,97},{33,1},{65,33},{97,65},{2,98}... | collective-permute-start | bytes 2359304 | tf_op jit(solution)/shard_map/cond/branch_1_fun/ppermute | solution.py:258
  49.2 5.3 %all-to-all-done.4.refs_0_ = bf16[32,1,16,512]{3,2,1,0:T(8,128)(2,1)S(1)} async-done(((bf16[32,1,16,512]{3,2,1,0:T(8,128)(2,1)}), bf16[32,1,16,512]{3,2,1,0:T(8,128)(2,1)S(1)}, u32[]{:S(2)}, u32[]{:S(2)}) %all-to-all-start.4) | async-done | bytes 524320 | tf_op jit(solution)/shard_map/cond/branch_1_fun/all_to_all | solution.py:268
  54.5 2.6 %branch_1_fun.25 = (bf16[32,1,16,512]{3,2,1,0:T(8,128)(2,1)S(1)}, f32[8,128]{1,0:T(8,128)}) custom-call(bf16[32,1,16,512]{3,2,1,0:T(8,128)(2,1)S(1)} %all-to-all-done.4.refs_0_, bf16[3,512,512]{2,1,0:T(8,128)(2,1)} %get-tuple-element.97.refs_1_, bf16[3,512,512]{2,1,0:T(8,128)(2,1)} %get-tuple-element.98.refs_2_, f32[8,128]{1,0:T(8,128)S(1)} %get-tuple-element.99.refs_3_), custom_call_target="tpu_custom_call" | custom-call | tf_op jit(solution)/shard_map/cond/branch_1_fun/pallas_call | solution.py:223
  57.1 15.2 %all_to_all.33.refs_0_ = bf16[32,1,16,512]{3,2,1,0:T(8,128)(2,1)S(1)} all-to-all(bf16[32,1,16,512]{3,2,1,0:T(8,128)(2,1)S(1)} %get-tuple-element.100), channel_id=1, replica_groups=mesh['rep'=4,'fsdp'=32] {'fsdp'}, dimensions={0} | all-to-all | bytes 1048576 | tf_op jit(solution)/shard_map/cond/branch_1_fun/all_to_all | solution.py:268
  72.4 1.7 %branch_1_fun.24 = (bf16[32,2,16,512]{3,2,1,0:T(8,128)(2,1)S(1)}, f32[8,128]{1,0:T(8,128)}) custom-call(s32[192]{0:T(256)S(1)} %select_reduce_fusion.2.refs_0_, s32[256]{0:T(256)S(1)} %get-tuple-element.127.refs_1_, bf16[48,16,512]{2,1,0:T(8,128)(2,1)S(1)} %get-tuple-element.86.refs_2_, bf16[48,16,512]{2,1,0:T(8,128)(2,1)S(1)} %collective-permute-done.30.refs_3_, ...), custom_call_target="tpu_custom_call" | custom-call | bytes 3932160 | tf_op jit(solution)/shard_map/cond/branch_1_fun/pallas_call | solution.py:223
  75.1 3.9 %all-to-all-start.6 = ((bf16[32,2,16,512]{3,2,1,0:T(8,128)(2,1)}), bf16[32,2,16,512]{3,2,1,0:T(8,128)(2,1)S(1)}, u32[]{:S(2)}, u32[]{:S(2)}) async-start(bf16[32,2,16,512]{3,2,1,0:T(8,128)(2,1)} %branch_1_fun.27), calls=%async_computation.6 | async-start | bytes 2097152 | tf_op jit(solution)/shard_map/cond/branch_1_fun/all_to_all | solution.py:268
  79.4 3.0 %collective-permute-start.33 = (bf16[16,16,512]{2,1,0:T(8,128)(2,1)}, bf16[16,16,512]{2,1,0:T(8,128)(2,1)S(1)}, u32[]{:S(2)}, u32[]{:S(2)}) collective-permute-start(bf16[16,16,512]{2,1,0:T(8,128)(2,1)} %copy-done.24), channel_id=1, source_target_pairs={{0,96},{32,0},{64,32},{96,64},{1,97},{33,1},{65,33},{97,65},{2,98}... | collective-permute-start | bytes 786440 | tf_op jit(solution)/shard_map/cond/branch_1_fun/ppermute | solution.py:258
  82.4 6.3 %collective-permute-done.32.refs_5_ = bf16[16,16,512]{2,1,0:T(8,128)(2,1)S(1)} collective-permute-done((bf16[16,16,512]{2,1,0:T(8,128)(2,1)S(1)}, bf16[16,16,512]{2,1,0:T(8,128)(2,1)S(1)}, u32[]{:S(2)}, u32[]{:S(2)}) %collective-permute-start.32) | collective-permute-done | bytes 262176 | tf_op jit(solution)/shard_map/cond/branch_1_fun/ppermute | solution.py:258
  88.7 7.7 %all-to-all-done.6.refs_0_.refs_1_ = bf16[32,2,16,512]{3,2,1,0:T(8,128)(2,1)S(1)} async-done(((bf16[32,2,16,512]{3,2,1,0:T(8,128)(2,1)}), bf16[32,2,16,512]{3,2,1,0:T(8,128)(2,1)S(1)}, u32[]{:S(2)}, u32[]{:S(2)}) %all-to-all-start.6) | async-done | bytes 1048608 | tf_op jit(solution)/shard_map/cond/branch_1_fun/all_to_all | solution.py:268
  96.4 4.3 %branch_1_fun.28 = (bf16[32,2,16,512]{3,2,1,0:T(8,128)(2,1)S(1)}, f32[8,128]{1,0:T(8,128)}) custom-call(bf16[32,2,16,512]{3,2,1,0:T(8,128)(2,1)S(1)} %all-to-all-done.6.refs_0_.refs_1_, bf16[3,512,512]{2,1,0:T(8,128)(2,1)} %get-tuple-element.97.refs_1_, bf16[3,512,512]{2,1,0:T(8,128)(2,1)} %get-tuple-element.98.refs_2_, ...), custom_call_target="tpu_custom_call" | custom-call | tf_op jit(solution)/shard_map/cond/branch_1_fun/pallas_call | solution.py:223
  101.6 3.9 %all-to-all-start.7 = ((bf16[32,2,16,512]{3,2,1,0:T(8,128)(2,1)}), bf16[32,2,16,512]{3,2,1,0:T(8,128)(2,1)S(1)}, u32[]{:S(2)}, u32[]{:S(2)}) async-start(bf16[32,2,16,512]{3,2,1,0:T(8,128)(2,1)} %copy-done.3), calls=%async_computation.7 | async-start | bytes 2097152 | tf_op jit(solution)/shard_map/cond/branch_1_fun/all_to_all | solution.py:268
  107.9 3.0 %collective-permute-start.37 = (bf16[16,16,512]{2,1,0:T(8,128)(2,1)S(1)}, bf16[16,16,512]{2,1,0:T(8,128)(2,1)S(1)}, u32[]{:S(2)}, u32[]{:S(2)}) collective-permute-start(bf16[16,16,512]{2,1,0:T(8,128)(2,1)S(1)} %collective-permute-done.33.refs_4_), channel_id=1, source_target_pairs={{0,96},{32,0},{64,32},{96,64},{1,97},{33,1},{65,33},{97,65},{2,98}... | collective-permute-start | bytes 786440 | tf_op jit(solution)/shard_map/cond/branch_1_fun/ppermute | solution.py:258
  110.9 3.9 %collective-permute-done.34.refs_3_ = bf16[16,16,512]{2,1,0:T(8,128)(2,1)S(1)} collective-permute-done((bf16[16,16,512]{2,1,0:T(8,128)(2,1)S(1)}, bf16[16,16,512]{2,1,0:T(8,128)(2,1)S(1)}, u32[]{:S(2)}, u32[]{:S(2)}) %collective-permute-start.34) | collective-permute-done | bytes 262176 | tf_op jit(solution)/shard_map/cond/branch_1_fun/ppermute | solution.py:258
  114.8 3.0 %collective-permute-done.35.refs_6_ = bf16[16,16,512]{2,1,0:T(8,128)(2,1)S(1)} collective-permute-done((bf16[16,16,512]{2,1,0:T(8,128)(2,1)}, bf16[16,16,512]{2,1,0:T(8,128)(2,1)S(1)}, u32[]{:S(2)}, u32[]{:S(2)}) %collective-permute-start.35) | collective-permute-done | bytes 262176 | tf_op jit(solution)/shard_map/cond/branch_1_fun/ppermute | solution.py:258
  118.7 2.2 %branch_1_fun.29 = (bf16[256,16,512]{2,1,0:T(8,128)(2,1)}, f32[8,128]{1,0:T(8,128)S(1)}) custom-call(s32[128]{0:T(128)S(1)} %select_reduce_fusion.3.refs_0_, bf16[16,16,512]{2,1,0:T(8,128)(2,1)S(1)} %get-tuple-element.104.refs_1_, bf16[16,16,512]{2,1,0:T(8,128)(2,1)S(1)} %copy-done.25, bf16[16,16,512]{2,1,0:T(8,128)(2,1)S(1)} %collective-permute-done.34.refs_3_, ...), custom_call_target="tpu_custom_call" | custom-call | bytes 3145728 | tf_op jit(solution)/shard_map/cond/branch_1_fun/pallas_call | solution.py:223
  124.6 3.2 %collective-permute-start.39 = (bf16[24,16,512]{2,1,0:T(8,128)(2,1)S(1)}, bf16[24,16,512]{2,1,0:T(8,128)(2,1)S(1)}, u32[]{:S(2)}, u32[]{:S(2)}) collective-permute-start(bf16[24,16,512]{2,1,0:T(8,128)(2,1)S(1)} %get-tuple-element.112.refs_2_), channel_id=1, source_target_pairs={{0,96},{32,0},{64,32},{96,64},{1,97},{33,1},{65,33},{97,65},{2,98}... | collective-permute-start | bytes 1179656 | tf_op jit(solution)/shard_map/cond/branch_1_fun/ppermute | solution.py:258
  127.9 2.0 %collective-permute-start.43 = (bf16[24,16,512]{2,1,0:T(8,128)(2,1)S(1)}, bf16[24,16,512]{2,1,0:T(8,128)(2,1)}, u32[]{:S(2)}, u32[]{:S(2)}) collective-permute-start(bf16[24,16,512]{2,1,0:T(8,128)(2,1)S(1)} %get-tuple-element.112.refs_2_), channel_id=1, source_target_pairs={{0,32},{32,64},{64,96},{96,0},{1,33},{33,65},{65,97},{97,1},{2,34}... | collective-permute-start | bytes 1179656 | tf_op jit(solution)/shard_map/cond/branch_1_fun/ppermute | solution.py:258
  129.9 7.0 %branch_1_fun.31 = (f32[3,512,512]{2,1,0:T(8,128)}, f32[3,512,512]{2,1,0:T(8,128)}, f32[8,128]{1,0:T(8,128)S(1)}) custom-call(bf16[32,1,16,512]{3,2,1,0:T(8,128)(2,1)S(1)} %all-to-all-done.4.refs_0_, bf16[32,2,16,512]{3,2,1,0:T(8,128)(2,1)S(1)} %all-to-all-done.6.refs_0_.refs_1_, f32[3,512,512]{2,1,0:T(8,128)} %get-tuple-element.102.refs_2_, ...), custom_call_target="tpu_custom_call" | custom-call | flops 1610612736 | bytes 14155776 | tf_op jit(solution)/shard_map/cond/branch_1_fun/pallas_call | solution.py:223
  138.8 3.2 %collective-permute-start.41 = (bf16[24,16,512]{2,1,0:T(8,128)(2,1)}, bf16[24,16,512]{2,1,0:T(8,128)(2,1)S(1)}, u32[]{:S(2)}, u32[]{:S(2)}) collective-permute-start(bf16[24,16,512]{2,1,0:T(8,128)(2,1)} %get-tuple-element.115.refs_4_), channel_id=1, source_target_pairs={{0,96},{32,0},{64,32},{96,64},{1,97},{33,1},{65,33},{97,65},{2,98}... | collective-permute-start | bytes 1179656 | tf_op jit(solution)/shard_map/cond/branch_1_fun/ppermute | solution.py:258
  142.1 2.0 %branch_1_fun.33 = (bf16[256,16,512]{2,1,0:T(8,128)(2,1)}, f32[8,128]{1,0:T(8,128)}) custom-call(s32[128]{0:T(128)S(1)} %select_reduce_fusion.3.refs_0_, bf16[16,16,512]{2,1,0:T(8,128)(2,1)S(1)} %copy-done.16, bf16[16,16,512]{2,1,0:T(8,128)(2,1)S(1)} %copy-done.20, bf16[256,16,512]{2,1,0:T(8,128)(2,1)} %get-tuple-element.116.refs_3_), custom_call_target="tpu_custom_call", output_to_operand_aliasing={{0}: (3, {})} | custom-call | bytes 1048576 | tf_op jit(solution)/shard_map/cond/branch_1_fun/pallas_call | solution.py:223
  144.0 1.8 %collective-permute-done.42.refs_3_ = bf16[24,16,512]{2,1,0:T(8,128)(2,1)} collective-permute-done((bf16[24,16,512]{2,1,0:T(8,128)(2,1)S(1)}, bf16[24,16,512]{2,1,0:T(8,128)(2,1)}, u32[]{:S(2)}, u32[]{:S(2)}) %collective-permute-start.42) | collective-permute-done | bytes 393248 | tf_op jit(solution)/shard_map/cond/branch_1_fun/ppermute | solution.py:258
  146.4 4.6 %branch_1_fun.34 = (bf16[256,16,512]{2,1,0:T(8,128)(2,1)}, f32[8,128]{1,0:T(8,128)}) custom-call(s32[192]{0:T(256)} %copy-done.27, bf16[24,16,512]{2,1,0:T(8,128)(2,1)} %copy-done.11, bf16[24,16,512]{2,1,0:T(8,128)(2,1)} %copy-done.12, bf16[24,16,512]{2,1,0:T(8,128)(2,1)} %collective-permute-done.42.refs_3_, ...), custom_call_target="tpu_custom_call", output_to_operand_aliasing={{0}: (7, {})} | custom-call | bytes 4718592 | tf_op jit(solution)/shard_map/cond/branch_1_fun/pallas_call | solution.py:223
  151.1 2.0 %collective-permute-done.40.refs_1_ = bf16[24,16,512]{2,1,0:T(8,128)(2,1)S(1)} collective-permute-done((bf16[24,16,512]{2,1,0:T(8,128)(2,1)}, bf16[24,16,512]{2,1,0:T(8,128)(2,1)S(1)}, u32[]{:S(2)}, u32[]{:S(2)}) %collective-permute-start.40) | collective-permute-done | bytes 393248 | tf_op jit(solution)/shard_map/cond/branch_1_fun/ppermute | solution.py:258
  153.9 2.7 %branch_1_fun.35 = (bf16[256,16,512]{2,1,0:T(8,128)(2,1)}, f32[8,128]{1,0:T(8,128)}) custom-call(s32[192]{0:T(256)} %copy-done.27, bf16[24,16,512]{2,1,0:T(8,128)(2,1)} %copy-done.48, bf16[24,16,512]{2,1,0:T(8,128)(2,1)} %copy-done.49, bf16[256,16,512]{2,1,0:T(8,128)(2,1)} %get-tuple-element.118.refs_3_), custom_call_target="tpu_custom_call", output_to_operand_aliasing={{0}: (3, {})} | custom-call | bytes 1572864 | tf_op jit(solution)/shard_map/cond/branch_1_fun/pallas_call | solution.py:223
  (96 shorter events, 31.9 us)
Async XLA Ops:
  2.9 20.6 %copy-start.41 = (bf16[1,256,16,512]{3,2,1,0:T(8,128)(2,1)S(1)}, bf16[1,256,16,512]{3,2,1,0:T(8,128)(2,1)}, u32[]{:S(2)}) copy-start(bf16[1,256,16,512]{3,2,1,0:T(8,128)(2,1)} %get-tuple-element.73) | copy-start | bytes 12582916 | tf_op jit(solution)/shard_map/cond
  9.0 10.4 %collective-permute-start.22 = (bf16[16,16,512]{2,1,0:T(8,128)(2,1)S(1)}, bf16[16,16,512]{2,1,0:T(8,128)(2,1)S(1)}, u32[]{:S(2)}, u32[]{:S(2)}) collective-permute-start(bf16[16,16,512]{2,1,0:T(8,128)(2,1)S(1)} %get-tuple-element.75), channel_id=1, source_target_pairs={{0,32},{32,64},{64,96},{96,0},{1,33},{33,65},{65,97},{97,1},{2,34}... | collective-permute-start | bytes 786440 | tf_op jit(solution)/shard_map/cond/branch_1_fun/ppermute | solution.py:258
  10.7 9.2 %collective-permute-start.23 = (bf16[16,16,512]{2,1,0:T(8,128)(2,1)S(1)}, bf16[16,16,512]{2,1,0:T(8,128)(2,1)S(1)}, u32[]{:S(2)}, u32[]{:S(2)}) collective-permute-start(bf16[16,16,512]{2,1,0:T(8,128)(2,1)S(1)} %get-tuple-element.76), channel_id=1, source_target_pairs={{0,96},{32,0},{64,32},{96,64},{1,97},{33,1},{65,33},{97,65},{2,98}... | collective-permute-start | bytes 786440 | tf_op jit(solution)/shard_map/cond/branch_1_fun/ppermute | solution.py:258
  12.3 13.2 %collective-permute-start.25 = (bf16[16,16,512]{2,1,0:T(8,128)(2,1)S(1)}, bf16[16,16,512]{2,1,0:T(8,128)(2,1)S(1)}, u32[]{:S(2)}, u32[]{:S(2)}) collective-permute-start(bf16[16,16,512]{2,1,0:T(8,128)(2,1)S(1)} %get-tuple-element.80), channel_id=1, source_target_pairs={{0,32},{32,64},{64,96},{96,0},{1,33},{33,65},{65,97},{97,1},{2,34}... | collective-permute-start | bytes 786440 | tf_op jit(solution)/shard_map/cond/branch_1_fun/ppermute | solution.py:258
  12.7 12.8 %collective-permute-start.26 = (bf16[16,16,512]{2,1,0:T(8,128)(2,1)S(1)}, bf16[16,16,512]{2,1,0:T(8,128)(2,1)S(1)}, u32[]{:S(2)}, u32[]{:S(2)}) collective-permute-start(bf16[16,16,512]{2,1,0:T(8,128)(2,1)S(1)} %get-tuple-element.81), channel_id=1, source_target_pairs={{0,96},{32,0},{64,32},{96,64},{1,97},{33,1},{65,33},{97,65},{2,98}... | collective-permute-start | bytes 786440 | tf_op jit(solution)/shard_map/cond/branch_1_fun/ppermute | solution.py:258
  20.1 9.6 %collective-permute-start.24 = (bf16[16,16,512]{2,1,0:T(8,128)(2,1)S(1)}, bf16[16,16,512]{2,1,0:T(8,128)(2,1)S(1)}, u32[]{:S(2)}, u32[]{:S(2)}) collective-permute-start(bf16[16,16,512]{2,1,0:T(8,128)(2,1)S(1)} %get-tuple-element.79), channel_id=1, source_target_pairs={{0,32},{32,64},{64,96},{96,0},{1,33},{33,65},{65,97},{97,1},{2,34}... | collective-permute-start | bytes 786440 | tf_op jit(solution)/shard_map/cond/branch_1_fun/ppermute | solution.py:258
  21.7 8.0 %collective-permute-start.27 = (bf16[16,16,512]{2,1,0:T(8,128)(2,1)S(1)}, bf16[16,16,512]{2,1,0:T(8,128)(2,1)S(1)}, u32[]{:S(2)}, u32[]{:S(2)}) collective-permute-start(bf16[16,16,512]{2,1,0:T(8,128)(2,1)S(1)} %get-tuple-element.82), channel_id=1, source_target_pairs={{0,96},{32,0},{64,32},{96,64},{1,97},{33,1},{65,33},{97,65},{2,98}... | collective-permute-start | bytes 786440 | tf_op jit(solution)/shard_map/cond/branch_1_fun/ppermute | solution.py:258
  23.5 100.2 %copy-start.27 = (s32[192]{0:T(256)}, s32[192]{0:T(256)S(1)}, u32[]{:S(2)}) copy-start(s32[192]{0:T(256)S(1)} %select_reduce_fusion.2.refs_0_) | copy-start | bytes 2308 | tf_op jit(solution)/shard_map/cond
  31.3 11.5 %collective-permute-start.28 = (bf16[24,16,512]{2,1,0:T(8,128)(2,1)}, bf16[24,16,512]{2,1,0:T(8,128)(2,1)S(1)}, u32[]{:S(2)}, u32[]{:S(2)}) collective-permute-start(bf16[24,16,512]{2,1,0:T(8,128)(2,1)} %get-tuple-element.90), channel_id=1, source_target_pairs={{0,32},{32,64},{64,96},{96,0},{1,33},{33,65},{65,97},{97,1},{2,34}... | collective-permute-start | bytes 1179656 | tf_op jit(solution)/shard_map/cond/branch_1_fun/ppermute | solution.py:258
  32.9 10.0 %collective-permute-start.29 = (bf16[24,16,512]{2,1,0:T(8,128)(2,1)}, bf16[24,16,512]{2,1,0:T(8,128)(2,1)}, u32[]{:S(2)}, u32[]{:S(2)}) collective-permute-start(bf16[24,16,512]{2,1,0:T(8,128)(2,1)} %get-tuple-element.91), channel_id=1, source_target_pairs={{0,96},{32,0},{64,32},{96,64},{1,97},{33,1},{65,33},{97,65},{2,98}... | collective-permute-start | bytes 1179656 | tf_op jit(solution)/shard_map/cond/branch_1_fun/ppermute | solution.py:258
  34.5 19.9 %all-to-all-start.4 = ((bf16[32,1,16,512]{3,2,1,0:T(8,128)(2,1)}), bf16[32,1,16,512]{3,2,1,0:T(8,128)(2,1)S(1)}, u32[]{:S(2)}, u32[]{:S(2)}) async-start(bf16[32,1,16,512]{3,2,1,0:T(8,128)(2,1)} %get-tuple-element.85), calls=%async_computation.4 | async-start | bytes 1048576 | tf_op jit(solution)/shard_map/cond/branch_1_fun/all_to_all | solution.py:268
  46.0 26.4 %collective-permute-start.30 = (bf16[48,16,512]{2,1,0:T(8,128)(2,1)}, bf16[48,16,512]{2,1,0:T(8,128)(2,1)S(1)}, u32[]{:S(2)}, u32[]{:S(2)}) collective-permute-start(bf16[48,16,512]{2,1,0:T(8,128)(2,1)} %get-tuple-element.94), channel_id=1, source_target_pairs={{0,32},{32,64},{64,96},{96,0},{1,33},{33,65},{65,97},{97,1},{2,34}... | collective-permute-start | bytes 2359304 | tf_op jit(solution)/shard_map/cond/branch_1_fun/ppermute | solution.py:258
  47.0 25.4 %collective-permute-start.31 = (bf16[48,16,512]{2,1,0:T(8,128)(2,1)}, bf16[48,16,512]{2,1,0:T(8,128)(2,1)S(1)}, u32[]{:S(2)}, u32[]{:S(2)}) collective-permute-start(bf16[48,16,512]{2,1,0:T(8,128)(2,1)} %get-tuple-element.95), channel_id=1, source_target_pairs={{0,96},{32,0},{64,32},{96,64},{1,97},{33,1},{65,33},{97,65},{2,98}... | collective-permute-start | bytes 2359304 | tf_op jit(solution)/shard_map/cond/branch_1_fun/ppermute | solution.py:258
  72.4 7.0 %copy-start.24 = (bf16[16,16,512]{2,1,0:T(8,128)(2,1)}, bf16[16,16,512]{2,1,0:T(8,128)(2,1)S(1)}, u32[]{:S(2)}) copy-start(bf16[16,16,512]{2,1,0:T(8,128)(2,1)S(1)} %get-tuple-element.105.refs_2_) | copy-start | bytes 786436 | tf_op jit(solution)/shard_map/cond
  75.1 21.3 %all-to-all-start.6 = ((bf16[32,2,16,512]{3,2,1,0:T(8,128)(2,1)}), bf16[32,2,16,512]{3,2,1,0:T(8,128)(2,1)S(1)}, u32[]{:S(2)}, u32[]{:S(2)}) async-start(bf16[32,2,16,512]{3,2,1,0:T(8,128)(2,1)} %branch_1_fun.27), calls=%async_computation.6 | async-start | bytes 2097152 | tf_op jit(solution)/shard_map/cond/branch_1_fun/all_to_all | solution.py:268
  79.1 9.7 %collective-permute-start.32 = (bf16[16,16,512]{2,1,0:T(8,128)(2,1)S(1)}, bf16[16,16,512]{2,1,0:T(8,128)(2,1)S(1)}, u32[]{:S(2)}, u32[]{:S(2)}) collective-permute-start(bf16[16,16,512]{2,1,0:T(8,128)(2,1)S(1)} %get-tuple-element.104.refs_1_), channel_id=1, source_target_pairs={{0,32},{32,64},{64,96},{96,0},{1,33},{33,65},{65,97},{97,1},{2,34}... | collective-permute-start | bytes 786440 | tf_op jit(solution)/shard_map/cond/branch_1_fun/ppermute | solution.py:258
  79.4 9.3 %collective-permute-start.33 = (bf16[16,16,512]{2,1,0:T(8,128)(2,1)}, bf16[16,16,512]{2,1,0:T(8,128)(2,1)S(1)}, u32[]{:S(2)}, u32[]{:S(2)}) collective-permute-start(bf16[16,16,512]{2,1,0:T(8,128)(2,1)} %copy-done.24), channel_id=1, source_target_pairs={{0,96},{32,0},{64,32},{96,64},{1,97},{33,1},{65,33},{97,65},{2,98}... | collective-permute-start | bytes 786440 | tf_op jit(solution)/shard_map/cond/branch_1_fun/ppermute | solution.py:258
  101.6 22.1 %all-to-all-start.7 = ((bf16[32,2,16,512]{3,2,1,0:T(8,128)(2,1)}), bf16[32,2,16,512]{3,2,1,0:T(8,128)(2,1)S(1)}, u32[]{:S(2)}, u32[]{:S(2)}) async-start(bf16[32,2,16,512]{3,2,1,0:T(8,128)(2,1)} %copy-done.3), calls=%async_computation.7 | async-start | bytes 2097152 | tf_op jit(solution)/shard_map/cond/branch_1_fun/all_to_all | solution.py:268
  105.6 9.2 %collective-permute-start.34 = (bf16[16,16,512]{2,1,0:T(8,128)(2,1)S(1)}, bf16[16,16,512]{2,1,0:T(8,128)(2,1)S(1)}, u32[]{:S(2)}, u32[]{:S(2)}) collective-permute-start(bf16[16,16,512]{2,1,0:T(8,128)(2,1)S(1)} %get-tuple-element.104.refs_1_), channel_id=1, source_target_pairs={{0,96},{32,0},{64,32},{96,64},{1,97},{33,1},{65,33},{97,65},{2,98}... | collective-permute-start | bytes 786440 | tf_op jit(solution)/shard_map/cond/branch_1_fun/ppermute | solution.py:258
  107.1 10.6 %collective-permute-start.35 = (bf16[16,16,512]{2,1,0:T(8,128)(2,1)}, bf16[16,16,512]{2,1,0:T(8,128)(2,1)S(1)}, u32[]{:S(2)}, u32[]{:S(2)}) collective-permute-start(bf16[16,16,512]{2,1,0:T(8,128)(2,1)} %copy-done.24), channel_id=1, source_target_pairs={{0,32},{32,64},{64,96},{96,0},{1,33},{33,65},{65,97},{97,1},{2,34}... | collective-permute-start | bytes 786440 | tf_op jit(solution)/shard_map/cond/branch_1_fun/ppermute | solution.py:258
  107.7 14.6 %collective-permute-start.36 = (bf16[16,16,512]{2,1,0:T(8,128)(2,1)S(1)}, bf16[16,16,512]{2,1,0:T(8,128)(2,1)S(1)}, u32[]{:S(2)}, u32[]{:S(2)}) collective-permute-start(bf16[16,16,512]{2,1,0:T(8,128)(2,1)S(1)} %collective-permute-done.32.refs_5_), channel_id=1, source_target_pairs={{0,32},{32,64},{64,96},{96,0},{1,33},{33,65},{65,97},{97,1},{2,34}... | collective-permute-start | bytes 786440 | tf_op jit(solution)/shard_map/cond/branch_1_fun/ppermute | solution.py:258
  107.9 15.0 %collective-permute-start.37 = (bf16[16,16,512]{2,1,0:T(8,128)(2,1)S(1)}, bf16[16,16,512]{2,1,0:T(8,128)(2,1)S(1)}, u32[]{:S(2)}, u32[]{:S(2)}) collective-permute-start(bf16[16,16,512]{2,1,0:T(8,128)(2,1)S(1)} %collective-permute-done.33.refs_4_), channel_id=1, source_target_pairs={{0,96},{32,0},{64,32},{96,64},{1,97},{33,1},{65,33},{97,65},{2,98}... | collective-permute-start | bytes 786440 | tf_op jit(solution)/shard_map/cond/branch_1_fun/ppermute | solution.py:258
  124.5 14.3 %copy-start.11 = (bf16[24,16,512]{2,1,0:T(8,128)(2,1)}, bf16[24,16,512]{2,1,0:T(8,128)(2,1)S(1)}, u32[]{:S(2)}) copy-start(bf16[24,16,512]{2,1,0:T(8,128)(2,1)S(1)} %get-tuple-element.111.refs_1_) | copy-start | bytes 1179652 | tf_op jit(solution)/shard_map/cond
  124.5 14.3 %copy-start.12 = (bf16[24,16,512]{2,1,0:T(8,128)(2,1)}, bf16[24,16,512]{2,1,0:T(8,128)(2,1)S(1)}, u32[]{:S(2)}) copy-start(bf16[24,16,512]{2,1,0:T(8,128)(2,1)S(1)} %get-tuple-element.112.refs_2_) | copy-start | bytes 1179652 | tf_op jit(solution)/shard_map/cond
  124.6 13.3 %collective-permute-start.38 = (bf16[24,16,512]{2,1,0:T(8,128)(2,1)S(1)}, bf16[24,16,512]{2,1,0:T(8,128)(2,1)S(1)}, u32[]{:S(2)}, u32[]{:S(2)}) collective-permute-start(bf16[24,16,512]{2,1,0:T(8,128)(2,1)S(1)} %get-tuple-element.111.refs_1_), channel_id=1, source_target_pairs={{0,32},{32,64},{64,96},{96,0},{1,33},{33,65},{65,97},{97,1},{2,34}... | collective-permute-start | bytes 1179656 | tf_op jit(solution)/shard_map/cond/branch_1_fun/ppermute | solution.py:258
  124.6 13.3 %collective-permute-start.39 = (bf16[24,16,512]{2,1,0:T(8,128)(2,1)S(1)}, bf16[24,16,512]{2,1,0:T(8,128)(2,1)S(1)}, u32[]{:S(2)}, u32[]{:S(2)}) collective-permute-start(bf16[24,16,512]{2,1,0:T(8,128)(2,1)S(1)} %get-tuple-element.112.refs_2_), channel_id=1, source_target_pairs={{0,96},{32,0},{64,32},{96,64},{1,97},{33,1},{65,33},{97,65},{2,98}... | collective-permute-start | bytes 1179656 | tf_op jit(solution)/shard_map/cond/branch_1_fun/ppermute | solution.py:258
  127.9 18.0 %collective-permute-start.42 = (bf16[24,16,512]{2,1,0:T(8,128)(2,1)S(1)}, bf16[24,16,512]{2,1,0:T(8,128)(2,1)}, u32[]{:S(2)}, u32[]{:S(2)}) collective-permute-start(bf16[24,16,512]{2,1,0:T(8,128)(2,1)S(1)} %get-tuple-element.111.refs_1_), channel_id=1, source_target_pairs={{0,96},{32,0},{64,32},{96,64},{1,97},{33,1},{65,33},{97,65},{2,98}... | collective-permute-start | bytes 1179656 | tf_op jit(solution)/shard_map/cond/branch_1_fun/ppermute | solution.py:258
  127.9 18.5 %collective-permute-start.43 = (bf16[24,16,512]{2,1,0:T(8,128)(2,1)S(1)}, bf16[24,16,512]{2,1,0:T(8,128)(2,1)}, u32[]{:S(2)}, u32[]{:S(2)}) collective-permute-start(bf16[24,16,512]{2,1,0:T(8,128)(2,1)S(1)} %get-tuple-element.112.refs_2_), channel_id=1, source_target_pairs={{0,32},{32,64},{64,96},{96,0},{1,33},{33,65},{65,97},{97,1},{2,34}... | collective-permute-start | bytes 1179656 | tf_op jit(solution)/shard_map/cond/branch_1_fun/ppermute | solution.py:258
  129.9 12.2 %copy-start.16 = (bf16[16,16,512]{2,1,0:T(8,128)(2,1)S(1)}, bf16[16,16,512]{2,1,0:T(8,128)(2,1)}, u32[]{:S(2)}) copy-start(bf16[16,16,512]{2,1,0:T(8,128)(2,1)} %copy-done.15) | copy-start | bytes 786436 | tf_op jit(solution)/shard_map/cond
  129.9 12.2 %copy-start.20 = (bf16[16,16,512]{2,1,0:T(8,128)(2,1)S(1)}, bf16[16,16,512]{2,1,0:T(8,128)(2,1)}, u32[]{:S(2)}) copy-start(bf16[16,16,512]{2,1,0:T(8,128)(2,1)} %copy-done.19) | copy-start | bytes 786436 | tf_op jit(solution)/shard_map/cond
  138.8 14.2 %collective-permute-start.40 = (bf16[24,16,512]{2,1,0:T(8,128)(2,1)}, bf16[24,16,512]{2,1,0:T(8,128)(2,1)S(1)}, u32[]{:S(2)}, u32[]{:S(2)}) collective-permute-start(bf16[24,16,512]{2,1,0:T(8,128)(2,1)} %get-tuple-element.114.refs_5_), channel_id=1, source_target_pairs={{0,32},{32,64},{64,96},{96,0},{1,33},{33,65},{65,97},{97,1},{2,34}... | collective-permute-start | bytes 1179656 | tf_op jit(solution)/shard_map/cond/branch_1_fun/ppermute | solution.py:258
  138.8 14.2 %collective-permute-start.41 = (bf16[24,16,512]{2,1,0:T(8,128)(2,1)}, bf16[24,16,512]{2,1,0:T(8,128)(2,1)S(1)}, u32[]{:S(2)}, u32[]{:S(2)}) collective-permute-start(bf16[24,16,512]{2,1,0:T(8,128)(2,1)} %get-tuple-element.115.refs_4_), channel_id=1, source_target_pairs={{0,96},{32,0},{64,32},{96,64},{1,97},{33,1},{65,33},{97,65},{2,98}... | collective-permute-start | bytes 1179656 | tf_op jit(solution)/shard_map/cond/branch_1_fun/ppermute | solution.py:258
  (15 other events, 18.2 us)

commit v5 on v4

--- a/solution.py
+++ b/solution.py
@@ -122,23 +122,25 @@
 
 def place_kernel(plan, last, table, *refs):
     sources, out, sem = refs[: len(plan)], refs[-2], refs[-1]
-
-    def each(act):
-        for source, (start, count, shift) in zip(sources, plan):
-
-            def one(j, _, source=source, start=start, shift=shift):
-                block = table[start + j]
-
-                @pl.when(block <= last)
-                def _():
-                    act(pltpu.make_async_copy(source.at[shift + j], out.at[block], sem))
-
-                return 0
-
-            lax.fori_loop(0, count, one, 0)
-
-    each(lambda copy: copy.start())
-    each(lambda copy: copy.wait())
+    started = jnp.int32(0)
+    for source, (start, count, shift) in zip(sources, plan):
+
+        def one(j, n, source=source, start=start, shift=shift):
+            block = table[start + j]
+
+            @pl.when(block <= last)
+            def _():
+                pltpu.make_async_copy(source.at[shift + j], out.at[block], sem).start()
+
+            return n + jnp.where(block <= last, 1, 0)
+
+        started = lax.fori_loop(0, count, one, started, unroll=4)
+
+    def done(_, n):
+        pltpu.make_async_copy(sources[0].at[0], out.at[0], sem).wait()
+        return n
+
+    lax.fori_loop(0, started, done, 0)
 
 
 def apply_kernel(held, left, right, shaped):
@@ -164,7 +166,7 @@
     new_right[0] = decay_rate * right[0] + weight * right_gram
 
 
-def step(size_rest, grads, owner, factor_left, factor_right, precond_left, precond_right):
+def step(size_rest, grads, owner, col_rank, factor_left, factor_right, precond_left, precond_right):
     rows = grads[0]
     blocks, band, width = rows.shape
     columns = lax.axis_size("fsdp")
@@ -178,8 +180,6 @@
 
     position = jnp.arange(blocks, dtype=jnp.int32)
     earlier = position[None, :] < position[:, None]
-    same_owner = (owner[:, None] == owner[None, :]) & earlier
-    col_rank = jnp.sum(same_owner.astype(jnp.int32), axis=1)
     rep_of = col_rank % replicas
     local_slot = col_rank // replicas
     relative = (rep_of - my_rep) % replicas
@@ -453,15 +453,17 @@
 
 
 def local(grads, owner, *others):
-    columns = jnp.arange(lax.axis_size("fsdp"), dtype=jnp.int32)
-    counts = jnp.sum((owner[None, :] == columns[:, None]).astype(jnp.int32), axis=1)
-    longest = jnp.sum((counts > 4).astype(jnp.int32) + (counts > 8).astype(jnp.int32))
+    position = jnp.arange(owner.shape[0], dtype=jnp.int32)
+    same_owner = (owner[:, None] == owner[None, :]) & (position[None, :] < position[:, None])
+    col_rank = jnp.sum(same_owner.astype(jnp.int32), axis=1)
+    longest = jnp.sum(((col_rank == 4) | (col_rank == 8)).astype(jnp.int32))
     return lax.cond(
         longest <= 48,
         functools.partial(step, 48),
         functools.partial(step, 56),
         grads,
         owner,
+        col_rank,
         *others,
     )
 

time: 158 us -> 156 us (0.987)
  Pallas kernels: 36.1 us -> 34 us
  waiting for transfers between devices: 40.9 us -> 42.7 us
    pallas_call x15, Pallas kernels: 36.1 us -> 34 us  [call(): pl.pallas_call(body, out_shape=(*results, token), in_specs=list(specs) +...]
    ppermute x11, waiting for transfers between devices: 21.6 us -> 23.3 us  [both_ways(): lax.ppermute(up, 'rep', up_pairs)]
  transfers between devices with their start and end apart: 25 -> 25, of which waited for: 15 -> 15; matrix products, arithmetic and copies ran while one was open for 0% -> 0% of each run, Pallas kernels for 14% -> 13%
where the time goes in v5:
time: 156 us
  starting transfers between devices  49.5 us (32%)
  waiting for transfers between devices  42.7 us (27%)
  Pallas kernels  34 us (22%)
  blocking collectives  15.2 us (10%)
  local copies, waits for them, and re-layouts  8.72 us (6%)
  other arithmetic  3.73 us (2%)
    pallas_call x15, Pallas kernels, call(): pl.pallas_call(body, out_shape=(*results, token), in_specs=list(specs) +...  34 us
    ppermute x11, starting transfers between devices, both_ways(): lax.ppermute(down, 'rep', down_pairs)  23.9 us
    ppermute x11, waiting for transfers between devices, both_ways(): lax.ppermute(up, 'rep', up_pairs)  23.3 us
    all_to_all x3, starting transfers between devices, exchange(): return lax.all_to_all(x, 'fsdp', split_axis=0, concat_axis=0, tiled=True)  16 us
    all_to_all x1, blocking collectives, exchange(): return lax.all_to_all(x, 'fsdp', split_axis=0, concat_axis=0, tiled=True)  15.2 us
    all_to_all x3, waiting for transfers between devices, exchange(): return lax.all_to_all(x, 'fsdp', split_axis=0, concat_axis=0, tiled=True)  12.9 us
    ppermute x11, starting transfers between devices, both_ways(): lax.ppermute(up, 'rep', up_pairs)  9.54 us
    cond x44, local copies, waits for them, and re-layouts  8.71 us
  transfers between devices with their start and end apart: 25, of which 15 were waited for; matrix products, arithmetic and copies ran while one was open for 0% of the time, Pallas kernels for 13%

profile of v5, /device:TPU:0, one launch (start us, length us, event | category | flops | bytes accessed | tf_op | source)
XLA Modules:
  0.0 155.8 jit_solution(13712776125277486381)
XLA Ops:
  2.9 152.7 %conditional.1 = (f32[3,512,512]{2,1,0:T(8,128)}, f32[3,512,512]{2,1,0:T(8,128)}, bf16[256,16,512]{2,1,0:T(8,128)(2,1)}) conditional(s32[]{:T(128)} %convert_element_type.17, (s32[256]{0:T(256)S(1)}, s32[256]{0:T(256)}, bf16[1,256,16,512]{3,2,1,0:T(8,128)(2,1)}, bf16[3,512,512]{2,1,0:T(8,128)(2,1)}, bf16[3,512,512]{2,1,0:T(8,128)(2,1)}, ...), branch_computations={%region_2.6_spmd, %region_6.10_spmd} | conditional | flops 1611291264 | bytes 144078016 | solution.py:460
  4.9 3.3 %branch_1_fun.18 = (bf16[16,16,512]{2,1,0:T(8,128)(2,1)S(1)}, bf16[16,16,512]{2,1,0:T(8,128)(2,1)S(1)}, bf16[16,16,512]{2,1,0:T(8,128)(2,1)S(1)}, bf16[16,16,512...) custom-call(s32[128]{0:T(128)S(1)} %select_reduce_fusion.3.refs_0_, ...), custom_call_target="tpu_custom_call" | custom-call | bytes 4194304 | tf_op jit(solution)/shard_map/cond/branch_1_fun/pallas_call | solution.py:223
  11.9 2.8 %collective-permute-start.26 = (bf16[16,16,512]{2,1,0:T(8,128)(2,1)S(1)}, bf16[16,16,512]{2,1,0:T(8,128)(2,1)S(1)}, u32[]{:S(2)}, u32[]{:S(2)}) collective-permute-start(bf16[16,16,512]{2,1,0:T(8,128)(2,1)S(1)} %get-tuple-element.87), channel_id=1, source_target_pairs={{0,96},{32,0},{64,32},{96,64},{1,97},{33,1},{65,33},{97,65},{2,98}... | collective-permute-start | bytes 786440 | tf_op jit(solution)/shard_map/cond/branch_1_fun/ppermute | solution.py:258
  14.9 3.7 %collective-permute-done.22.refs_0_ = bf16[16,16,512]{2,1,0:T(8,128)(2,1)S(1)} collective-permute-done((bf16[16,16,512]{2,1,0:T(8,128)(2,1)S(1)}, bf16[16,16,512]{2,1,0:T(8,128)(2,1)S(1)}, u32[]{:S(2)}, u32[]{:S(2)}) %collective-permute-start.22) | collective-permute-done | bytes 262176 | tf_op jit(solution)/shard_map/cond/branch_1_fun/ppermute | solution.py:258
  24.7 4.1 %collective-permute-done.24.refs_1_ = bf16[16,16,512]{2,1,0:T(8,128)(2,1)S(1)} collective-permute-done((bf16[16,16,512]{2,1,0:T(8,128)(2,1)S(1)}, bf16[16,16,512]{2,1,0:T(8,128)(2,1)S(1)}, u32[]{:S(2)}, u32[]{:S(2)}) %collective-permute-start.24) | collective-permute-done | bytes 262176 | tf_op jit(solution)/shard_map/cond/branch_1_fun/ppermute | solution.py:258
  33.7 8.2 %all-to-all-start.4 = ((bf16[32,1,16,512]{3,2,1,0:T(8,128)(2,1)}), bf16[32,1,16,512]{3,2,1,0:T(8,128)(2,1)S(1)}, u32[]{:S(2)}, u32[]{:S(2)}) async-start(bf16[32,1,16,512]{3,2,1,0:T(8,128)(2,1)} %get-tuple-element.91), calls=%async_computation.4 | async-start | bytes 1048576 | tf_op jit(solution)/shard_map/cond/branch_1_fun/all_to_all | solution.py:268
  42.7 2.4 %branch_1_fun.23 = (bf16[48,16,512]{2,1,0:T(8,128)(2,1)}, bf16[48,16,512]{2,1,0:T(8,128)(2,1)}, f32[8,128]{1,0:T(8,128)S(1)}) custom-call(bf16[24,16,512]{2,1,0:T(8,128)(2,1)S(1)} %collective-permute-done.28.refs_0_, bf16[24,16,512]{2,1,0:T(8,128)(2,1)} %collective-permute-done.29.refs_1_, bf16[48,16,512]{2,1,0:T(8,128)(2,1)S(1)} %get-tuple-element.98.refs_2_, ...), custom_call_target="tpu_custom_call" | custom-call | bytes 2359296 | tf_op jit(solution)/shard_map/cond/branch_1_fun/pallas_call | solution.py:223
  46.2 2.2 %collective-permute-start.31 = (bf16[48,16,512]{2,1,0:T(8,128)(2,1)}, bf16[48,16,512]{2,1,0:T(8,128)(2,1)S(1)}, u32[]{:S(2)}, u32[]{:S(2)}) collective-permute-start(bf16[48,16,512]{2,1,0:T(8,128)(2,1)} %get-tuple-element.101), channel_id=1, source_target_pairs={{0,96},{32,0},{64,32},{96,64},{1,97},{33,1},{65,33},{97,65},{2,98}... | collective-permute-start | bytes 2359304 | tf_op jit(solution)/shard_map/cond/branch_1_fun/ppermute | solution.py:258
  48.4 5.3 %all-to-all-done.4.refs_0_ = bf16[32,1,16,512]{3,2,1,0:T(8,128)(2,1)S(1)} async-done(((bf16[32,1,16,512]{3,2,1,0:T(8,128)(2,1)}), bf16[32,1,16,512]{3,2,1,0:T(8,128)(2,1)S(1)}, u32[]{:S(2)}, u32[]{:S(2)}) %all-to-all-start.4) | async-done | bytes 524320 | tf_op jit(solution)/shard_map/cond/branch_1_fun/all_to_all | solution.py:268
  53.7 2.6 %branch_1_fun.25 = (bf16[32,1,16,512]{3,2,1,0:T(8,128)(2,1)S(1)}, f32[8,128]{1,0:T(8,128)}) custom-call(bf16[32,1,16,512]{3,2,1,0:T(8,128)(2,1)S(1)} %all-to-all-done.4.refs_0_, bf16[3,512,512]{2,1,0:T(8,128)(2,1)} %get-tuple-element.103.refs_1_, bf16[3,512,512]{2,1,0:T(8,128)(2,1)} %get-tuple-element.104.refs_2_, f32[8,128]{1,0:T(8,128)S(1)} %get-tuple-element.105.refs_3_), custom_call_target="tpu_custom_call" | custom-call | tf_op jit(solution)/shard_map/cond/branch_1_fun/pallas_call | solution.py:223
  56.3 15.2 %all_to_all.33.refs_0_ = bf16[32,1,16,512]{3,2,1,0:T(8,128)(2,1)S(1)} all-to-all(bf16[32,1,16,512]{3,2,1,0:T(8,128)(2,1)S(1)} %get-tuple-element.106), channel_id=1, replica_groups=mesh['rep'=4,'fsdp'=32] {'fsdp'}, dimensions={0} | all-to-all | bytes 1048576 | tf_op jit(solution)/shard_map/cond/branch_1_fun/all_to_all | solution.py:268
  71.6 1.7 %branch_1_fun.24 = (bf16[32,2,16,512]{3,2,1,0:T(8,128)(2,1)S(1)}, f32[8,128]{1,0:T(8,128)}) custom-call(s32[192]{0:T(256)S(1)} %select_reduce_fusion.2.refs_0_, s32[256]{0:T(256)S(1)} %get-tuple-element.133.refs_1_, bf16[48,16,512]{2,1,0:T(8,128)(2,1)S(1)} %get-tuple-element.92.refs_2_, bf16[48,16,512]{2,1,0:T(8,128)(2,1)S(1)} %collective-permute-done.30.refs_3_, ...), custom_call_target="tpu_custom_call" | custom-call | bytes 3932160 | tf_op jit(solution)/shard_map/cond/branch_1_fun/pallas_call | solution.py:223
  74.3 3.9 %all-to-all-start.6 = ((bf16[32,2,16,512]{3,2,1,0:T(8,128)(2,1)}), bf16[32,2,16,512]{3,2,1,0:T(8,128)(2,1)S(1)}, u32[]{:S(2)}, u32[]{:S(2)}) async-start(bf16[32,2,16,512]{3,2,1,0:T(8,128)(2,1)} %branch_1_fun.27), calls=%async_computation.6 | async-start | bytes 2097152 | tf_op jit(solution)/shard_map/cond/branch_1_fun/all_to_all | solution.py:268
  78.6 3.0 %collective-permute-start.33 = (bf16[16,16,512]{2,1,0:T(8,128)(2,1)}, bf16[16,16,512]{2,1,0:T(8,128)(2,1)S(1)}, u32[]{:S(2)}, u32[]{:S(2)}) collective-permute-start(bf16[16,16,512]{2,1,0:T(8,128)(2,1)} %copy-done.24), channel_id=1, source_target_pairs={{0,96},{32,0},{64,32},{96,64},{1,97},{33,1},{65,33},{97,65},{2,98}... | collective-permute-start | bytes 786440 | tf_op jit(solution)/shard_map/cond/branch_1_fun/ppermute | solution.py:258
  81.6 6.3 %collective-permute-done.32.refs_5_ = bf16[16,16,512]{2,1,0:T(8,128)(2,1)S(1)} collective-permute-done((bf16[16,16,512]{2,1,0:T(8,128)(2,1)S(1)}, bf16[16,16,512]{2,1,0:T(8,128)(2,1)S(1)}, u32[]{:S(2)}, u32[]{:S(2)}) %collective-permute-start.32) | collective-permute-done | bytes 262176 | tf_op jit(solution)/shard_map/cond/branch_1_fun/ppermute | solution.py:258
  87.9 7.7 %all-to-all-done.6.refs_0_.refs_1_ = bf16[32,2,16,512]{3,2,1,0:T(8,128)(2,1)S(1)} async-done(((bf16[32,2,16,512]{3,2,1,0:T(8,128)(2,1)}), bf16[32,2,16,512]{3,2,1,0:T(8,128)(2,1)S(1)}, u32[]{:S(2)}, u32[]{:S(2)}) %all-to-all-start.6) | async-done | bytes 1048608 | tf_op jit(solution)/shard_map/cond/branch_1_fun/all_to_all | solution.py:268
  95.6 4.3 %branch_1_fun.28 = (bf16[32,2,16,512]{3,2,1,0:T(8,128)(2,1)S(1)}, f32[8,128]{1,0:T(8,128)}) custom-call(bf16[32,2,16,512]{3,2,1,0:T(8,128)(2,1)S(1)} %all-to-all-done.6.refs_0_.refs_1_, bf16[3,512,512]{2,1,0:T(8,128)(2,1)} %get-tuple-element.103.refs_1_, bf16[3,512,512]{2,1,0:T(8,128)(2,1)} %get-tuple-element.104.refs_2_, ...), custom_call_target="tpu_custom_call" | custom-call | tf_op jit(solution)/shard_map/cond/branch_1_fun/pallas_call | solution.py:223
  100.8 3.9 %all-to-all-start.7 = ((bf16[32,2,16,512]{3,2,1,0:T(8,128)(2,1)}), bf16[32,2,16,512]{3,2,1,0:T(8,128)(2,1)S(1)}, u32[]{:S(2)}, u32[]{:S(2)}) async-start(bf16[32,2,16,512]{3,2,1,0:T(8,128)(2,1)} %copy-done.3), calls=%async_computation.7 | async-start | bytes 2097152 | tf_op jit(solution)/shard_map/cond/branch_1_fun/all_to_all | solution.py:268
  107.1 3.0 %collective-permute-start.37 = (bf16[16,16,512]{2,1,0:T(8,128)(2,1)S(1)}, bf16[16,16,512]{2,1,0:T(8,128)(2,1)S(1)}, u32[]{:S(2)}, u32[]{:S(2)}) collective-permute-start(bf16[16,16,512]{2,1,0:T(8,128)(2,1)S(1)} %collective-permute-done.33.refs_4_), channel_id=1, source_target_pairs={{0,96},{32,0},{64,32},{96,64},{1,97},{33,1},{65,33},{97,65},{2,98}... | collective-permute-start | bytes 786440 | tf_op jit(solution)/shard_map/cond/branch_1_fun/ppermute | solution.py:258
  110.1 3.9 %collective-permute-done.34.refs_3_ = bf16[16,16,512]{2,1,0:T(8,128)(2,1)S(1)} collective-permute-done((bf16[16,16,512]{2,1,0:T(8,128)(2,1)S(1)}, bf16[16,16,512]{2,1,0:T(8,128)(2,1)S(1)}, u32[]{:S(2)}, u32[]{:S(2)}) %collective-permute-start.34) | collective-permute-done | bytes 262176 | tf_op jit(solution)/shard_map/cond/branch_1_fun/ppermute | solution.py:258
  114.0 3.0 %collective-permute-done.35.refs_6_ = bf16[16,16,512]{2,1,0:T(8,128)(2,1)S(1)} collective-permute-done((bf16[16,16,512]{2,1,0:T(8,128)(2,1)}, bf16[16,16,512]{2,1,0:T(8,128)(2,1)S(1)}, u32[]{:S(2)}, u32[]{:S(2)}) %collective-permute-start.35) | collective-permute-done | bytes 262176 | tf_op jit(solution)/shard_map/cond/branch_1_fun/ppermute | solution.py:258
  117.9 1.7 %branch_1_fun.29 = (bf16[256,16,512]{2,1,0:T(8,128)(2,1)}, f32[8,128]{1,0:T(8,128)S(1)}) custom-call(s32[128]{0:T(128)S(1)} %select_reduce_fusion.3.refs_0_, bf16[16,16,512]{2,1,0:T(8,128)(2,1)S(1)} %get-tuple-element.110.refs_1_, bf16[16,16,512]{2,1,0:T(8,128)(2,1)S(1)} %copy-done.25, bf16[16,16,512]{2,1,0:T(8,128)(2,1)S(1)} %collective-permute-done.34.refs_3_, ...), custom_call_target="tpu_custom_call" | custom-call | bytes 3145728 | tf_op jit(solution)/shard_map/cond/branch_1_fun/pallas_call | solution.py:223
  119.6 1.9 %collective-permute-done.36.refs_1_ = bf16[16,16,512]{2,1,0:T(8,128)(2,1)S(1)} collective-permute-done((bf16[16,16,512]{2,1,0:T(8,128)(2,1)S(1)}, bf16[16,16,512]{2,1,0:T(8,128)(2,1)S(1)}, u32[]{:S(2)}, u32[]{:S(2)}) %collective-permute-start.36) | collective-permute-done | bytes 262176 | tf_op jit(solution)/shard_map/cond/branch_1_fun/ppermute | solution.py:258
  123.9 3.2 %collective-permute-start.39 = (bf16[24,16,512]{2,1,0:T(8,128)(2,1)S(1)}, bf16[24,16,512]{2,1,0:T(8,128)(2,1)S(1)}, u32[]{:S(2)}, u32[]{:S(2)}) collective-permute-start(bf16[24,16,512]{2,1,0:T(8,128)(2,1)S(1)} %get-tuple-element.118.refs_2_), channel_id=1, source_target_pairs={{0,96},{32,0},{64,32},{96,64},{1,97},{33,1},{65,33},{97,65},{2,98}... | collective-permute-start | bytes 1179656 | tf_op jit(solution)/shard_map/cond/branch_1_fun/ppermute | solution.py:258
  127.1 2.0 %collective-permute-start.43 = (bf16[24,16,512]{2,1,0:T(8,128)(2,1)S(1)}, bf16[24,16,512]{2,1,0:T(8,128)(2,1)}, u32[]{:S(2)}, u32[]{:S(2)}) collective-permute-start(bf16[24,16,512]{2,1,0:T(8,128)(2,1)S(1)} %get-tuple-element.118.refs_2_), channel_id=1, source_target_pairs={{0,32},{32,64},{64,96},{96,0},{1,33},{33,65},{65,97},{97,1},{2,34}... | collective-permute-start | bytes 1179656 | tf_op jit(solution)/shard_map/cond/branch_1_fun/ppermute | solution.py:258
  129.1 7.0 %branch_1_fun.31 = (f32[3,512,512]{2,1,0:T(8,128)}, f32[3,512,512]{2,1,0:T(8,128)}, f32[8,128]{1,0:T(8,128)S(1)}) custom-call(bf16[32,1,16,512]{3,2,1,0:T(8,128)(2,1)S(1)} %all-to-all-done.4.refs_0_, bf16[32,2,16,512]{3,2,1,0:T(8,128)(2,1)S(1)} %all-to-all-done.6.refs_0_.refs_1_, f32[3,512,512]{2,1,0:T(8,128)} %get-tuple-element.108.refs_2_, ...), custom_call_target="tpu_custom_call" | custom-call | flops 1610612736 | bytes 14155776 | tf_op jit(solution)/shard_map/cond/branch_1_fun/pallas_call | solution.py:223
  138.0 3.2 %collective-permute-start.41 = (bf16[24,16,512]{2,1,0:T(8,128)(2,1)}, bf16[24,16,512]{2,1,0:T(8,128)(2,1)S(1)}, u32[]{:S(2)}, u32[]{:S(2)}) collective-permute-start(bf16[24,16,512]{2,1,0:T(8,128)(2,1)} %get-tuple-element.121.refs_4_), channel_id=1, source_target_pairs={{0,96},{32,0},{64,32},{96,64},{1,97},{33,1},{65,33},{97,65},{2,98}... | collective-permute-start | bytes 1179656 | tf_op jit(solution)/shard_map/cond/branch_1_fun/ppermute | solution.py:258
  141.3 1.9 %branch_1_fun.33 = (bf16[256,16,512]{2,1,0:T(8,128)(2,1)}, f32[8,128]{1,0:T(8,128)}) custom-call(s32[128]{0:T(128)S(1)} %select_reduce_fusion.3.refs_0_, bf16[16,16,512]{2,1,0:T(8,128)(2,1)S(1)} %copy-done.16, bf16[16,16,512]{2,1,0:T(8,128)(2,1)S(1)} %copy-done.20, bf16[256,16,512]{2,1,0:T(8,128)(2,1)} %get-tuple-element.122.refs_3_), custom_call_target="tpu_custom_call", output_to_operand_aliasing={{0}: (3, {})} | custom-call | bytes 1048576 | tf_op jit(solution)/shard_map/cond/branch_1_fun/pallas_call | solution.py:223
  143.2 1.9 %collective-permute-done.42.refs_3_ = bf16[24,16,512]{2,1,0:T(8,128)(2,1)} collective-permute-done((bf16[24,16,512]{2,1,0:T(8,128)(2,1)S(1)}, bf16[24,16,512]{2,1,0:T(8,128)(2,1)}, u32[]{:S(2)}, u32[]{:S(2)}) %collective-permute-start.42) | collective-permute-done | bytes 393248 | tf_op jit(solution)/shard_map/cond/branch_1_fun/ppermute | solution.py:258
  145.6 3.4 %branch_1_fun.34 = (bf16[256,16,512]{2,1,0:T(8,128)(2,1)}, f32[8,128]{1,0:T(8,128)}) custom-call(s32[192]{0:T(256)} %copy-done.27, bf16[24,16,512]{2,1,0:T(8,128)(2,1)} %copy-done.11, bf16[24,16,512]{2,1,0:T(8,128)(2,1)} %copy-done.12, bf16[24,16,512]{2,1,0:T(8,128)(2,1)} %collective-permute-done.42.refs_3_, ...), custom_call_target="tpu_custom_call", output_to_operand_aliasing={{0}: (7, {})} | custom-call | bytes 4718592 | tf_op jit(solution)/shard_map/cond/branch_1_fun/pallas_call | solution.py:223
  149.0 3.2 %collective-permute-done.40.refs_1_ = bf16[24,16,512]{2,1,0:T(8,128)(2,1)S(1)} collective-permute-done((bf16[24,16,512]{2,1,0:T(8,128)(2,1)}, bf16[24,16,512]{2,1,0:T(8,128)(2,1)S(1)}, u32[]{:S(2)}, u32[]{:S(2)}) %collective-permute-start.40) | collective-permute-done | bytes 393248 | tf_op jit(solution)/shard_map/cond/branch_1_fun/ppermute | solution.py:258
  153.1 2.5 %branch_1_fun.35 = (bf16[256,16,512]{2,1,0:T(8,128)(2,1)}, f32[8,128]{1,0:T(8,128)}) custom-call(s32[192]{0:T(256)} %copy-done.27, bf16[24,16,512]{2,1,0:T(8,128)(2,1)} %copy-done.48, bf16[24,16,512]{2,1,0:T(8,128)(2,1)} %copy-done.49, bf16[256,16,512]{2,1,0:T(8,128)(2,1)} %get-tuple-element.124.refs_3_), custom_call_target="tpu_custom_call", output_to_operand_aliasing={{0}: (3, {})} | custom-call | bytes 1572864 | tf_op jit(solution)/shard_map/cond/branch_1_fun/pallas_call | solution.py:223
  (95 shorter events, 31.4 us)
Async XLA Ops:
  3.1 19.7 %copy-start.41 = (bf16[1,256,16,512]{3,2,1,0:T(8,128)(2,1)S(1)}, bf16[1,256,16,512]{3,2,1,0:T(8,128)(2,1)}, u32[]{:S(2)}) copy-start(bf16[1,256,16,512]{3,2,1,0:T(8,128)(2,1)} %get-tuple-element.79) | copy-start | bytes 12582916 | tf_op jit(solution)/shard_map/cond
  8.2 10.4 %collective-permute-start.22 = (bf16[16,16,512]{2,1,0:T(8,128)(2,1)S(1)}, bf16[16,16,512]{2,1,0:T(8,128)(2,1)S(1)}, u32[]{:S(2)}, u32[]{:S(2)}) collective-permute-start(bf16[16,16,512]{2,1,0:T(8,128)(2,1)S(1)} %get-tuple-element.81), channel_id=1, source_target_pairs={{0,32},{32,64},{64,96},{96,0},{1,33},{33,65},{65,97},{97,1},{2,34}... | collective-permute-start | bytes 786440 | tf_op jit(solution)/shard_map/cond/branch_1_fun/ppermute | solution.py:258
  9.9 9.2 %collective-permute-start.23 = (bf16[16,16,512]{2,1,0:T(8,128)(2,1)S(1)}, bf16[16,16,512]{2,1,0:T(8,128)(2,1)S(1)}, u32[]{:S(2)}, u32[]{:S(2)}) collective-permute-start(bf16[16,16,512]{2,1,0:T(8,128)(2,1)S(1)} %get-tuple-element.82), channel_id=1, source_target_pairs={{0,96},{32,0},{64,32},{96,64},{1,97},{33,1},{65,33},{97,65},{2,98}... | collective-permute-start | bytes 786440 | tf_op jit(solution)/shard_map/cond/branch_1_fun/ppermute | solution.py:258
  11.5 13.2 %collective-permute-start.25 = (bf16[16,16,512]{2,1,0:T(8,128)(2,1)S(1)}, bf16[16,16,512]{2,1,0:T(8,128)(2,1)S(1)}, u32[]{:S(2)}, u32[]{:S(2)}) collective-permute-start(bf16[16,16,512]{2,1,0:T(8,128)(2,1)S(1)} %get-tuple-element.86), channel_id=1, source_target_pairs={{0,32},{32,64},{64,96},{96,0},{1,33},{33,65},{65,97},{97,1},{2,34}... | collective-permute-start | bytes 786440 | tf_op jit(solution)/shard_map/cond/branch_1_fun/ppermute | solution.py:258
  11.9 12.8 %collective-permute-start.26 = (bf16[16,16,512]{2,1,0:T(8,128)(2,1)S(1)}, bf16[16,16,512]{2,1,0:T(8,128)(2,1)S(1)}, u32[]{:S(2)}, u32[]{:S(2)}) collective-permute-start(bf16[16,16,512]{2,1,0:T(8,128)(2,1)S(1)} %get-tuple-element.87), channel_id=1, source_target_pairs={{0,96},{32,0},{64,32},{96,64},{1,97},{33,1},{65,33},{97,65},{2,98}... | collective-permute-start | bytes 786440 | tf_op jit(solution)/shard_map/cond/branch_1_fun/ppermute | solution.py:258
  19.3 9.6 %collective-permute-start.24 = (bf16[16,16,512]{2,1,0:T(8,128)(2,1)S(1)}, bf16[16,16,512]{2,1,0:T(8,128)(2,1)S(1)}, u32[]{:S(2)}, u32[]{:S(2)}) collective-permute-start(bf16[16,16,512]{2,1,0:T(8,128)(2,1)S(1)} %get-tuple-element.85), channel_id=1, source_target_pairs={{0,32},{32,64},{64,96},{96,0},{1,33},{33,65},{65,97},{97,1},{2,34}... | collective-permute-start | bytes 786440 | tf_op jit(solution)/shard_map/cond/branch_1_fun/ppermute | solution.py:258
  20.9 8.0 %collective-permute-start.27 = (bf16[16,16,512]{2,1,0:T(8,128)(2,1)S(1)}, bf16[16,16,512]{2,1,0:T(8,128)(2,1)S(1)}, u32[]{:S(2)}, u32[]{:S(2)}) collective-permute-start(bf16[16,16,512]{2,1,0:T(8,128)(2,1)S(1)} %get-tuple-element.88), channel_id=1, source_target_pairs={{0,96},{32,0},{64,32},{96,64},{1,97},{33,1},{65,33},{97,65},{2,98}... | collective-permute-start | bytes 786440 | tf_op jit(solution)/shard_map/cond/branch_1_fun/ppermute | solution.py:258
  22.7 100.2 %copy-start.27 = (s32[192]{0:T(256)}, s32[192]{0:T(256)S(1)}, u32[]{:S(2)}) copy-start(s32[192]{0:T(256)S(1)} %select_reduce_fusion.2.refs_0_) | copy-start | bytes 2308 | tf_op jit(solution)/shard_map/cond
  30.5 11.5 %collective-permute-start.28 = (bf16[24,16,512]{2,1,0:T(8,128)(2,1)}, bf16[24,16,512]{2,1,0:T(8,128)(2,1)S(1)}, u32[]{:S(2)}, u32[]{:S(2)}) collective-permute-start(bf16[24,16,512]{2,1,0:T(8,128)(2,1)} %get-tuple-element.96), channel_id=1, source_target_pairs={{0,32},{32,64},{64,96},{96,0},{1,33},{33,65},{65,97},{97,1},{2,34}... | collective-permute-start | bytes 1179656 | tf_op jit(solution)/shard_map/cond/branch_1_fun/ppermute | solution.py:258
  32.1 10.0 %collective-permute-start.29 = (bf16[24,16,512]{2,1,0:T(8,128)(2,1)}, bf16[24,16,512]{2,1,0:T(8,128)(2,1)}, u32[]{:S(2)}, u32[]{:S(2)}) collective-permute-start(bf16[24,16,512]{2,1,0:T(8,128)(2,1)} %get-tuple-element.97), channel_id=1, source_target_pairs={{0,96},{32,0},{64,32},{96,64},{1,97},{33,1},{65,33},{97,65},{2,98}... | collective-permute-start | bytes 1179656 | tf_op jit(solution)/shard_map/cond/branch_1_fun/ppermute | solution.py:258
  33.7 19.9 %all-to-all-start.4 = ((bf16[32,1,16,512]{3,2,1,0:T(8,128)(2,1)}), bf16[32,1,16,512]{3,2,1,0:T(8,128)(2,1)S(1)}, u32[]{:S(2)}, u32[]{:S(2)}) async-start(bf16[32,1,16,512]{3,2,1,0:T(8,128)(2,1)} %get-tuple-element.91), calls=%async_computation.4 | async-start | bytes 1048576 | tf_op jit(solution)/shard_map/cond/branch_1_fun/all_to_all | solution.py:268
  45.2 26.4 %collective-permute-start.30 = (bf16[48,16,512]{2,1,0:T(8,128)(2,1)}, bf16[48,16,512]{2,1,0:T(8,128)(2,1)S(1)}, u32[]{:S(2)}, u32[]{:S(2)}) collective-permute-start(bf16[48,16,512]{2,1,0:T(8,128)(2,1)} %get-tuple-element.100), channel_id=1, source_target_pairs={{0,32},{32,64},{64,96},{96,0},{1,33},{33,65},{65,97},{97,1},{2,34}... | collective-permute-start | bytes 2359304 | tf_op jit(solution)/shard_map/cond/branch_1_fun/ppermute | solution.py:258
  46.2 25.4 %collective-permute-start.31 = (bf16[48,16,512]{2,1,0:T(8,128)(2,1)}, bf16[48,16,512]{2,1,0:T(8,128)(2,1)S(1)}, u32[]{:S(2)}, u32[]{:S(2)}) collective-permute-start(bf16[48,16,512]{2,1,0:T(8,128)(2,1)} %get-tuple-element.101), channel_id=1, source_target_pairs={{0,96},{32,0},{64,32},{96,64},{1,97},{33,1},{65,33},{97,65},{2,98}... | collective-permute-start | bytes 2359304 | tf_op jit(solution)/shard_map/cond/branch_1_fun/ppermute | solution.py:258
  71.6 7.0 %copy-start.24 = (bf16[16,16,512]{2,1,0:T(8,128)(2,1)}, bf16[16,16,512]{2,1,0:T(8,128)(2,1)S(1)}, u32[]{:S(2)}) copy-start(bf16[16,16,512]{2,1,0:T(8,128)(2,1)S(1)} %get-tuple-element.111.refs_2_) | copy-start | bytes 786436 | tf_op jit(solution)/shard_map/cond
  74.3 21.3 %all-to-all-start.6 = ((bf16[32,2,16,512]{3,2,1,0:T(8,128)(2,1)}), bf16[32,2,16,512]{3,2,1,0:T(8,128)(2,1)S(1)}, u32[]{:S(2)}, u32[]{:S(2)}) async-start(bf16[32,2,16,512]{3,2,1,0:T(8,128)(2,1)} %branch_1_fun.27), calls=%async_computation.6 | async-start | bytes 2097152 | tf_op jit(solution)/shard_map/cond/branch_1_fun/all_to_all | solution.py:268
  78.3 9.7 %collective-permute-start.32 = (bf16[16,16,512]{2,1,0:T(8,128)(2,1)S(1)}, bf16[16,16,512]{2,1,0:T(8,128)(2,1)S(1)}, u32[]{:S(2)}, u32[]{:S(2)}) collective-permute-start(bf16[16,16,512]{2,1,0:T(8,128)(2,1)S(1)} %get-tuple-element.110.refs_1_), channel_id=1, source_target_pairs={{0,32},{32,64},{64,96},{96,0},{1,33},{33,65},{65,97},{97,1},{2,34}... | collective-permute-start | bytes 786440 | tf_op jit(solution)/shard_map/cond/branch_1_fun/ppermute | solution.py:258
  78.6 9.3 %collective-permute-start.33 = (bf16[16,16,512]{2,1,0:T(8,128)(2,1)}, bf16[16,16,512]{2,1,0:T(8,128)(2,1)S(1)}, u32[]{:S(2)}, u32[]{:S(2)}) collective-permute-start(bf16[16,16,512]{2,1,0:T(8,128)(2,1)} %copy-done.24), channel_id=1, source_target_pairs={{0,96},{32,0},{64,32},{96,64},{1,97},{33,1},{65,33},{97,65},{2,98}... | collective-permute-start | bytes 786440 | tf_op jit(solution)/shard_map/cond/branch_1_fun/ppermute | solution.py:258
  100.8 22.1 %all-to-all-start.7 = ((bf16[32,2,16,512]{3,2,1,0:T(8,128)(2,1)}), bf16[32,2,16,512]{3,2,1,0:T(8,128)(2,1)S(1)}, u32[]{:S(2)}, u32[]{:S(2)}) async-start(bf16[32,2,16,512]{3,2,1,0:T(8,128)(2,1)} %copy-done.3), calls=%async_computation.7 | async-start | bytes 2097152 | tf_op jit(solution)/shard_map/cond/branch_1_fun/all_to_all | solution.py:268
  104.8 9.2 %collective-permute-start.34 = (bf16[16,16,512]{2,1,0:T(8,128)(2,1)S(1)}, bf16[16,16,512]{2,1,0:T(8,128)(2,1)S(1)}, u32[]{:S(2)}, u32[]{:S(2)}) collective-permute-start(bf16[16,16,512]{2,1,0:T(8,128)(2,1)S(1)} %get-tuple-element.110.refs_1_), channel_id=1, source_target_pairs={{0,96},{32,0},{64,32},{96,64},{1,97},{33,1},{65,33},{97,65},{2,98}... | collective-permute-start | bytes 786440 | tf_op jit(solution)/shard_map/cond/branch_1_fun/ppermute | solution.py:258
  106.3 10.6 %collective-permute-start.35 = (bf16[16,16,512]{2,1,0:T(8,128)(2,1)}, bf16[16,16,512]{2,1,0:T(8,128)(2,1)S(1)}, u32[]{:S(2)}, u32[]{:S(2)}) collective-permute-start(bf16[16,16,512]{2,1,0:T(8,128)(2,1)} %copy-done.24), channel_id=1, source_target_pairs={{0,32},{32,64},{64,96},{96,0},{1,33},{33,65},{65,97},{97,1},{2,34}... | collective-permute-start | bytes 786440 | tf_op jit(solution)/shard_map/cond/branch_1_fun/ppermute | solution.py:258
  106.9 14.6 %collective-permute-start.36 = (bf16[16,16,512]{2,1,0:T(8,128)(2,1)S(1)}, bf16[16,16,512]{2,1,0:T(8,128)(2,1)S(1)}, u32[]{:S(2)}, u32[]{:S(2)}) collective-permute-start(bf16[16,16,512]{2,1,0:T(8,128)(2,1)S(1)} %collective-permute-done.32.refs_5_), channel_id=1, source_target_pairs={{0,32},{32,64},{64,96},{96,0},{1,33},{33,65},{65,97},{97,1},{2,34}... | collective-permute-start | bytes 786440 | tf_op jit(solution)/shard_map/cond/branch_1_fun/ppermute | solution.py:258
  107.1 15.0 %collective-permute-start.37 = (bf16[16,16,512]{2,1,0:T(8,128)(2,1)S(1)}, bf16[16,16,512]{2,1,0:T(8,128)(2,1)S(1)}, u32[]{:S(2)}, u32[]{:S(2)}) collective-permute-start(bf16[16,16,512]{2,1,0:T(8,128)(2,1)S(1)} %collective-permute-done.33.refs_4_), channel_id=1, source_target_pairs={{0,96},{32,0},{64,32},{96,64},{1,97},{33,1},{65,33},{97,65},{2,98}... | collective-permute-start | bytes 786440 | tf_op jit(solution)/shard_map/cond/branch_1_fun/ppermute | solution.py:258
  123.7 14.3 %copy-start.11 = (bf16[24,16,512]{2,1,0:T(8,128)(2,1)}, bf16[24,16,512]{2,1,0:T(8,128)(2,1)S(1)}, u32[]{:S(2)}) copy-start(bf16[24,16,512]{2,1,0:T(8,128)(2,1)S(1)} %get-tuple-element.117.refs_1_) | copy-start | bytes 1179652 | tf_op jit(solution)/shard_map/cond
  123.8 14.2 %copy-start.12 = (bf16[24,16,512]{2,1,0:T(8,128)(2,1)}, bf16[24,16,512]{2,1,0:T(8,128)(2,1)S(1)}, u32[]{:S(2)}) copy-start(bf16[24,16,512]{2,1,0:T(8,128)(2,1)S(1)} %get-tuple-element.118.refs_2_) | copy-start | bytes 1179652 | tf_op jit(solution)/shard_map/cond
  123.8 13.3 %collective-permute-start.38 = (bf16[24,16,512]{2,1,0:T(8,128)(2,1)S(1)}, bf16[24,16,512]{2,1,0:T(8,128)(2,1)S(1)}, u32[]{:S(2)}, u32[]{:S(2)}) collective-permute-start(bf16[24,16,512]{2,1,0:T(8,128)(2,1)S(1)} %get-tuple-element.117.refs_1_), channel_id=1, source_target_pairs={{0,32},{32,64},{64,96},{96,0},{1,33},{33,65},{65,97},{97,1},{2,34}... | collective-permute-start | bytes 1179656 | tf_op jit(solution)/shard_map/cond/branch_1_fun/ppermute | solution.py:258
  123.9 13.3 %collective-permute-start.39 = (bf16[24,16,512]{2,1,0:T(8,128)(2,1)S(1)}, bf16[24,16,512]{2,1,0:T(8,128)(2,1)S(1)}, u32[]{:S(2)}, u32[]{:S(2)}) collective-permute-start(bf16[24,16,512]{2,1,0:T(8,128)(2,1)S(1)} %get-tuple-element.118.refs_2_), channel_id=1, source_target_pairs={{0,96},{32,0},{64,32},{96,64},{1,97},{33,1},{65,33},{97,65},{2,98}... | collective-permute-start | bytes 1179656 | tf_op jit(solution)/shard_map/cond/branch_1_fun/ppermute | solution.py:258
  127.1 18.0 %collective-permute-start.42 = (bf16[24,16,512]{2,1,0:T(8,128)(2,1)S(1)}, bf16[24,16,512]{2,1,0:T(8,128)(2,1)}, u32[]{:S(2)}, u32[]{:S(2)}) collective-permute-start(bf16[24,16,512]{2,1,0:T(8,128)(2,1)S(1)} %get-tuple-element.117.refs_1_), channel_id=1, source_target_pairs={{0,96},{32,0},{64,32},{96,64},{1,97},{33,1},{65,33},{97,65},{2,98}... | collective-permute-start | bytes 1179656 | tf_op jit(solution)/shard_map/cond/branch_1_fun/ppermute | solution.py:258
  127.1 18.5 %collective-permute-start.43 = (bf16[24,16,512]{2,1,0:T(8,128)(2,1)S(1)}, bf16[24,16,512]{2,1,0:T(8,128)(2,1)}, u32[]{:S(2)}, u32[]{:S(2)}) collective-permute-start(bf16[24,16,512]{2,1,0:T(8,128)(2,1)S(1)} %get-tuple-element.118.refs_2_), channel_id=1, source_target_pairs={{0,32},{32,64},{64,96},{96,0},{1,33},{33,65},{65,97},{97,1},{2,34}... | collective-permute-start | bytes 1179656 | tf_op jit(solution)/shard_map/cond/branch_1_fun/ppermute | solution.py:258
  129.1 12.2 %copy-start.16 = (bf16[16,16,512]{2,1,0:T(8,128)(2,1)S(1)}, bf16[16,16,512]{2,1,0:T(8,128)(2,1)}, u32[]{:S(2)}) copy-start(bf16[16,16,512]{2,1,0:T(8,128)(2,1)} %copy-done.15) | copy-start | bytes 786436 | tf_op jit(solution)/shard_map/cond
  129.1 12.2 %copy-start.20 = (bf16[16,16,512]{2,1,0:T(8,128)(2,1)S(1)}, bf16[16,16,512]{2,1,0:T(8,128)(2,1)}, u32[]{:S(2)}) copy-start(bf16[16,16,512]{2,1,0:T(8,128)(2,1)} %copy-done.19) | copy-start | bytes 786436 | tf_op jit(solution)/shard_map/cond
  138.0 14.2 %collective-permute-start.40 = (bf16[24,16,512]{2,1,0:T(8,128)(2,1)}, bf16[24,16,512]{2,1,0:T(8,128)(2,1)S(1)}, u32[]{:S(2)}, u32[]{:S(2)}) collective-permute-start(bf16[24,16,512]{2,1,0:T(8,128)(2,1)} %get-tuple-element.120.refs_5_), channel_id=1, source_target_pairs={{0,32},{32,64},{64,96},{96,0},{1,33},{33,65},{65,97},{97,1},{2,34}... | collective-permute-start | bytes 1179656 | tf_op jit(solution)/shard_map/cond/branch_1_fun/ppermute | solution.py:258
  138.0 14.2 %collective-permute-start.41 = (bf16[24,16,512]{2,1,0:T(8,128)(2,1)}, bf16[24,16,512]{2,1,0:T(8,128)(2,1)S(1)}, u32[]{:S(2)}, u32[]{:S(2)}) collective-permute-start(bf16[24,16,512]{2,1,0:T(8,128)(2,1)} %get-tuple-element.121.refs_4_), channel_id=1, source_target_pairs={{0,96},{32,0},{64,32},{96,64},{1,97},{33,1},{65,33},{97,65},{2,98}... | collective-permute-start | bytes 1179656 | tf_op jit(solution)/shard_map/cond/branch_1_fun/ppermute | solution.py:258
  (15 other events, 18.3 us)

commit v6 on v5

--- a/solution.py
+++ b/solution.py
@@ -448,7 +448,7 @@
     direction, _ = placed(
         table_rest, plan[:6], [low, high, above_low, above_high, below_low, below_high], direction, (), 59
     )
-    direction, _ = placed(table_rest, plan[6:], [far_low, far_high], direction, (), 59)
+    direction, _ = placed(table_rest, plan[6:], [far_low, far_high], direction, (), 61)
     return (new_left, new_right, direction)
 
 

time: 156 us -> 157 us (level)
  no operation moved by 1% of the time
where the time goes in v6:
time: 157 us; the launch traced here: 156 us
  starting transfers between devices  49.5 us (32%)
  waiting for transfers between devices  42.7 us (27%)
  Pallas kernels  34 us (22%)
  blocking collectives  15.2 us (10%)
  local copies, waits for them, and re-layouts  8.72 us (6%)
  other arithmetic  3.73 us (2%)
    pallas_call x15, Pallas kernels, call(): pl.pallas_call(body, out_shape=(*results, token), in_specs=list(specs) +...  34 us
    ppermute x11, starting transfers between devices, both_ways(): lax.ppermute(down, 'rep', down_pairs)  23.9 us
    ppermute x11, waiting for transfers between devices, both_ways(): lax.ppermute(up, 'rep', up_pairs)  23.3 us
    all_to_all x3, starting transfers between devices, exchange(): return lax.all_to_all(x, 'fsdp', split_axis=0, concat_axis=0, tiled=True)  16 us
    all_to_all x1, blocking collectives, exchange(): return lax.all_to_all(x, 'fsdp', split_axis=0, concat_axis=0, tiled=True)  15.2 us
    all_to_all x3, waiting for transfers between devices, exchange(): return lax.all_to_all(x, 'fsdp', split_axis=0, concat_axis=0, tiled=True)  12.9 us
    ppermute x11, starting transfers between devices, both_ways(): lax.ppermute(up, 'rep', up_pairs)  9.57 us
    cond x44, local copies, waits for them, and re-layouts  8.71 us
  transfers between devices with their start and end apart: 25, of which 15 were waited for; matrix products, arithmetic and copies ran while one was open for 0% of the time, Pallas kernels for 13%

profile of v6, /device:TPU:0, one launch (start us, length us, event | category | flops | bytes accessed | tf_op | source)
XLA Modules:
  0.0 155.7 jit_solution(12147493329786134885)
XLA Ops:
  2.9 152.7 %conditional.1 = (f32[3,512,512]{2,1,0:T(8,128)}, f32[3,512,512]{2,1,0:T(8,128)}, bf16[256,16,512]{2,1,0:T(8,128)(2,1)}) conditional(s32[]{:T(128)} %convert_element_type.17, (s32[256]{0:T(256)S(1)}, s32[256]{0:T(256)}, bf16[1,256,16,512]{3,2,1,0:T(8,128)(2,1)}, bf16[3,512,512]{2,1,0:T(8,128)(2,1)}, bf16[3,512,512]{2,1,0:T(8,128)(2,1)}, ...), branch_computations={%region_2.6_spmd, %region_6.10_spmd} | conditional | flops 1611291264 | bytes 144078016 | solution.py:460
  4.9 3.3 %branch_1_fun.18 = (bf16[16,16,512]{2,1,0:T(8,128)(2,1)S(1)}, bf16[16,16,512]{2,1,0:T(8,128)(2,1)S(1)}, bf16[16,16,512]{2,1,0:T(8,128)(2,1)S(1)}, bf16[16,16,512...) custom-call(s32[128]{0:T(128)S(1)} %select_reduce_fusion.3.refs_0_, ...), custom_call_target="tpu_custom_call" | custom-call | bytes 4194304 | tf_op jit(solution)/shard_map/cond/branch_1_fun/pallas_call | solution.py:223
  11.9 2.8 %collective-permute-start.26 = (bf16[16,16,512]{2,1,0:T(8,128)(2,1)S(1)}, bf16[16,16,512]{2,1,0:T(8,128)(2,1)S(1)}, u32[]{:S(2)}, u32[]{:S(2)}) collective-permute-start(bf16[16,16,512]{2,1,0:T(8,128)(2,1)S(1)} %get-tuple-element.87), channel_id=1, source_target_pairs={{0,96},{32,0},{64,32},{96,64},{1,97},{33,1},{65,33},{97,65},{2,98}... | collective-permute-start | bytes 786440 | tf_op jit(solution)/shard_map/cond/branch_1_fun/ppermute | solution.py:258
  14.9 3.7 %collective-permute-done.22.refs_0_ = bf16[16,16,512]{2,1,0:T(8,128)(2,1)S(1)} collective-permute-done((bf16[16,16,512]{2,1,0:T(8,128)(2,1)S(1)}, bf16[16,16,512]{2,1,0:T(8,128)(2,1)S(1)}, u32[]{:S(2)}, u32[]{:S(2)}) %collective-permute-start.22) | collective-permute-done | bytes 262176 | tf_op jit(solution)/shard_map/cond/branch_1_fun/ppermute | solution.py:258
  24.7 4.1 %collective-permute-done.24.refs_1_ = bf16[16,16,512]{2,1,0:T(8,128)(2,1)S(1)} collective-permute-done((bf16[16,16,512]{2,1,0:T(8,128)(2,1)S(1)}, bf16[16,16,512]{2,1,0:T(8,128)(2,1)S(1)}, u32[]{:S(2)}, u32[]{:S(2)}) %collective-permute-start.24) | collective-permute-done | bytes 262176 | tf_op jit(solution)/shard_map/cond/branch_1_fun/ppermute | solution.py:258
  33.7 8.2 %all-to-all-start.4 = ((bf16[32,1,16,512]{3,2,1,0:T(8,128)(2,1)}), bf16[32,1,16,512]{3,2,1,0:T(8,128)(2,1)S(1)}, u32[]{:S(2)}, u32[]{:S(2)}) async-start(bf16[32,1,16,512]{3,2,1,0:T(8,128)(2,1)} %get-tuple-element.91), calls=%async_computation.4 | async-start | bytes 1048576 | tf_op jit(solution)/shard_map/cond/branch_1_fun/all_to_all | solution.py:268
  42.7 2.4 %branch_1_fun.23 = (bf16[48,16,512]{2,1,0:T(8,128)(2,1)}, bf16[48,16,512]{2,1,0:T(8,128)(2,1)}, f32[8,128]{1,0:T(8,128)S(1)}) custom-call(bf16[24,16,512]{2,1,0:T(8,128)(2,1)S(1)} %collective-permute-done.28.refs_0_, bf16[24,16,512]{2,1,0:T(8,128)(2,1)} %collective-permute-done.29.refs_1_, bf16[48,16,512]{2,1,0:T(8,128)(2,1)S(1)} %get-tuple-element.98.refs_2_, ...), custom_call_target="tpu_custom_call" | custom-call | bytes 2359296 | tf_op jit(solution)/shard_map/cond/branch_1_fun/pallas_call | solution.py:223
  46.2 2.2 %collective-permute-start.31 = (bf16[48,16,512]{2,1,0:T(8,128)(2,1)}, bf16[48,16,512]{2,1,0:T(8,128)(2,1)S(1)}, u32[]{:S(2)}, u32[]{:S(2)}) collective-permute-start(bf16[48,16,512]{2,1,0:T(8,128)(2,1)} %get-tuple-element.101), channel_id=1, source_target_pairs={{0,96},{32,0},{64,32},{96,64},{1,97},{33,1},{65,33},{97,65},{2,98}... | collective-permute-start | bytes 2359304 | tf_op jit(solution)/shard_map/cond/branch_1_fun/ppermute | solution.py:258
  48.4 5.3 %all-to-all-done.4.refs_0_ = bf16[32,1,16,512]{3,2,1,0:T(8,128)(2,1)S(1)} async-done(((bf16[32,1,16,512]{3,2,1,0:T(8,128)(2,1)}), bf16[32,1,16,512]{3,2,1,0:T(8,128)(2,1)S(1)}, u32[]{:S(2)}, u32[]{:S(2)}) %all-to-all-start.4) | async-done | bytes 524320 | tf_op jit(solution)/shard_map/cond/branch_1_fun/all_to_all | solution.py:268
  53.7 2.6 %branch_1_fun.25 = (bf16[32,1,16,512]{3,2,1,0:T(8,128)(2,1)S(1)}, f32[8,128]{1,0:T(8,128)}) custom-call(bf16[32,1,16,512]{3,2,1,0:T(8,128)(2,1)S(1)} %all-to-all-done.4.refs_0_, bf16[3,512,512]{2,1,0:T(8,128)(2,1)} %get-tuple-element.103.refs_1_, bf16[3,512,512]{2,1,0:T(8,128)(2,1)} %get-tuple-element.104.refs_2_, f32[8,128]{1,0:T(8,128)S(1)} %get-tuple-element.105.refs_3_), custom_call_target="tpu_custom_call" | custom-call | tf_op jit(solution)/shard_map/cond/branch_1_fun/pallas_call | solution.py:223
  56.3 15.2 %all_to_all.33.refs_0_ = bf16[32,1,16,512]{3,2,1,0:T(8,128)(2,1)S(1)} all-to-all(bf16[32,1,16,512]{3,2,1,0:T(8,128)(2,1)S(1)} %get-tuple-element.106), channel_id=1, replica_groups=mesh['rep'=4,'fsdp'=32] {'fsdp'}, dimensions={0} | all-to-all | bytes 1048576 | tf_op jit(solution)/shard_map/cond/branch_1_fun/all_to_all | solution.py:268
  71.6 1.7 %branch_1_fun.24 = (bf16[32,2,16,512]{3,2,1,0:T(8,128)(2,1)S(1)}, f32[8,128]{1,0:T(8,128)}) custom-call(s32[192]{0:T(256)S(1)} %select_reduce_fusion.2.refs_0_, s32[256]{0:T(256)S(1)} %get-tuple-element.133.refs_1_, bf16[48,16,512]{2,1,0:T(8,128)(2,1)S(1)} %get-tuple-element.92.refs_2_, bf16[48,16,512]{2,1,0:T(8,128)(2,1)S(1)} %collective-permute-done.30.refs_3_, ...), custom_call_target="tpu_custom_call" | custom-call | bytes 3932160 | tf_op jit(solution)/shard_map/cond/branch_1_fun/pallas_call | solution.py:223
  74.3 3.9 %all-to-all-start.6 = ((bf16[32,2,16,512]{3,2,1,0:T(8,128)(2,1)}), bf16[32,2,16,512]{3,2,1,0:T(8,128)(2,1)S(1)}, u32[]{:S(2)}, u32[]{:S(2)}) async-start(bf16[32,2,16,512]{3,2,1,0:T(8,128)(2,1)} %branch_1_fun.27), calls=%async_computation.6 | async-start | bytes 2097152 | tf_op jit(solution)/shard_map/cond/branch_1_fun/all_to_all | solution.py:268
  78.6 2.9 %collective-permute-start.33 = (bf16[16,16,512]{2,1,0:T(8,128)(2,1)}, bf16[16,16,512]{2,1,0:T(8,128)(2,1)S(1)}, u32[]{:S(2)}, u32[]{:S(2)}) collective-permute-start(bf16[16,16,512]{2,1,0:T(8,128)(2,1)} %copy-done.24), channel_id=1, source_target_pairs={{0,96},{32,0},{64,32},{96,64},{1,97},{33,1},{65,33},{97,65},{2,98}... | collective-permute-start | bytes 786440 | tf_op jit(solution)/shard_map/cond/branch_1_fun/ppermute | solution.py:258
  81.6 6.3 %collective-permute-done.32.refs_5_ = bf16[16,16,512]{2,1,0:T(8,128)(2,1)S(1)} collective-permute-done((bf16[16,16,512]{2,1,0:T(8,128)(2,1)S(1)}, bf16[16,16,512]{2,1,0:T(8,128)(2,1)S(1)}, u32[]{:S(2)}, u32[]{:S(2)}) %collective-permute-start.32) | collective-permute-done | bytes 262176 | tf_op jit(solution)/shard_map/cond/branch_1_fun/ppermute | solution.py:258
  87.9 7.7 %all-to-all-done.6.refs_0_.refs_1_ = bf16[32,2,16,512]{3,2,1,0:T(8,128)(2,1)S(1)} async-done(((bf16[32,2,16,512]{3,2,1,0:T(8,128)(2,1)}), bf16[32,2,16,512]{3,2,1,0:T(8,128)(2,1)S(1)}, u32[]{:S(2)}, u32[]{:S(2)}) %all-to-all-start.6) | async-done | bytes 1048608 | tf_op jit(solution)/shard_map/cond/branch_1_fun/all_to_all | solution.py:268
  95.6 4.3 %branch_1_fun.28 = (bf16[32,2,16,512]{3,2,1,0:T(8,128)(2,1)S(1)}, f32[8,128]{1,0:T(8,128)}) custom-call(bf16[32,2,16,512]{3,2,1,0:T(8,128)(2,1)S(1)} %all-to-all-done.6.refs_0_.refs_1_, bf16[3,512,512]{2,1,0:T(8,128)(2,1)} %get-tuple-element.103.refs_1_, bf16[3,512,512]{2,1,0:T(8,128)(2,1)} %get-tuple-element.104.refs_2_, ...), custom_call_target="tpu_custom_call" | custom-call | tf_op jit(solution)/shard_map/cond/branch_1_fun/pallas_call | solution.py:223
  100.8 3.9 %all-to-all-start.7 = ((bf16[32,2,16,512]{3,2,1,0:T(8,128)(2,1)}), bf16[32,2,16,512]{3,2,1,0:T(8,128)(2,1)S(1)}, u32[]{:S(2)}, u32[]{:S(2)}) async-start(bf16[32,2,16,512]{3,2,1,0:T(8,128)(2,1)} %copy-done.3), calls=%async_computation.7 | async-start | bytes 2097152 | tf_op jit(solution)/shard_map/cond/branch_1_fun/all_to_all | solution.py:268
  107.1 2.9 %collective-permute-start.37 = (bf16[16,16,512]{2,1,0:T(8,128)(2,1)S(1)}, bf16[16,16,512]{2,1,0:T(8,128)(2,1)S(1)}, u32[]{:S(2)}, u32[]{:S(2)}) collective-permute-start(bf16[16,16,512]{2,1,0:T(8,128)(2,1)S(1)} %collective-permute-done.33.refs_4_), channel_id=1, source_target_pairs={{0,96},{32,0},{64,32},{96,64},{1,97},{33,1},{65,33},{97,65},{2,98}... | collective-permute-start | bytes 786440 | tf_op jit(solution)/shard_map/cond/branch_1_fun/ppermute | solution.py:258
  110.1 3.9 %collective-permute-done.34.refs_3_ = bf16[16,16,512]{2,1,0:T(8,128)(2,1)S(1)} collective-permute-done((bf16[16,16,512]{2,1,0:T(8,128)(2,1)S(1)}, bf16[16,16,512]{2,1,0:T(8,128)(2,1)S(1)}, u32[]{:S(2)}, u32[]{:S(2)}) %collective-permute-start.34) | collective-permute-done | bytes 262176 | tf_op jit(solution)/shard_map/cond/branch_1_fun/ppermute | solution.py:258
  114.0 3.0 %collective-permute-done.35.refs_6_ = bf16[16,16,512]{2,1,0:T(8,128)(2,1)S(1)} collective-permute-done((bf16[16,16,512]{2,1,0:T(8,128)(2,1)}, bf16[16,16,512]{2,1,0:T(8,128)(2,1)S(1)}, u32[]{:S(2)}, u32[]{:S(2)}) %collective-permute-start.35) | collective-permute-done | bytes 262176 | tf_op jit(solution)/shard_map/cond/branch_1_fun/ppermute | solution.py:258
  117.9 1.7 %branch_1_fun.29 = (bf16[256,16,512]{2,1,0:T(8,128)(2,1)}, f32[8,128]{1,0:T(8,128)S(1)}) custom-call(s32[128]{0:T(128)S(1)} %select_reduce_fusion.3.refs_0_, bf16[16,16,512]{2,1,0:T(8,128)(2,1)S(1)} %get-tuple-element.110.refs_1_, bf16[16,16,512]{2,1,0:T(8,128)(2,1)S(1)} %copy-done.25, bf16[16,16,512]{2,1,0:T(8,128)(2,1)S(1)} %collective-permute-done.34.refs_3_, ...), custom_call_target="tpu_custom_call" | custom-call | bytes 3145728 | tf_op jit(solution)/shard_map/cond/branch_1_fun/pallas_call | solution.py:223
  119.6 1.9 %collective-permute-done.36.refs_1_ = bf16[16,16,512]{2,1,0:T(8,128)(2,1)S(1)} collective-permute-done((bf16[16,16,512]{2,1,0:T(8,128)(2,1)S(1)}, bf16[16,16,512]{2,1,0:T(8,128)(2,1)S(1)}, u32[]{:S(2)}, u32[]{:S(2)}) %collective-permute-start.36) | collective-permute-done | bytes 262176 | tf_op jit(solution)/shard_map/cond/branch_1_fun/ppermute | solution.py:258
  123.9 3.2 %collective-permute-start.39 = (bf16[24,16,512]{2,1,0:T(8,128)(2,1)S(1)}, bf16[24,16,512]{2,1,0:T(8,128)(2,1)S(1)}, u32[]{:S(2)}, u32[]{:S(2)}) collective-permute-start(bf16[24,16,512]{2,1,0:T(8,128)(2,1)S(1)} %get-tuple-element.118.refs_2_), channel_id=1, source_target_pairs={{0,96},{32,0},{64,32},{96,64},{1,97},{33,1},{65,33},{97,65},{2,98}... | collective-permute-start | bytes 1179656 | tf_op jit(solution)/shard_map/cond/branch_1_fun/ppermute | solution.py:258
  127.1 2.0 %collective-permute-start.43 = (bf16[24,16,512]{2,1,0:T(8,128)(2,1)S(1)}, bf16[24,16,512]{2,1,0:T(8,128)(2,1)}, u32[]{:S(2)}, u32[]{:S(2)}) collective-permute-start(bf16[24,16,512]{2,1,0:T(8,128)(2,1)S(1)} %get-tuple-element.118.refs_2_), channel_id=1, source_target_pairs={{0,32},{32,64},{64,96},{96,0},{1,33},{33,65},{65,97},{97,1},{2,34}... | collective-permute-start | bytes 1179656 | tf_op jit(solution)/shard_map/cond/branch_1_fun/ppermute | solution.py:258
  129.1 7.0 %branch_1_fun.31 = (f32[3,512,512]{2,1,0:T(8,128)}, f32[3,512,512]{2,1,0:T(8,128)}, f32[8,128]{1,0:T(8,128)S(1)}) custom-call(bf16[32,1,16,512]{3,2,1,0:T(8,128)(2,1)S(1)} %all-to-all-done.4.refs_0_, bf16[32,2,16,512]{3,2,1,0:T(8,128)(2,1)S(1)} %all-to-all-done.6.refs_0_.refs_1_, f32[3,512,512]{2,1,0:T(8,128)} %get-tuple-element.108.refs_2_, ...), custom_call_target="tpu_custom_call" | custom-call | flops 1610612736 | bytes 14155776 | tf_op jit(solution)/shard_map/cond/branch_1_fun/pallas_call | solution.py:223
  138.0 3.2 %collective-permute-start.41 = (bf16[24,16,512]{2,1,0:T(8,128)(2,1)}, bf16[24,16,512]{2,1,0:T(8,128)(2,1)S(1)}, u32[]{:S(2)}, u32[]{:S(2)}) collective-permute-start(bf16[24,16,512]{2,1,0:T(8,128)(2,1)} %get-tuple-element.121.refs_4_), channel_id=1, source_target_pairs={{0,96},{32,0},{64,32},{96,64},{1,97},{33,1},{65,33},{97,65},{2,98}... | collective-permute-start | bytes 1179656 | tf_op jit(solution)/shard_map/cond/branch_1_fun/ppermute | solution.py:258
  141.3 1.9 %branch_1_fun.33 = (bf16[256,16,512]{2,1,0:T(8,128)(2,1)}, f32[8,128]{1,0:T(8,128)}) custom-call(s32[128]{0:T(128)S(1)} %select_reduce_fusion.3.refs_0_, bf16[16,16,512]{2,1,0:T(8,128)(2,1)S(1)} %copy-done.16, bf16[16,16,512]{2,1,0:T(8,128)(2,1)S(1)} %copy-done.20, bf16[256,16,512]{2,1,0:T(8,128)(2,1)} %get-tuple-element.122.refs_3_), custom_call_target="tpu_custom_call", output_to_operand_aliasing={{0}: (3, {})} | custom-call | bytes 1048576 | tf_op jit(solution)/shard_map/cond/branch_1_fun/pallas_call | solution.py:223
  143.2 1.9 %collective-permute-done.42.refs_3_ = bf16[24,16,512]{2,1,0:T(8,128)(2,1)} collective-permute-done((bf16[24,16,512]{2,1,0:T(8,128)(2,1)S(1)}, bf16[24,16,512]{2,1,0:T(8,128)(2,1)}, u32[]{:S(2)}, u32[]{:S(2)}) %collective-permute-start.42) | collective-permute-done | bytes 393248 | tf_op jit(solution)/shard_map/cond/branch_1_fun/ppermute | solution.py:258
  145.6 3.4 %branch_1_fun.34 = (bf16[256,16,512]{2,1,0:T(8,128)(2,1)}, f32[8,128]{1,0:T(8,128)}) custom-call(s32[192]{0:T(256)} %copy-done.27, bf16[24,16,512]{2,1,0:T(8,128)(2,1)} %copy-done.11, bf16[24,16,512]{2,1,0:T(8,128)(2,1)} %copy-done.12, bf16[24,16,512]{2,1,0:T(8,128)(2,1)} %collective-permute-done.42.refs_3_, ...), custom_call_target="tpu_custom_call", output_to_operand_aliasing={{0}: (7, {})} | custom-call | bytes 4718592 | tf_op jit(solution)/shard_map/cond/branch_1_fun/pallas_call | solution.py:223
  149.0 3.2 %collective-permute-done.40.refs_1_ = bf16[24,16,512]{2,1,0:T(8,128)(2,1)S(1)} collective-permute-done((bf16[24,16,512]{2,1,0:T(8,128)(2,1)}, bf16[24,16,512]{2,1,0:T(8,128)(2,1)S(1)}, u32[]{:S(2)}, u32[]{:S(2)}) %collective-permute-start.40) | collective-permute-done | bytes 393248 | tf_op jit(solution)/shard_map/cond/branch_1_fun/ppermute | solution.py:258
  153.1 2.5 %branch_1_fun.35 = (bf16[256,16,512]{2,1,0:T(8,128)(2,1)}, f32[8,128]{1,0:T(8,128)}) custom-call(s32[192]{0:T(256)} %copy-done.27, bf16[24,16,512]{2,1,0:T(8,128)(2,1)} %copy-done.48, bf16[24,16,512]{2,1,0:T(8,128)(2,1)} %copy-done.49, bf16[256,16,512]{2,1,0:T(8,128)(2,1)} %get-tuple-element.124.refs_3_), custom_call_target="tpu_custom_call", output_to_operand_aliasing={{0}: (3, {})} | custom-call | bytes 1572864 | tf_op jit(solution)/shard_map/cond/branch_1_fun/pallas_call | solution.py:223
  (95 shorter events, 31.5 us)
Async XLA Ops:
  3.1 19.7 %copy-start.41 = (bf16[1,256,16,512]{3,2,1,0:T(8,128)(2,1)S(1)}, bf16[1,256,16,512]{3,2,1,0:T(8,128)(2,1)}, u32[]{:S(2)}) copy-start(bf16[1,256,16,512]{3,2,1,0:T(8,128)(2,1)} %get-tuple-element.79) | copy-start | bytes 12582916 | tf_op jit(solution)/shard_map/cond
  8.2 10.4 %collective-permute-start.22 = (bf16[16,16,512]{2,1,0:T(8,128)(2,1)S(1)}, bf16[16,16,512]{2,1,0:T(8,128)(2,1)S(1)}, u32[]{:S(2)}, u32[]{:S(2)}) collective-permute-start(bf16[16,16,512]{2,1,0:T(8,128)(2,1)S(1)} %get-tuple-element.81), channel_id=1, source_target_pairs={{0,32},{32,64},{64,96},{96,0},{1,33},{33,65},{65,97},{97,1},{2,34}... | collective-permute-start | bytes 786440 | tf_op jit(solution)/shard_map/cond/branch_1_fun/ppermute | solution.py:258
  9.9 9.2 %collective-permute-start.23 = (bf16[16,16,512]{2,1,0:T(8,128)(2,1)S(1)}, bf16[16,16,512]{2,1,0:T(8,128)(2,1)S(1)}, u32[]{:S(2)}, u32[]{:S(2)}) collective-permute-start(bf16[16,16,512]{2,1,0:T(8,128)(2,1)S(1)} %get-tuple-element.82), channel_id=1, source_target_pairs={{0,96},{32,0},{64,32},{96,64},{1,97},{33,1},{65,33},{97,65},{2,98}... | collective-permute-start | bytes 786440 | tf_op jit(solution)/shard_map/cond/branch_1_fun/ppermute | solution.py:258
  11.5 13.2 %collective-permute-start.25 = (bf16[16,16,512]{2,1,0:T(8,128)(2,1)S(1)}, bf16[16,16,512]{2,1,0:T(8,128)(2,1)S(1)}, u32[]{:S(2)}, u32[]{:S(2)}) collective-permute-start(bf16[16,16,512]{2,1,0:T(8,128)(2,1)S(1)} %get-tuple-element.86), channel_id=1, source_target_pairs={{0,32},{32,64},{64,96},{96,0},{1,33},{33,65},{65,97},{97,1},{2,34}... | collective-permute-start | bytes 786440 | tf_op jit(solution)/shard_map/cond/branch_1_fun/ppermute | solution.py:258
  11.9 12.8 %collective-permute-start.26 = (bf16[16,16,512]{2,1,0:T(8,128)(2,1)S(1)}, bf16[16,16,512]{2,1,0:T(8,128)(2,1)S(1)}, u32[]{:S(2)}, u32[]{:S(2)}) collective-permute-start(bf16[16,16,512]{2,1,0:T(8,128)(2,1)S(1)} %get-tuple-element.87), channel_id=1, source_target_pairs={{0,96},{32,0},{64,32},{96,64},{1,97},{33,1},{65,33},{97,65},{2,98}... | collective-permute-start | bytes 786440 | tf_op jit(solution)/shard_map/cond/branch_1_fun/ppermute | solution.py:258
  19.3 9.6 %collective-permute-start.24 = (bf16[16,16,512]{2,1,0:T(8,128)(2,1)S(1)}, bf16[16,16,512]{2,1,0:T(8,128)(2,1)S(1)}, u32[]{:S(2)}, u32[]{:S(2)}) collective-permute-start(bf16[16,16,512]{2,1,0:T(8,128)(2,1)S(1)} %get-tuple-element.85), channel_id=1, source_target_pairs={{0,32},{32,64},{64,96},{96,0},{1,33},{33,65},{65,97},{97,1},{2,34}... | collective-permute-start | bytes 786440 | tf_op jit(solution)/shard_map/cond/branch_1_fun/ppermute | solution.py:258
  20.9 8.0 %collective-permute-start.27 = (bf16[16,16,512]{2,1,0:T(8,128)(2,1)S(1)}, bf16[16,16,512]{2,1,0:T(8,128)(2,1)S(1)}, u32[]{:S(2)}, u32[]{:S(2)}) collective-permute-start(bf16[16,16,512]{2,1,0:T(8,128)(2,1)S(1)} %get-tuple-element.88), channel_id=1, source_target_pairs={{0,96},{32,0},{64,32},{96,64},{1,97},{33,1},{65,33},{97,65},{2,98}... | collective-permute-start | bytes 786440 | tf_op jit(solution)/shard_map/cond/branch_1_fun/ppermute | solution.py:258
  22.7 100.2 %copy-start.27 = (s32[192]{0:T(256)}, s32[192]{0:T(256)S(1)}, u32[]{:S(2)}) copy-start(s32[192]{0:T(256)S(1)} %select_reduce_fusion.2.refs_0_) | copy-start | bytes 2308 | tf_op jit(solution)/shard_map/cond
  30.5 11.5 %collective-permute-start.28 = (bf16[24,16,512]{2,1,0:T(8,128)(2,1)}, bf16[24,16,512]{2,1,0:T(8,128)(2,1)S(1)}, u32[]{:S(2)}, u32[]{:S(2)}) collective-permute-start(bf16[24,16,512]{2,1,0:T(8,128)(2,1)} %get-tuple-element.96), channel_id=1, source_target_pairs={{0,32},{32,64},{64,96},{96,0},{1,33},{33,65},{65,97},{97,1},{2,34}... | collective-permute-start | bytes 1179656 | tf_op jit(solution)/shard_map/cond/branch_1_fun/ppermute | solution.py:258
  32.1 10.0 %collective-permute-start.29 = (bf16[24,16,512]{2,1,0:T(8,128)(2,1)}, bf16[24,16,512]{2,1,0:T(8,128)(2,1)}, u32[]{:S(2)}, u32[]{:S(2)}) collective-permute-start(bf16[24,16,512]{2,1,0:T(8,128)(2,1)} %get-tuple-element.97), channel_id=1, source_target_pairs={{0,96},{32,0},{64,32},{96,64},{1,97},{33,1},{65,33},{97,65},{2,98}... | collective-permute-start | bytes 1179656 | tf_op jit(solution)/shard_map/cond/branch_1_fun/ppermute | solution.py:258
  33.7 19.9 %all-to-all-start.4 = ((bf16[32,1,16,512]{3,2,1,0:T(8,128)(2,1)}), bf16[32,1,16,512]{3,2,1,0:T(8,128)(2,1)S(1)}, u32[]{:S(2)}, u32[]{:S(2)}) async-start(bf16[32,1,16,512]{3,2,1,0:T(8,128)(2,1)} %get-tuple-element.91), calls=%async_computation.4 | async-start | bytes 1048576 | tf_op jit(solution)/shard_map/cond/branch_1_fun/all_to_all | solution.py:268
  45.2 26.4 %collective-permute-start.30 = (bf16[48,16,512]{2,1,0:T(8,128)(2,1)}, bf16[48,16,512]{2,1,0:T(8,128)(2,1)S(1)}, u32[]{:S(2)}, u32[]{:S(2)}) collective-permute-start(bf16[48,16,512]{2,1,0:T(8,128)(2,1)} %get-tuple-element.100), channel_id=1, source_target_pairs={{0,32},{32,64},{64,96},{96,0},{1,33},{33,65},{65,97},{97,1},{2,34}... | collective-permute-start | bytes 2359304 | tf_op jit(solution)/shard_map/cond/branch_1_fun/ppermute | solution.py:258
  46.2 25.4 %collective-permute-start.31 = (bf16[48,16,512]{2,1,0:T(8,128)(2,1)}, bf16[48,16,512]{2,1,0:T(8,128)(2,1)S(1)}, u32[]{:S(2)}, u32[]{:S(2)}) collective-permute-start(bf16[48,16,512]{2,1,0:T(8,128)(2,1)} %get-tuple-element.101), channel_id=1, source_target_pairs={{0,96},{32,0},{64,32},{96,64},{1,97},{33,1},{65,33},{97,65},{2,98}... | collective-permute-start | bytes 2359304 | tf_op jit(solution)/shard_map/cond/branch_1_fun/ppermute | solution.py:258
  71.6 7.0 %copy-start.24 = (bf16[16,16,512]{2,1,0:T(8,128)(2,1)}, bf16[16,16,512]{2,1,0:T(8,128)(2,1)S(1)}, u32[]{:S(2)}) copy-start(bf16[16,16,512]{2,1,0:T(8,128)(2,1)S(1)} %get-tuple-element.111.refs_2_) | copy-start | bytes 786436 | tf_op jit(solution)/shard_map/cond
  74.3 21.3 %all-to-all-start.6 = ((bf16[32,2,16,512]{3,2,1,0:T(8,128)(2,1)}), bf16[32,2,16,512]{3,2,1,0:T(8,128)(2,1)S(1)}, u32[]{:S(2)}, u32[]{:S(2)}) async-start(bf16[32,2,16,512]{3,2,1,0:T(8,128)(2,1)} %branch_1_fun.27), calls=%async_computation.6 | async-start | bytes 2097152 | tf_op jit(solution)/shard_map/cond/branch_1_fun/all_to_all | solution.py:268
  78.2 9.7 %collective-permute-start.32 = (bf16[16,16,512]{2,1,0:T(8,128)(2,1)S(1)}, bf16[16,16,512]{2,1,0:T(8,128)(2,1)S(1)}, u32[]{:S(2)}, u32[]{:S(2)}) collective-permute-start(bf16[16,16,512]{2,1,0:T(8,128)(2,1)S(1)} %get-tuple-element.110.refs_1_), channel_id=1, source_target_pairs={{0,32},{32,64},{64,96},{96,0},{1,33},{33,65},{65,97},{97,1},{2,34}... | collective-permute-start | bytes 786440 | tf_op jit(solution)/shard_map/cond/branch_1_fun/ppermute | solution.py:258
  78.6 9.3 %collective-permute-start.33 = (bf16[16,16,512]{2,1,0:T(8,128)(2,1)}, bf16[16,16,512]{2,1,0:T(8,128)(2,1)S(1)}, u32[]{:S(2)}, u32[]{:S(2)}) collective-permute-start(bf16[16,16,512]{2,1,0:T(8,128)(2,1)} %copy-done.24), channel_id=1, source_target_pairs={{0,96},{32,0},{64,32},{96,64},{1,97},{33,1},{65,33},{97,65},{2,98}... | collective-permute-start | bytes 786440 | tf_op jit(solution)/shard_map/cond/branch_1_fun/ppermute | solution.py:258
  100.8 22.1 %all-to-all-start.7 = ((bf16[32,2,16,512]{3,2,1,0:T(8,128)(2,1)}), bf16[32,2,16,512]{3,2,1,0:T(8,128)(2,1)S(1)}, u32[]{:S(2)}, u32[]{:S(2)}) async-start(bf16[32,2,16,512]{3,2,1,0:T(8,128)(2,1)} %copy-done.3), calls=%async_computation.7 | async-start | bytes 2097152 | tf_op jit(solution)/shard_map/cond/branch_1_fun/all_to_all | solution.py:268
  104.7 9.2 %collective-permute-start.34 = (bf16[16,16,512]{2,1,0:T(8,128)(2,1)S(1)}, bf16[16,16,512]{2,1,0:T(8,128)(2,1)S(1)}, u32[]{:S(2)}, u32[]{:S(2)}) collective-permute-start(bf16[16,16,512]{2,1,0:T(8,128)(2,1)S(1)} %get-tuple-element.110.refs_1_), channel_id=1, source_target_pairs={{0,96},{32,0},{64,32},{96,64},{1,97},{33,1},{65,33},{97,65},{2,98}... | collective-permute-start | bytes 786440 | tf_op jit(solution)/shard_map/cond/branch_1_fun/ppermute | solution.py:258
  106.3 10.6 %collective-permute-start.35 = (bf16[16,16,512]{2,1,0:T(8,128)(2,1)}, bf16[16,16,512]{2,1,0:T(8,128)(2,1)S(1)}, u32[]{:S(2)}, u32[]{:S(2)}) collective-permute-start(bf16[16,16,512]{2,1,0:T(8,128)(2,1)} %copy-done.24), channel_id=1, source_target_pairs={{0,32},{32,64},{64,96},{96,0},{1,33},{33,65},{65,97},{97,1},{2,34}... | collective-permute-start | bytes 786440 | tf_op jit(solution)/shard_map/cond/branch_1_fun/ppermute | solution.py:258
  106.8 14.6 %collective-permute-start.36 = (bf16[16,16,512]{2,1,0:T(8,128)(2,1)S(1)}, bf16[16,16,512]{2,1,0:T(8,128)(2,1)S(1)}, u32[]{:S(2)}, u32[]{:S(2)}) collective-permute-start(bf16[16,16,512]{2,1,0:T(8,128)(2,1)S(1)} %collective-permute-done.32.refs_5_), channel_id=1, source_target_pairs={{0,32},{32,64},{64,96},{96,0},{1,33},{33,65},{65,97},{97,1},{2,34}... | collective-permute-start | bytes 786440 | tf_op jit(solution)/shard_map/cond/branch_1_fun/ppermute | solution.py:258
  107.1 15.0 %collective-permute-start.37 = (bf16[16,16,512]{2,1,0:T(8,128)(2,1)S(1)}, bf16[16,16,512]{2,1,0:T(8,128)(2,1)S(1)}, u32[]{:S(2)}, u32[]{:S(2)}) collective-permute-start(bf16[16,16,512]{2,1,0:T(8,128)(2,1)S(1)} %collective-permute-done.33.refs_4_), channel_id=1, source_target_pairs={{0,96},{32,0},{64,32},{96,64},{1,97},{33,1},{65,33},{97,65},{2,98}... | collective-permute-start | bytes 786440 | tf_op jit(solution)/shard_map/cond/branch_1_fun/ppermute | solution.py:258
  123.7 14.2 %copy-start.11 = (bf16[24,16,512]{2,1,0:T(8,128)(2,1)}, bf16[24,16,512]{2,1,0:T(8,128)(2,1)S(1)}, u32[]{:S(2)}) copy-start(bf16[24,16,512]{2,1,0:T(8,128)(2,1)S(1)} %get-tuple-element.117.refs_1_) | copy-start | bytes 1179652 | tf_op jit(solution)/shard_map/cond
  123.8 14.2 %copy-start.12 = (bf16[24,16,512]{2,1,0:T(8,128)(2,1)}, bf16[24,16,512]{2,1,0:T(8,128)(2,1)S(1)}, u32[]{:S(2)}) copy-start(bf16[24,16,512]{2,1,0:T(8,128)(2,1)S(1)} %get-tuple-element.118.refs_2_) | copy-start | bytes 1179652 | tf_op jit(solution)/shard_map/cond
  123.8 13.3 %collective-permute-start.38 = (bf16[24,16,512]{2,1,0:T(8,128)(2,1)S(1)}, bf16[24,16,512]{2,1,0:T(8,128)(2,1)S(1)}, u32[]{:S(2)}, u32[]{:S(2)}) collective-permute-start(bf16[24,16,512]{2,1,0:T(8,128)(2,1)S(1)} %get-tuple-element.117.refs_1_), channel_id=1, source_target_pairs={{0,32},{32,64},{64,96},{96,0},{1,33},{33,65},{65,97},{97,1},{2,34}... | collective-permute-start | bytes 1179656 | tf_op jit(solution)/shard_map/cond/branch_1_fun/ppermute | solution.py:258
  123.9 13.3 %collective-permute-start.39 = (bf16[24,16,512]{2,1,0:T(8,128)(2,1)S(1)}, bf16[24,16,512]{2,1,0:T(8,128)(2,1)S(1)}, u32[]{:S(2)}, u32[]{:S(2)}) collective-permute-start(bf16[24,16,512]{2,1,0:T(8,128)(2,1)S(1)} %get-tuple-element.118.refs_2_), channel_id=1, source_target_pairs={{0,96},{32,0},{64,32},{96,64},{1,97},{33,1},{65,33},{97,65},{2,98}... | collective-permute-start | bytes 1179656 | tf_op jit(solution)/shard_map/cond/branch_1_fun/ppermute | solution.py:258
  127.1 18.0 %collective-permute-start.42 = (bf16[24,16,512]{2,1,0:T(8,128)(2,1)S(1)}, bf16[24,16,512]{2,1,0:T(8,128)(2,1)}, u32[]{:S(2)}, u32[]{:S(2)}) collective-permute-start(bf16[24,16,512]{2,1,0:T(8,128)(2,1)S(1)} %get-tuple-element.117.refs_1_), channel_id=1, source_target_pairs={{0,96},{32,0},{64,32},{96,64},{1,97},{33,1},{65,33},{97,65},{2,98}... | collective-permute-start | bytes 1179656 | tf_op jit(solution)/shard_map/cond/branch_1_fun/ppermute | solution.py:258
  127.1 18.5 %collective-permute-start.43 = (bf16[24,16,512]{2,1,0:T(8,128)(2,1)S(1)}, bf16[24,16,512]{2,1,0:T(8,128)(2,1)}, u32[]{:S(2)}, u32[]{:S(2)}) collective-permute-start(bf16[24,16,512]{2,1,0:T(8,128)(2,1)S(1)} %get-tuple-element.118.refs_2_), channel_id=1, source_target_pairs={{0,32},{32,64},{64,96},{96,0},{1,33},{33,65},{65,97},{97,1},{2,34}... | collective-permute-start | bytes 1179656 | tf_op jit(solution)/shard_map/cond/branch_1_fun/ppermute | solution.py:258
  129.1 12.2 %copy-start.16 = (bf16[16,16,512]{2,1,0:T(8,128)(2,1)S(1)}, bf16[16,16,512]{2,1,0:T(8,128)(2,1)}, u32[]{:S(2)}) copy-start(bf16[16,16,512]{2,1,0:T(8,128)(2,1)} %copy-done.15) | copy-start | bytes 786436 | tf_op jit(solution)/shard_map/cond
  129.1 12.2 %copy-start.20 = (bf16[16,16,512]{2,1,0:T(8,128)(2,1)S(1)}, bf16[16,16,512]{2,1,0:T(8,128)(2,1)}, u32[]{:S(2)}) copy-start(bf16[16,16,512]{2,1,0:T(8,128)(2,1)} %copy-done.19) | copy-start | bytes 786436 | tf_op jit(solution)/shard_map/cond
  138.0 14.2 %collective-permute-start.40 = (bf16[24,16,512]{2,1,0:T(8,128)(2,1)}, bf16[24,16,512]{2,1,0:T(8,128)(2,1)S(1)}, u32[]{:S(2)}, u32[]{:S(2)}) collective-permute-start(bf16[24,16,512]{2,1,0:T(8,128)(2,1)} %get-tuple-element.120.refs_5_), channel_id=1, source_target_pairs={{0,32},{32,64},{64,96},{96,0},{1,33},{33,65},{65,97},{97,1},{2,34}... | collective-permute-start | bytes 1179656 | tf_op jit(solution)/shard_map/cond/branch_1_fun/ppermute | solution.py:258
  138.0 14.2 %collective-permute-start.41 = (bf16[24,16,512]{2,1,0:T(8,128)(2,1)}, bf16[24,16,512]{2,1,0:T(8,128)(2,1)S(1)}, u32[]{:S(2)}, u32[]{:S(2)}) collective-permute-start(bf16[24,16,512]{2,1,0:T(8,128)(2,1)} %get-tuple-element.121.refs_4_), channel_id=1, source_target_pairs={{0,96},{32,0},{64,32},{96,64},{1,97},{33,1},{65,33},{97,65},{2,98}... | collective-permute-start | bytes 1179656 | tf_op jit(solution)/shard_map/cond/branch_1_fun/ppermute | solution.py:258
  (15 other events, 18.2 us)
